TPU v7x, 32 devices: a whole 2x2x4 slice. The times are simulated.
32 devices in a mesh: section: 2 (over core), mp: 4 (over z), dp: 4 (over y, x).
Axes of the slice: x: 2, y: 2, z: 4, core: 2. Of those that a mesh axis runs over, the one named last changes fastest.
Arguments:
- expression: bfloat16 [3968, 13504], P('dp', 'mp'), may hold values from -19.2 to 19.2
- cell_xy: float32 [2, 3968], P(None, 'dp'), may hold values from 0 to 100
- live_mask: int32 [3968], P('dp'), may hold values from 0 to 1, as said below
- lengths: int32 [8, 3], P('dp'), may hold values from 1 to 434, 496 in all within a row
- ramp_step: int32 [1], replicated, may hold values from 0 to 1999
- latent_noise: float32 [3968, 512], P('dp', 'mp'), may hold values from -7.5 to 7.5
- gene_embed: bfloat16 [13504, 1024], P('mp', ('section', 'dp')), may hold values from -0.0546875 to 0.0546875
- ln1_gain: bfloat16 [1024], P(('section', 'dp')), may hold values from 0.5 to 1.5
- ln1_bias: bfloat16 [1024], P(('section', 'dp')), may hold values from -1.5 to 1.5
- w_query: bfloat16 [1024, 1024], P(('section', 'dp'), 'mp'), may hold values from -0.25 to 0.25
- w_key: bfloat16 [1024, 1024], P(('section', 'dp'), 'mp'), may hold values from -0.25 to 0.25
- w_value: bfloat16 [1024, 1024], P(('section', 'dp'), 'mp'), may hold values from -0.1875 to 0.1875
- w_out: bfloat16 [1024, 1024], P('mp', ('section', 'dp')), may hold values from -0.75 to 0.75
- ln2_gain: bfloat16 [1024], P(('section', 'dp')), may hold values from 0.5 to 1.5
- ln2_bias: bfloat16 [1024], P(('section', 'dp')), may hold values from -1.5 to 1.5
- w_up: bfloat16 [1024, 4096], P(('section', 'dp'), 'mp'), may hold values from -0.1875 to 0.1875
- w_down: bfloat16 [4096, 1024], P('mp', ('section', 'dp')), may hold values from -0.09375 to 0.09375
- w_mean: bfloat16 [1024, 512], P(('section', 'dp'), 'mp'), may hold values from -0.1875 to 0.1875
- w_logvar: bfloat16 [1024, 512], P(('section', 'dp'), 'mp'), may hold values from -0.09375 to 0.09375
- comp_mean: bfloat16 [16, 512], P(None, ('mp', 'section', 'dp')), may hold values from -4 to 4
- comp_logvar: bfloat16 [16, 512], P(None, ('mp', 'section', 'dp')), may hold values from -0.5 to 0.5
- w_dec: bfloat16 [512, 1024], P('mp', ('section', 'dp')), may hold values from -0.25 to 0.25
- w_genes: bfloat16 [1024, 13504], P(('section', 'dp'), 'mp'), may hold values from -0.1875 to 0.1875
Outputs:
- grad_gene_embed: float32 [13504, 1024], P('mp', ('section', 'dp'))
- grad_ln1_gain: float32 [1024], P(('section', 'dp'))
- grad_ln1_bias: float32 [1024], P(('section', 'dp'))
- grad_query: float32 [1024, 1024], P(('section', 'dp'), 'mp')
- grad_key: float32 [1024, 1024], P(('section', 'dp'), 'mp')
- grad_value: float32 [1024, 1024], P(('section', 'dp'), 'mp')
- grad_out: float32 [1024, 1024], P('mp', ('section', 'dp'))
- grad_ln2_gain: float32 [1024], P(('section', 'dp'))
- grad_ln2_bias: float32 [1024], P(('section', 'dp'))
- grad_up: float32 [1024, 4096], P(('section', 'dp'), 'mp')
- grad_down: float32 [4096, 1024], P('mp', ('section', 'dp'))
- grad_mean: float32 [1024, 512], P(('section', 'dp'), 'mp')
- grad_logvar: float32 [1024, 512], P(('section', 'dp'), 'mp')
- grad_comp_mean: float32 [16, 512], P(None, ('mp', 'section', 'dp'))
- grad_comp_logvar: float32 [16, 512], P(None, ('mp', 'section', 'dp'))
- grad_dec: float32 [512, 1024], P('mp', ('section', 'dp'))
- grad_genes: float32 [1024, 13504], P(('section', 'dp'), 'mp')
- grad_expression: bfloat16 [3968, 13504], P('dp', 'mp')
Inputs may be any that keep to these rules, and one draw needn't show every extreme that they name: `live_mask`: 1 marks a kept cell; the first cell of each buffer of 496 cells is kept. Row b gives the lengths of the 3 slides of buffer b in order; each row sums to 496.
All inputs are finite; a program needn't handle non-finite values.
Results may differ from a plain program's by a relative error of at most 0.03.
Values may be sent and summed in bfloat16 or wider, within the bound.
A program may use at most 256 MiB of HBM per device.

v0:
```python
import math

import jax
import jax.numpy as jnp
from jax import lax
from jax.sharding import PartitionSpec as P

HEAD = 64
LATENT = 512
RAMP = 1000


LOG_TWO_PI = 1.8378770664093453
NEG_LARGE = -1e30
FREE_BITS = 1.0


def from_partner(shard, axis, stride):
    return lax.ppermute(shard, axis, [(i, i ^ 1 << stride) for i in range(lax.axis_size(axis))])


def mat_nn(left, right):
    return jnp.dot(left, right, preferred_element_type=jnp.float32)


def mat_tn(left, right):
    return lax.dot_general(
        left, right, (((0,), (0,)), ((), ())), preferred_element_type=jnp.float32
    )


def mat_nt(left, right):
    return lax.dot_general(
        left, right, (((1,), (1,)), ((), ())), preferred_element_type=jnp.float32
    )


def gelu_slope(values):
    return (
        0.5 * (1.0 + lax.erf(values * 0.7071067811865476))
        + values * jnp.exp(-0.5 * values * values) * 0.3989422804014327
    )


def layer_norm(values, gain, offset):
    center = values - jnp.mean(values, axis=-1, keepdims=True)
    scale = lax.rsqrt(jnp.mean(center * center, axis=-1, keepdims=True) + 1e-05)
    normed = center * scale
    return (normed * gain + offset, normed, scale)


def norm_back(grad_in, normed, scale, gain):
    scaled = grad_in * gain
    return scale * (
        scaled
        - jnp.mean(scaled, axis=-1, keepdims=True)
        - normed * jnp.mean(scaled * normed, axis=-1, keepdims=True)
    )


def position_code(places, feature_count):
    quarter = feature_count // 4
    frequency = jnp.exp(jnp.arange(quarter, dtype=jnp.float32) * (-math.log(10000.0) / quarter))
    along_x = places[0][:, None] * frequency[None, :]
    along_y = places[1][:, None] * frequency[None, :]
    return jnp.concatenate(
        [jnp.sin(along_x), jnp.cos(along_x), jnp.sin(along_y), jnp.cos(along_y)], axis=1
    )


def slide_ids(length_row, cell_count):
    bounds = jnp.cumsum(length_row)[:-1]
    cell_index = jnp.arange(cell_count, dtype=jnp.int32)
    return jnp.sum((cell_index[:, None] >= bounds[None, :]).astype(jnp.int32), axis=1)


def allow_mask(row_index, slide_rows, slide_all, alive_all):
    key_index = jnp.arange(slide_all.shape[0], dtype=jnp.int32)
    same_slide = slide_rows[:, None] == slide_all[None, :]
    usable = (alive_all[None, :] == 1) | (row_index[:, None] == key_index[None, :])
    return same_slide & usable


def block_plan(cell_count):
    pieces = max(1, cell_count // 512)
    return (pieces, cell_count // pieces)


def reduce_rows(partial_value):
    return lax.psum(partial_value, "mp")


def attend(queries, keys_in, values_in, slide_all, alive_all):
    cell_count = queries.shape[0]
    head_count = queries.shape[1] // HEAD
    pieces, block_rows = block_plan(cell_count)
    factor = HEAD ** (-0.5)
    keys_heads = keys_in.reshape(cell_count, head_count, HEAD)
    values_heads = values_in.reshape(cell_count, head_count, HEAD)
    packed = (
        queries.reshape(pieces, block_rows, head_count, HEAD),
        jnp.arange(cell_count, dtype=jnp.int32).reshape(pieces, block_rows),
        slide_all.reshape(pieces, block_rows),
    )

    def one_block(block_pack):
        query_block, row_index, slide_rows = block_pack
        allowed = allow_mask(row_index, slide_rows, slide_all, alive_all)
        scores = (
            jnp.einsum("qhd,khd->hqk", query_block, keys_heads, preferred_element_type=jnp.float32)
            * factor
        )
        scores = jnp.where(allowed[None], scores, NEG_LARGE)
        largest = jnp.max(scores, axis=2, keepdims=True)
        exponents = jnp.exp(scores - largest)
        row_sums = jnp.sum(exponents, axis=2, keepdims=True)
        attn_probs = (exponents / row_sums).astype(jnp.bfloat16)
        attended = jnp.einsum(
            "hqk,khd->qhd", attn_probs, values_heads, preferred_element_type=jnp.float32
        )
        return (
            attended.reshape(block_rows, head_count * HEAD).astype(jnp.bfloat16),
            (largest + jnp.log(row_sums))[:, :, 0],
        )

    attended, log_totals = lax.map(one_block, packed)
    return (attended.reshape(cell_count, head_count * HEAD), log_totals)


def attend_back(queries, keys_in, values_in, grad_attended, log_totals, slide_all, alive_all):
    cell_count = queries.shape[0]
    head_count = queries.shape[1] // HEAD
    pieces, block_rows = block_plan(cell_count)
    factor = HEAD ** (-0.5)
    keys_heads = keys_in.reshape(cell_count, head_count, HEAD)
    values_heads = values_in.reshape(cell_count, head_count, HEAD)
    packed = (
        queries.reshape(pieces, block_rows, head_count, HEAD),
        grad_attended.reshape(pieces, block_rows, head_count, HEAD),
        log_totals,
        jnp.arange(cell_count, dtype=jnp.int32).reshape(pieces, block_rows),
        slide_all.reshape(pieces, block_rows),
    )

    def one_block(carried, block_pack):
        grad_keys, grad_values = carried
        query_block, grad_block, log_block, row_index, slide_rows = block_pack
        allowed = allow_mask(row_index, slide_rows, slide_all, alive_all)
        scores = (
            jnp.einsum("qhd,khd->hqk", query_block, keys_heads, preferred_element_type=jnp.float32)
            * factor
        )
        attn_probs = jnp.where(
            allowed[None], jnp.exp(jnp.minimum(scores - log_block[:, :, None], 0.0)), 0.0
        )
        grad_values = grad_values + jnp.einsum(
            "hqk,qhd->khd",
            attn_probs.astype(jnp.bfloat16),
            grad_block,
            preferred_element_type=jnp.float32,
        )
        grad_probs = jnp.einsum(
            "qhd,khd->hqk", grad_block, values_heads, preferred_element_type=jnp.float32
        )
        inner_sum = jnp.sum(attn_probs * grad_probs, axis=2, keepdims=True)
        grad_scores = (attn_probs * (grad_probs - inner_sum)).astype(jnp.bfloat16)
        grad_query = (
            jnp.einsum("hqk,khd->qhd", grad_scores, keys_heads, preferred_element_type=jnp.float32)
            * factor
        )
        grad_keys = (
            grad_keys
            + jnp.einsum(
                "hqk,qhd->khd", grad_scores, query_block, preferred_element_type=jnp.float32
            )
            * factor
        )
        return ((grad_keys, grad_values), grad_query.reshape(block_rows, head_count * HEAD))

    empty_heads = jnp.zeros((cell_count, head_count, HEAD), jnp.float32)
    (grad_keys, grad_values), grad_query = lax.scan(one_block, (empty_heads, empty_heads), packed)
    return (
        grad_query.reshape(cell_count, head_count * HEAD).astype(jnp.bfloat16),
        grad_keys.reshape(cell_count, head_count * HEAD).astype(jnp.bfloat16),
        grad_values.reshape(cell_count, head_count * HEAD).astype(jnp.bfloat16),
    )


def first_forward(weights, gene_rows, places, slide_now, alive_now):
    (
        embed_w,
        gain_one,
        bias_one,
        query_w,
        key_w,
        value_w,
        out_w,
        gain_two,
        bias_two,
        up_w,
        down_w,
    ) = weights[:11]
    feature_count = embed_w.shape[1]
    start = reduce_rows(mat_nn(gene_rows, embed_w)) + position_code(places, feature_count)
    first_full, normed_one, scale_one = layer_norm(
        start, gain_one.astype(jnp.float32), bias_one.astype(jnp.float32)
    )
    first_low = first_full.astype(jnp.bfloat16)
    queries = mat_nn(first_low, query_w).astype(jnp.bfloat16)
    keys_now = mat_nn(first_low, key_w).astype(jnp.bfloat16)
    values_now = mat_nn(first_low, value_w).astype(jnp.bfloat16)
    attended, log_totals = attend(queries, keys_now, values_now, slide_now, alive_now)
    after_attn = start + reduce_rows(mat_nn(attended, out_w))
    second_full, normed_two, scale_two = layer_norm(
        after_attn, gain_two.astype(jnp.float32), bias_two.astype(jnp.float32)
    )
    second_low = second_full.astype(jnp.bfloat16)
    upper = mat_nn(second_low, up_w)
    activated = jax.nn.gelu(upper, approximate=False).astype(jnp.bfloat16)
    result = (after_attn + reduce_rows(mat_nn(activated, down_w))).astype(jnp.bfloat16)
    return (
        result,
        (
            normed_one,
            scale_one,
            first_low,
            queries,
            keys_now,
            values_now,
            attended,
            log_totals,
            normed_two,
            scale_two,
            second_low,
            upper,
            activated,
        ),
    )


def second_forward(weights, hidden, gene_rows, noise_rows, alive_float):
    mean_w, logvar_w, centers_w, spreads_w, dec_w, genes_w = weights[11:]
    means = mat_nn(hidden, mean_w)
    log_vars = mat_nn(hidden, logvar_w)
    latent = means + jnp.exp(0.5 * log_vars) * noise_rows
    latent_low = latent.astype(jnp.bfloat16)
    post_part = jnp.sum(-0.5 * LOG_TWO_PI - 0.5 * log_vars - 0.5 * noise_rows * noise_rows, axis=1)
    centers = centers_w.astype(jnp.float32)
    comp_logs = spreads_w.astype(jnp.float32)
    offsets = latent[None] - centers[:, None, :]
    comp_part = jnp.sum(
        -0.5 * LOG_TWO_PI
        - 0.5 * comp_logs[:, None, :]
        - 0.5 * offsets * offsets * jnp.exp(-comp_logs)[:, None, :],
        axis=2,
    )
    decoder_part = mat_nn(latent_low, dec_w)
    comp_total, log_post, decoder_pre = lax.psum((comp_part, post_part, decoder_part), "mp")
    logits = comp_total - math.log(centers.shape[0])
    largest = jnp.max(logits, axis=0, keepdims=True)
    log_prior = largest[0] + jnp.log(jnp.sum(jnp.exp(logits - largest), axis=0))
    respons = jnp.exp(logits - log_prior[None, :])
    divergence = log_post - log_prior
    decoder_act = jax.nn.gelu(decoder_pre, approximate=False).astype(jnp.bfloat16)
    rebuilt = mat_nn(decoder_act, genes_w)
    residual = (rebuilt - gene_rows.astype(jnp.float32)) * alive_float[:, None]
    return (
        hidden,
        latent,
        log_vars,
        respons,
        latent_low,
        decoder_pre,
        decoder_act,
        residual.astype(jnp.bfloat16),
        (-residual).astype(jnp.bfloat16),
        jnp.sum(divergence * alive_float),
    )


def second_backward(weights, kept, noise_rows, alive_float, kl_scale, grads_in):
    mean_w, logvar_w, centers_w, spreads_w, dec_w, genes_w = weights[11:]
    (
        hidden,
        latent,
        log_vars,
        respons,
        latent_low,
        decoder_pre,
        decoder_act,
        grad_rebuilt,
        target_grad,
        divergence_sum,
    ) = kept
    grads = list(grads_in)
    grads[16] = grads[16] + mat_tn(decoder_act, grad_rebuilt)
    grad_act = lax.psum(mat_nt(grad_rebuilt, genes_w).astype(jnp.bfloat16), "mp").astype(
        jnp.float32
    )
    grad_pre = (grad_act * gelu_slope(decoder_pre)).astype(jnp.bfloat16)
    grads[15] = grads[15] + mat_tn(latent_low, grad_pre)
    grad_latent = mat_nt(grad_pre, dec_w)
    cell_weight = kl_scale * alive_float
    centers = centers_w.astype(jnp.float32)
    comp_logs = spreads_w.astype(jnp.float32)
    offsets = latent[None] - centers[:, None, :]
    pulled = offsets * jnp.exp(-comp_logs)[:, None, :]
    weighted = (respons * cell_weight[None, :])[:, :, None]
    grad_latent = grad_latent + jnp.sum(weighted * pulled, axis=0)
    grads[13] = grads[13] - jnp.sum(weighted * pulled, axis=1)
    grads[14] = grads[14] - jnp.sum(weighted * (0.5 * offsets * pulled - 0.5), axis=1)
    grad_means = grad_latent.astype(jnp.bfloat16)
    grad_logs = (
        grad_latent * (0.5 * jnp.exp(0.5 * log_vars) * noise_rows) - 0.5 * cell_weight[:, None]
    ).astype(jnp.bfloat16)
    grads[11] = grads[11] + mat_tn(hidden, grad_means)
    grads[12] = grads[12] + mat_tn(hidden, grad_logs)
    grad_hidden = lax.psum(
        (mat_nt(grad_means, mean_w) + mat_nt(grad_logs, logvar_w)).astype(jnp.bfloat16), "mp"
    )
    return (grad_hidden, tuple(grads))


def first_backward(weights, kept, gene_rows, grad_result, slide_now, alive_now, grads_in):
    (
        embed_w,
        gain_one,
        bias_one,
        query_w,
        key_w,
        value_w,
        out_w,
        gain_two,
        bias_two,
        up_w,
        down_w,
    ) = weights[:11]
    (
        normed_one,
        scale_one,
        first_low,
        queries,
        keys_now,
        values_now,
        attended,
        log_totals,
        normed_two,
        scale_two,
        second_low,
        upper,
        activated,
    ) = kept
    grads = list(grads_in)
    grads[10] = grads[10] + mat_tn(activated, grad_result)
    grad_upper = (mat_nt(grad_result, down_w) * gelu_slope(upper)).astype(jnp.bfloat16)
    grads[9] = grads[9] + mat_tn(second_low, grad_upper)
    grad_norm_two = reduce_rows(mat_nt(grad_upper, up_w))
    grads[7] = grads[7] + jnp.sum(grad_norm_two * normed_two, axis=0)
    grads[8] = grads[8] + jnp.sum(grad_norm_two, axis=0)
    grad_middle = grad_result.astype(jnp.float32) + norm_back(
        grad_norm_two, normed_two, scale_two, gain_two.astype(jnp.float32)
    )
    middle_low = grad_middle.astype(jnp.bfloat16)
    grads[6] = grads[6] + mat_tn(attended, middle_low)
    grad_attended = mat_nt(middle_low, out_w).astype(jnp.bfloat16)
    grad_query, grad_keys, grad_values = attend_back(
        queries, keys_now, values_now, grad_attended, log_totals, slide_now, alive_now
    )
    grads[3] = grads[3] + mat_tn(first_low, grad_query)
    grads[4] = grads[4] + mat_tn(first_low, grad_keys)
    grads[5] = grads[5] + mat_tn(first_low, grad_values)
    grad_norm_one = reduce_rows(
        mat_nt(grad_query, query_w) + mat_nt(grad_keys, key_w) + mat_nt(grad_values, value_w)
    )
    grads[1] = grads[1] + jnp.sum(grad_norm_one * normed_one, axis=0)
    grads[2] = grads[2] + jnp.sum(grad_norm_one, axis=0)
    grad_start = grad_middle + norm_back(
        grad_norm_one, normed_one, scale_one, gain_one.astype(jnp.float32)
    )
    start_low = grad_start.astype(jnp.bfloat16)
    grads[0] = grads[0] + mat_tn(gene_rows, start_low)
    return (tuple(grads), mat_nt(start_low, embed_w).astype(jnp.bfloat16))


def swap_section(value):
    return from_partner(value, "section", 0)


def place_at(store, index, values):
    return tuple((slot.at[index].set(item) for slot, item in zip(store, values)))


def local(
    expression,
    cell_xy,
    live_mask,
    lengths,
    ramp_step,
    latent_noise,
    gene_embed,
    ln1_gain,
    ln1_bias,
    w_query,
    w_key,
    w_value,
    w_out,
    ln2_gain,
    ln2_bias,
    w_up,
    w_down,
    w_mean,
    w_logvar,
    comp_mean,
    comp_logvar,
    w_dec,
    w_genes,
):
    weights = (
        lax.all_gather(gene_embed, ("section", "dp"), axis=1, tiled=True),
        lax.all_gather(ln1_gain, ("section", "dp"), axis=0, tiled=True),
        lax.all_gather(ln1_bias, ("section", "dp"), axis=0, tiled=True),
        lax.all_gather(w_query, ("section", "dp"), axis=0, tiled=True),
        lax.all_gather(w_key, ("section", "dp"), axis=0, tiled=True),
        lax.all_gather(w_value, ("section", "dp"), axis=0, tiled=True),
        lax.all_gather(w_out, ("section", "dp"), axis=1, tiled=True),
        lax.all_gather(ln2_gain, ("section", "dp"), axis=0, tiled=True),
        lax.all_gather(ln2_bias, ("section", "dp"), axis=0, tiled=True),
        lax.all_gather(w_up, ("section", "dp"), axis=0, tiled=True),
        lax.all_gather(w_down, ("section", "dp"), axis=1, tiled=True),
        lax.all_gather(w_mean, ("section", "dp"), axis=0, tiled=True),
        lax.all_gather(w_logvar, ("section", "dp"), axis=0, tiled=True),
        lax.all_gather(comp_mean, ("section", "dp"), axis=1, tiled=True),
        lax.all_gather(comp_logvar, ("section", "dp"), axis=1, tiled=True),
        lax.all_gather(w_dec, ("section", "dp"), axis=1, tiled=True),
        lax.all_gather(w_genes, ("section", "dp"), axis=0, tiled=True),
    )
    micro_count = lengths.shape[0]
    cell_count = expression.shape[0] // micro_count
    feature_count = weights[1].shape[0]
    gene_cols = expression.shape[1]
    head_cols = weights[3].shape[1]
    unit_cols = weights[9].shape[1]
    latent_cols = weights[11].shape[1]
    comp_count = weights[13].shape[0]
    pieces, block_rows = block_plan(cell_count)
    head_count = head_cols // HEAD
    is_first = lax.axis_index("section") == 0
    floats = jnp.float32
    halves = jnp.bfloat16

    def rows_of(array, index):
        return lax.slice_in_dim(array, index * cell_count, (index + 1) * cell_count, axis=0)

    slides = [slide_ids(lengths[index], cell_count) for index in range(micro_count)]
    alive_int = [rows_of(live_mask, index) for index in range(micro_count)]
    alive_float = [item.astype(floats) for item in alive_int]
    places = [
        lax.slice_in_dim(cell_xy, index * cell_count, (index + 1) * cell_count, axis=1)
        for index in range(micro_count)
    ]

    def blank(shape, kind):
        return jnp.zeros((micro_count,) + shape, kind)

    store_one = (
        blank((cell_count, feature_count), floats),
        blank((cell_count, 1), floats),
        blank((cell_count, feature_count), halves),
        blank((cell_count, head_cols), halves),
        blank((cell_count, head_cols), halves),
        blank((cell_count, head_cols), halves),
        blank((cell_count, head_cols), halves),
        blank((pieces, head_count, block_rows), floats),
        blank((cell_count, feature_count), floats),
        blank((cell_count, 1), floats),
        blank((cell_count, feature_count), halves),
        blank((cell_count, unit_cols), floats),
        blank((cell_count, unit_cols), halves),
    )
    store_two = (
        blank((cell_count, feature_count), halves),
        blank((cell_count, latent_cols), floats),
        blank((cell_count, latent_cols), floats),
        blank((comp_count, cell_count), floats),
        blank((cell_count, latent_cols), halves),
        blank((cell_count, feature_count), floats),
        blank((cell_count, feature_count), halves),
        blank((cell_count, gene_cols), halves),
        blank((cell_count, gene_cols), halves),
        blank((), floats),
    )
    received = jnp.zeros((cell_count, feature_count), halves)
    for moment in range(micro_count + 1):
        outgoing = jnp.zeros_like(received)
        if moment < micro_count:
            first_out, kept = first_forward(
                weights,
                rows_of(expression, moment),
                places[moment],
                slides[moment],
                alive_int[moment],
            )
            store_one = place_at(store_one, moment, kept)
            outgoing = jnp.where(is_first, first_out, outgoing)
        if moment >= 1:
            earlier = moment - 1
            kept = second_forward(
                weights,
                received,
                rows_of(expression, earlier),
                rows_of(latent_noise, earlier),
                alive_float[earlier],
            )
            store_two = place_at(store_two, earlier, kept)
        if moment < micro_count:
            received = swap_section(outgoing)
    divergence_local = jnp.where(is_first, 0.0, jnp.sum(store_two[9]))
    live_local = jnp.sum(live_mask.astype(floats))
    divergence_total, live_total = lax.psum((divergence_local, live_local), "dp")
    mean_kl = divergence_total / (LATENT * live_total)
    ramp_weight = jnp.minimum(1.0, (ramp_step[0] + 1).astype(floats) / RAMP)
    kl_scale = (
        ramp_weight * jax.nn.softplus(mean_kl - FREE_BITS) * jax.nn.sigmoid(mean_kl - FREE_BITS)
    )
    grad_store = jnp.zeros((micro_count, cell_count, gene_cols), halves)
    arriving = jnp.zeros((cell_count, feature_count), halves)
    grads_run = tuple((jnp.zeros(item.shape, floats) for item in weights))
    for moment in range(micro_count + 1):
        backward_grad_store = grad_store
        grads_first = grads_run
        grads_second = grads_run
        backward_outgoing = jnp.zeros_like(arriving)
        if moment >= 1:
            backward_earlier = moment - 1
            backward_kept = tuple((slot[backward_earlier] for slot in store_one))
            grads_first, grad_piece = first_backward(
                weights,
                backward_kept,
                rows_of(expression, backward_earlier),
                arriving,
                slides[backward_earlier],
                alive_int[backward_earlier],
                grads_run,
            )
            backward_grad_store = backward_grad_store.at[backward_earlier].set(grad_piece)
        if moment < micro_count:
            backward_kept = tuple((slot[moment] for slot in store_two))
            sent_back, grads_second = second_backward(
                weights,
                backward_kept,
                rows_of(latent_noise, moment),
                alive_float[moment],
                kl_scale,
                grads_run,
            )
            backward_outgoing = jnp.where(is_first, backward_outgoing, sent_back)
        grads_out = tuple(
            (jnp.where(is_first, early, late) for early, late in zip(grads_first, grads_second))
        )
        outgoing = backward_outgoing
        grads_run = grads_out
        grad_store = backward_grad_store
        if moment < micro_count:
            arriving = swap_section(outgoing)
    grads_run = tuple(grads_run)
    shares = (
        lax.psum_scatter(
            grads_run[0].astype(jnp.bfloat16), ("section", "dp"), scatter_dimension=1, tiled=True
        ).astype(jnp.float32),
        lax.psum_scatter(
            grads_run[1].astype(jnp.bfloat16), ("section", "dp"), scatter_dimension=0, tiled=True
        ).astype(jnp.float32),
        lax.psum_scatter(
            grads_run[2].astype(jnp.bfloat16), ("section", "dp"), scatter_dimension=0, tiled=True
        ).astype(jnp.float32),
        lax.psum_scatter(
            grads_run[3].astype(jnp.bfloat16), ("section", "dp"), scatter_dimension=0, tiled=True
        ).astype(jnp.float32),
        lax.psum_scatter(
            grads_run[4].astype(jnp.bfloat16), ("section", "dp"), scatter_dimension=0, tiled=True
        ).astype(jnp.float32),
        lax.psum_scatter(
            grads_run[5].astype(jnp.bfloat16), ("section", "dp"), scatter_dimension=0, tiled=True
        ).astype(jnp.float32),
        lax.psum_scatter(
            grads_run[6].astype(jnp.bfloat16), ("section", "dp"), scatter_dimension=1, tiled=True
        ).astype(jnp.float32),
        lax.psum_scatter(
            grads_run[7].astype(jnp.bfloat16), ("section", "dp"), scatter_dimension=0, tiled=True
        ).astype(jnp.float32),
        lax.psum_scatter(
            grads_run[8].astype(jnp.bfloat16), ("section", "dp"), scatter_dimension=0, tiled=True
        ).astype(jnp.float32),
        lax.psum_scatter(
            grads_run[9].astype(jnp.bfloat16), ("section", "dp"), scatter_dimension=0, tiled=True
        ).astype(jnp.float32),
        lax.psum_scatter(
            grads_run[10].astype(jnp.bfloat16), ("section", "dp"), scatter_dimension=1, tiled=True
        ).astype(jnp.float32),
        lax.psum_scatter(
            grads_run[11].astype(jnp.bfloat16), ("section", "dp"), scatter_dimension=0, tiled=True
        ).astype(jnp.float32),
        lax.psum_scatter(
            grads_run[12].astype(jnp.bfloat16), ("section", "dp"), scatter_dimension=0, tiled=True
        ).astype(jnp.float32),
        lax.psum_scatter(
            grads_run[13].astype(jnp.bfloat16), ("section", "dp"), scatter_dimension=1, tiled=True
        ).astype(jnp.float32),
        lax.psum_scatter(
            grads_run[14].astype(jnp.bfloat16), ("section", "dp"), scatter_dimension=1, tiled=True
        ).astype(jnp.float32),
        lax.psum_scatter(
            grads_run[15].astype(jnp.bfloat16), ("section", "dp"), scatter_dimension=1, tiled=True
        ).astype(jnp.float32),
        lax.psum_scatter(
            grads_run[16].astype(jnp.bfloat16), ("section", "dp"), scatter_dimension=0, tiled=True
        ).astype(jnp.float32),
    )
    own_part = jnp.where(is_first, grad_store, store_two[8]).reshape(
        micro_count * cell_count, gene_cols
    )
    other_part = swap_section(own_part)
    grad_expression = (own_part.astype(floats) + other_part.astype(floats)).astype(halves)
    return tuple(shares) + (grad_expression,)


def solution(mesh):
    return jax.shard_map(
        local,
        mesh=mesh,
        in_specs=(
            P("dp", "mp"),
            P(None, "dp"),
            P("dp"),
            P("dp", None),
            P(),
            P("dp", "mp"),
            P("mp", ("section", "dp")),
            P(("section", "dp")),
            P(("section", "dp")),
            P(("section", "dp"), "mp"),
            P(("section", "dp"), "mp"),
            P(("section", "dp"), "mp"),
            P("mp", ("section", "dp")),
            P(("section", "dp")),
            P(("section", "dp")),
            P(("section", "dp"), "mp"),
            P("mp", ("section", "dp")),
            P(("section", "dp"), "mp"),
            P(("section", "dp"), "mp"),
            P(None, ("mp", "section", "dp")),
            P(None, ("mp", "section", "dp")),
            P("mp", ("section", "dp")),
            P(("section", "dp"), "mp"),
        ),
        out_specs=(
            P("mp", ("section", "dp")),
            P(("section", "dp")),
            P(("section", "dp")),
            P(("section", "dp"), "mp"),
            P(("section", "dp"), "mp"),
            P(("section", "dp"), "mp"),
            P("mp", ("section", "dp")),
            P(("section", "dp")),
            P(("section", "dp")),
            P(("section", "dp"), "mp"),
            P("mp", ("section", "dp")),
            P(("section", "dp"), "mp"),
            P(("section", "dp"), "mp"),
            P(None, ("mp", "section", "dp")),
            P(None, ("mp", "section", "dp")),
            P("mp", ("section", "dp")),
            P(("section", "dp"), "mp"),
            P("dp", "mp"),
        ),
        check_vma=False,
    )
```

profile of v0, /device:TPU:0, one launch (start us, length us, event | category | flops | bytes accessed | tf_op | source)
XLA Modules:
  0.0 2003.7 jit_solution(7960563660069515738)
XLA Ops:
  8.0 54.1 %all-gather.9.cloned.1.call-done = bf16[3376,1024]{1,0:T(8,128)(2,1)} async-done(((bf16[3376,128]{1,0:T(8,128)(2,1)}), bf16[3376,1024]{1,0:T(8,128)(2,1)}) %all-gather.9.cloned.1.call-update) | async-done | bytes 6914064 | tf_op jit(solution)/shard_map/all_gather | solution.py:419
  62.1 9.3 fusion.31
  71.3 7.1 fusion.35
  79.1 13.6 all-gather
  92.7 12.8 all-gather.1
  106.2 27.0 %all_gather.56 = bf16[1024,256]{1,0:T(8,128)(2,1)} all-gather(bf16[128,256]{1,0:T(8,128)(2,1)S(1)} %copy-done.128), channel_id=1, replica_groups=mesh['section'=2,'mp'=4,'dp'=4] {'section','dp'}, dimensions={0}, use_global_device_ids=true | all-gather | bytes 589824 | tf_op jit(solution)/shard_map/all_gather | solution.py:423
  133.2 26.5 %all_gather.55 = bf16[1024,256]{1,0:T(8,128)(2,1)} all-gather(bf16[128,256]{1,0:T(8,128)(2,1)S(1)} %copy-done.129), channel_id=1, replica_groups=mesh['section'=2,'mp'=4,'dp'=4] {'section','dp'}, dimensions={0}, use_global_device_ids=true | all-gather | bytes 589824 | tf_op jit(solution)/shard_map/all_gather | solution.py:422
  159.7 26.8 %all_gather.54 = bf16[1024,256]{1,0:T(8,128)(2,1)} all-gather(bf16[128,256]{1,0:T(8,128)(2,1)S(1)} %copy-done.130), channel_id=1, replica_groups=mesh['section'=2,'mp'=4,'dp'=4] {'section','dp'}, dimensions={0}, use_global_device_ids=true | all-gather | bytes 589824 | tf_op jit(solution)/shard_map/all_gather | solution.py:424
  186.5 23.4 %all_gather.57 = bf16[256,1024]{1,0:T(8,128)(2,1)S(1)} all-gather(bf16[256,128]{1,0:T(8,128)(2,1)S(1)} %copy-done.131), channel_id=1, replica_groups=mesh['section'=2,'mp'=4,'dp'=4] {'section','dp'}, dimensions={1}, use_global_device_ids=true | all-gather | bytes 589824 | tf_op jit(solution)/shard_map/all_gather | solution.py:425
  210.4 9.1 multiply_sine_fusion.3
  219.5 10.3 all-reduce.37.cloned.1.call-done
  268.7 13.6 all-gather.2
  282.3 13.6 all-gather.3
  295.9 121.8 %all-reduce.35.cloned.1.call-done = (f32[496,1024]{1,0:T(8,128)}, f32[496,1024]{1,0:T(8,128)}) async-done(((f32[496,1024]{1,0:T(8,128)}, f32[496,1024]{1,0:T(8,128)}), (f32[496,1024]{1,0:T(8,128)}, f32[496,1024]{1,0:T(8,128)})) %all-reduce.35.cloned.1.call-update) | async-done | bytes 4063248 | tf_op jit(solution)/shard_map/psum | solution.py:90
  423.0 23.4 %all-gather.11.cloned.1.call-done = bf16[1024,1024]{1,0:T(8,128)(2,1)} async-done(((bf16[128,1024]{1,0:T(8,128)(2,1)}), bf16[1024,1024]{1,0:T(8,128)(2,1)}) %all-gather.11.cloned.1.call-update) | async-done | bytes 2097168 | tf_op jit(solution)/shard_map/all_gather | solution.py:428
  446.4 8.7 fusion.39
  455.2 7.0 fusion.51
  462.2 14.2 all-gather.13.cloned.1.call-done
  476.4 4.3 fusion.200
  484.0 150.4 %all-reduce.33.cloned.1.call-done = (f32[496,1024]{1,0:T(8,128)}, f32[496,1024]{1,0:T(8,128)}) async-done(((f32[496,1024]{1,0:T(8,128)}, f32[496,1024]{1,0:T(8,128)}), (f32[496,1024]{1,0:T(8,128)}, f32[496,1024]{1,0:T(8,128)})) %all-reduce.33.cloned.1.call-update) | async-done | bytes 4063248 | tf_op jit(solution)/shard_map/psum | solution.py:90
  638.4 24.9 %all_gather.63 = bf16[1024,128]{1,0:T(8,128)(2,1)S(1)} all-gather(bf16[128,128]{1,0:T(8,128)(2,1)S(1)} %copy-done.142), channel_id=1, replica_groups=mesh['section'=2,'mp'=4,'dp'=4] {'section','dp'}, dimensions={0}, use_global_device_ids=true | all-gather | bytes 294912 | tf_op jit(solution)/shard_map/all_gather | solution.py:431
  663.3 25.2 %all_gather.62 = bf16[1024,128]{1,0:T(8,128)(2,1)S(1)} all-gather(bf16[128,128]{1,0:T(8,128)(2,1)S(1)} %copy-done.143), channel_id=1, replica_groups=mesh['section'=2,'mp'=4,'dp'=4] {'section','dp'}, dimensions={0}, use_global_device_ids=true | all-gather | bytes 294912 | tf_op jit(solution)/shard_map/all_gather | solution.py:430
  688.5 20.8 %all_gather.64 = bf16[128,1024]{1,0:T(8,128)(2,1)S(1)} all-gather(bf16[128,128]{1,0:T(8,128)(2,1)S(1)} %copy-done.144), channel_id=1, replica_groups=mesh['section'=2,'mp'=4,'dp'=4] {'section','dp'}, dimensions={1}, use_global_device_ids=true | all-gather | bytes 294912 | tf_op jit(solution)/shard_map/all_gather | solution.py:434
  716.1 23.2 %all_gather.66 = bf16[16,128]{0,1:T(8,128)(2,1)S(1)} all-gather(bf16[16,16]{0,1:T(8,128)(2,1)S(1)} %copy.127), channel_id=1, replica_groups=mesh['section'=2,'mp'=4,'dp'=4] {'section','dp'}, dimensions={1}, use_global_device_ids=true | all-gather | bytes 4608 | tf_op jit(solution)/shard_map/all_gather | solution.py:433
  739.4 23.3 %all_gather.67 = bf16[16,128]{0,1:T(8,128)(2,1)S(1)} all-gather(bf16[16,16]{0,1:T(8,128)(2,1)S(1)} %copy.129), channel_id=1, replica_groups=mesh['section'=2,'mp'=4,'dp'=4] {'section','dp'}, dimensions={1}, use_global_device_ids=true | all-gather | bytes 4608 | tf_op jit(solution)/shard_map/all_gather | solution.py:432
  762.8 4.0 fusion.25
  767.1 98.4 %all-reduce.31.cloned.1.call-done = (f32[496,1024]{1,0:T(8,128)}, f32[496,1024]{1,0:T(8,128)}) async-done(((f32[496,1024]{1,0:T(8,128)}, f32[496,1024]{1,0:T(8,128)}), (f32[496,1024]{1,0:T(8,128)}, f32[496,1024]{1,0:T(8,128)})) %all-reduce.31.cloned.1.call-update) | async-done | bytes 4063248 | tf_op jit(solution)/shard_map/psum | solution.py:258
  865.5 12.3 subtract_multiply_fusion.6
  877.8 4.9 fusion.117
  882.7 9.8 subtract_multiply_fusion.7
  895.4 4.9 fusion.114
  907.7 10.5 all-reduce.4
  921.3 5.3 fusion.19
  926.6 62.8 %all-reduce.41.cloned.1.call-done = (bf16[496,1024]{1,0:T(8,128)(2,1)}, bf16[496,1024]{1,0:T(8,128)(2,1)}) async-done(((bf16[496,1024]{1,0:T(8,128)(2,1)}, bf16[496,1024]{1,0:T(8,128)(2,1)}), (bf16[496,1024]{1,0:T(8,128)(2,1)}, bf16[496,1024]{1,0:T(8,128)(2,1)})) %all-reduce.41.cloned.1.call-update) | async-done | bytes 2031632 | tf_op jit(solution)/shard_map/psum | solution.py:297
  998.8 83.6 %all-reduce.39.cloned.1.call-done = (bf16[496,1024]{1,0:T(8,128)(2,1)}, bf16[496,1024]{1,0:T(8,128)(2,1)}) async-done(((bf16[496,1024]{1,0:T(8,128)(2,1)}, bf16[496,1024]{1,0:T(8,128)(2,1)}), (bf16[496,1024]{1,0:T(8,128)(2,1)}, bf16[496,1024]{1,0:T(8,128)(2,1)})) %all-reduce.39.cloned.1.call-update) | async-done | bytes 2031632 | tf_op jit(solution)/shard_map/psum | solution.py:318
  1099.5 148.6 %all-reduce.29.cloned.1.call-done = (f32[496,1024]{1,0:T(8,128)}, f32[496,1024]{1,0:T(8,128)}) async-done(((f32[496,1024]{1,0:T(8,128)}, f32[496,1024]{1,0:T(8,128)}), (f32[496,1024]{1,0:T(8,128)}, f32[496,1024]{1,0:T(8,128)})) %all-reduce.29.cloned.1.call-update) | async-done | bytes 4063248 | tf_op jit(solution)/shard_map/psum | solution.py:90
  1257.9 4.2 fusion.130
  1308.8 3.9 copy.155
  1332.8 13.8 fusion.107
  1349.6 15.1 fusion.1
  1364.7 10.2 copy.163
  1375.0 5.1 fusion.26
  1380.1 5.2 fusion.27
  1385.3 51.5 %all-reduce.27.cloned.1.call-done = (f32[496,1024]{1,0:T(8,128)}, f32[496,1024]{1,0:T(8,128)}) async-done(((f32[496,1024]{1,0:T(8,128)}, f32[496,1024]{1,0:T(8,128)}), (f32[496,1024]{1,0:T(8,128)}, f32[496,1024]{1,0:T(8,128)})) %all-reduce.27.cloned.1.call-update) | async-done | bytes 4063248 | tf_op jit(solution)/shard_map/psum | solution.py:90
  1443.9 8.9 fusion.33
  1452.8 10.3 fusion
  1463.1 10.2 copy.151
  1473.4 7.2 fusion.6
  1480.6 7.4 fusion.7
  1488.0 5.4 maximum_select_fusion
  1496.1 9.4 reduce-scatter.48.cloned.1.call-done
  1506.9 35.4 %reduce-scatter.50.cloned.1.call-done = bf16[128,128]{1,0:T(8,128)(2,1)} async-done(((bf16[1024,128]{1,0:T(8,128)(2,1)}), bf16[128,128]{1,0:T(8,128)(2,1)}) %reduce-scatter.50.cloned.1.call-update) | async-done | bytes 32784
  1543.8 35.0 %reduce-scatter.38.cloned.1.call-done = bf16[128,128]{1,0:T(8,128)(2,1)} async-done(((bf16[1024,128]{1,0:T(8,128)(2,1)}), bf16[128,128]{1,0:T(8,128)(2,1)}) %reduce-scatter.38.cloned.1.call-update) | async-done | bytes 32784 | tf_op jit(solution)/shard_map/reduce_scatter | solution.py:603
  1580.2 35.4 %reduce-scatter.36.cloned.1.call-done = bf16[128,128]{1,0:T(8,128)(2,1)} async-done(((bf16[1024,128]{1,0:T(8,128)(2,1)}), bf16[128,128]{1,0:T(8,128)(2,1)}) %reduce-scatter.36.cloned.1.call-update) | async-done | bytes 32784 | tf_op jit(solution)/shard_map/reduce_scatter | solution.py:600
  1617.0 43.1 %reduce-scatter.44.cloned.1.call-done = bf16[128,1024]{1,0:T(8,128)(2,1)} async-done(((bf16[1024,1024]{1,0:T(8,128)(2,1)}), bf16[128,1024]{1,0:T(8,128)(2,1)}) %reduce-scatter.44.cloned.1.call-update) | async-done | bytes 262160
  1662.1 42.8 %reduce-scatter.34.cloned.1.call-done = bf16[128,1024]{1,0:T(8,128)(2,1)} async-done(((bf16[1024,1024]{1,0:T(8,128)(2,1)}), bf16[128,1024]{1,0:T(8,128)(2,1)}) %reduce-scatter.34.cloned.1.call-update) | async-done | bytes 262160 | tf_op jit(solution)/shard_map/reduce_scatter | solution.py:594
  1706.7 35.4 %reduce-scatter.42.cloned.1.call-done = bf16[128,256]{1,0:T(8,128)(2,1)} async-done(((bf16[1024,256]{1,0:T(8,128)(2,1)}), bf16[128,256]{1,0:T(8,128)(2,1)}) %reduce-scatter.42.cloned.1.call-update) | async-done | bytes 65552
  1743.7 35.9 %reduce-scatter.32.cloned.1.call-done = bf16[128,256]{1,0:T(8,128)(2,1)} async-done(((bf16[1024,256]{1,0:T(8,128)(2,1)}), bf16[128,256]{1,0:T(8,128)(2,1)}) %reduce-scatter.32.cloned.1.call-update) | async-done | bytes 65552 | tf_op jit(solution)/shard_map/reduce_scatter | solution.py:582
  1781.2 36.3 %reduce-scatter.30.cloned.1.call-done = bf16[128,256]{1,0:T(8,128)(2,1)} async-done(((bf16[1024,256]{1,0:T(8,128)(2,1)}), bf16[128,256]{1,0:T(8,128)(2,1)}) %reduce-scatter.30.cloned.1.call-update) | async-done | bytes 65552 | tf_op jit(solution)/shard_map/reduce_scatter | solution.py:579
  1819.0 36.5 %reduce-scatter.28.cloned.1.call-done = bf16[128,256]{1,0:T(8,128)(2,1)} async-done(((bf16[1024,256]{1,0:T(8,128)(2,1)}), bf16[128,256]{1,0:T(8,128)(2,1)}) %reduce-scatter.28.cloned.1.call-update) | async-done | bytes 65552 | tf_op jit(solution)/shard_map/reduce_scatter | solution.py:576
  1856.9 67.5 %reduce-scatter.52.cloned.1.call-done = bf16[128,3376]{1,0:T(8,128)(2,1)} async-done(((bf16[1024,3376]{1,0:T(8,128)(2,1)}), bf16[128,3376]{1,0:T(8,128)(2,1)}) %reduce-scatter.52.cloned.1.call-update) | async-done | bytes 864272
  1927.8 14.6 all-reduce.12
  1944.7 10.0 add_convert_fusion
  1954.7 39.1 %reduce-scatter.40.cloned.1.call-done = bf16[128,3376]{1,0:T(8,128)(2,1)} async-done(((bf16[1024,3376]{1,0:T(8,128)(2,1)}), bf16[128,3376]{1,0:T(8,128)(2,1)}) %reduce-scatter.40.cloned.1.call-update) | async-done | bytes 864272
  (618 shorter events, 209.1 us)
Async XLA Ops:
  7.2 54.9 %all-gather.9.cloned.1.call-start = ((), (), s32[]{:S(2)}) async-start(), calls=%async_computation.13 | async-start | bytes 7778304 | tf_op jit(solution)/shard_map/all_gather | solution.py:419
  7.9 221.9 %all-reduce.37.cloned.1.call-start = ((), (), s32[]{:S(2)}) async-start(), calls=%async_computation.36 | async-start | bytes 8126464 | tf_op jit(solution)/shard_map/psum | solution.py:90
  78.5 27.0 %copy-start.168 = (s32[2,3]{1,0:T(2,128)S(1)}, s32[2,3]{1,0:T(2,128)}, u32[]{:S(2)}) copy-start(s32[2,3]{1,0:T(2,128)} %param.122) | copy-start | bytes 76
  78.5 27.6 %copy-start.118 = (s32[992]{0:T(1024)S(1)}, s32[992]{0:T(1024)}, u32[]{:S(2)}) copy-start(s32[992]{0:T(1024)} %param.121) | copy-start | bytes 11908
  78.5 27.7 %copy-start.163 = (f32[2,992]{1,0:T(2,128)S(1)}, f32[2,992]{1,0:T(2,128)}, u32[]{:S(2)}) copy-start(f32[2,992]{1,0:T(2,128)} %param.120) | copy-start | bytes 23812
  78.5 27.7 %copy-start.128 = (bf16[128,256]{1,0:T(8,128)(2,1)S(1)}, bf16[128,256]{1,0:T(8,128)(2,1)}, u32[]{:S(2)}) copy-start(bf16[128,256]{1,0:T(8,128)(2,1)} %param.129) | copy-start | bytes 196612
  78.5 54.8 %copy-start.129 = (bf16[128,256]{1,0:T(8,128)(2,1)S(1)}, bf16[128,256]{1,0:T(8,128)(2,1)}, u32[]{:S(2)}) copy-start(bf16[128,256]{1,0:T(8,128)(2,1)} %param.128) | copy-start | bytes 196612
  78.5 81.2 %copy-start.130 = (bf16[128,256]{1,0:T(8,128)(2,1)S(1)}, bf16[128,256]{1,0:T(8,128)(2,1)}, u32[]{:S(2)}) copy-start(bf16[128,256]{1,0:T(8,128)(2,1)} %param.130) | copy-start | bytes 196612
  78.5 108.0 %copy-start.131 = (bf16[256,128]{1,0:T(8,128)(2,1)S(1)}, bf16[256,128]{1,0:T(8,128)(2,1)}, u32[]{:S(2)}) copy-start(bf16[256,128]{1,0:T(8,128)(2,1)} %param.131) | copy-start | bytes 196612
  78.6 339.2 %all-reduce.35.cloned.1.call-start = ((), (), s32[]{:S(2)}) async-start(), calls=%async_computation.35 | async-start | bytes 8126464 | tf_op jit(solution)/shard_map/psum | solution.py:90
  92.7 142.7 %copy-start.116 = (f32[8,1,128]{2,1,0:T(1,128)}, f32[8,1,128]{2,1,0:T(1,128)S(1)}, u32[]{:S(2)}) copy-start(f32[8,1,128]{2,1,0:T(1,128)S(1)} %convert_element_type.545) | copy-start | bytes 12292
  209.9 55.1 %copy-start.23 = (bf16[256,1024]{1,0:T(8,128)(2,1)}, bf16[256,1024]{1,0:T(8,128)(2,1)S(1)}, u32[]{:S(2)}) copy-start(bf16[256,1024]{1,0:T(8,128)(2,1)S(1)} %all_gather.57) | copy-start | bytes 1572868
  210.1 46.5 %copy-start.38 = (pred[496,496]{0,1:T(8,128)(4,1)}, pred[496,496]{0,1:T(8,128)(4,1)S(1)}, u32[]{:S(2)}) copy-start(pred[496,496]{0,1:T(8,128)(4,1)S(1)} %fusion.146) | copy-start | bytes 738052
  210.4 52.2 %copy-start.40 = (pred[496,496]{0,1:T(8,128)(4,1)}, pred[496,496]{0,1:T(8,128)(4,1)S(1)}, u32[]{:S(2)}) copy-start(pred[496,496]{0,1:T(8,128)(4,1)S(1)} %fusion.147) | copy-start | bytes 738052
  232.3 185.4 %copy-start = (f32[496,1024]{1,0:T(8,128)}, f32[496,1024]{1,0:T(8,128)S(1)}, u32[]{:S(2)}) copy-start(f32[496,1024]{1,0:T(8,128)S(1)} %get-tuple-element.802) | copy-start | bytes 6094852
  267.5 179.0 %all-gather.11.cloned.1.call-start = ((), (), s32[]{:S(2)}) async-start(), calls=%async_computation.14 | async-start | bytes 2359296 | tf_op jit(solution)/shard_map/all_gather | solution.py:428
  268.1 208.3 %all-gather.13.cloned.1.call-start = ((), (), s32[]{:S(2)}) async-start(), calls=%async_computation.15 | async-start | bytes 2359296 | tf_op jit(solution)/shard_map/all_gather | solution.py:429
  268.7 365.8 %all-reduce.33.cloned.1.call-start = ((), (), s32[]{:S(2)}) async-start(), calls=%async_computation.34 | async-start | bytes 8126464 | tf_op jit(solution)/shard_map/psum | solution.py:90
  282.3 968.9 %copy-start.125 = (f32[8,1,128]{2,1,0:T(1,128)}, f32[8,1,128]{2,1,0:T(1,128)S(1)}, u32[]{:S(2)}) copy-start(f32[8,1,128]{2,1,0:T(1,128)S(1)} %convert_element_type.547) | copy-start | bytes 12292
  295.9 159.2 %copy-start.166 = (f32[8,1,128]{2,1,0:T(1,128)}, f32[8,1,128]{2,1,0:T(1,128)S(1)}, u32[]{:S(2)}) copy-start(f32[8,1,128]{2,1,0:T(1,128)S(1)} %convert_element_type.548) | copy-start | bytes 12292
  421.1 830.2 %copy-start.149 = (f32[496]{0:T(512)}, f32[496]{0:T(512)S(1)}, u32[]{:S(2)}) copy-start(f32[496]{0:T(512)S(1)} %broadcast_multiply_fusion.14) | copy-start | bytes 5956
  421.1 830.2 %copy-start.145 = (f32[496]{0:T(512)}, f32[496]{0:T(512)S(1)}, u32[]{:S(2)}) copy-start(f32[496]{0:T(512)S(1)} %broadcast_multiply_fusion.12) | copy-start | bytes 5956
  423.0 828.3 %copy-start.154 = (f32[496]{0:T(512)}, f32[496]{0:T(512)S(1)}, u32[]{:S(2)}) copy-start(f32[496]{0:T(512)S(1)} %add_rsqrt_fusion.2) | copy-start | bytes 5956
  423.0 828.3 %copy-start.152 = (f32[496]{0:T(512)}, f32[496]{0:T(512)S(1)}, u32[]{:S(2)}) copy-start(f32[496]{0:T(512)S(1)} %add_rsqrt_fusion) | copy-start | bytes 5956
  455.2 21.2 %copy-start.81 = (bf16[496,1024]{1,0:T(8,128)(2,1)}, bf16[496,1024]{1,0:T(8,128)(2,1)S(1)}, u32[]{:S(2)}) copy-start(bf16[496,1024]{1,0:T(8,128)(2,1)S(1)} %get-tuple-element.843) | copy-start | bytes 3047428
  483.2 283.8 %all-gather.15.cloned.1.call-start = ((), (), s32[]{:S(2)}) async-start(), calls=%async_computation.16 | async-start | bytes 7778304 | tf_op jit(solution)/shard_map/all_gather | solution.py:435
  484.0 381.5 %all-reduce.31.cloned.1.call-start = ((), (), s32[]{:S(2)}) async-start(), calls=%async_computation.33 | async-start | bytes 8126464 | tf_op jit(solution)/shard_map/psum | solution.py:258
  637.3 72.0 %collective-permute-start = (bf16[496,1024]{1,0:T(8,128)(2,1)S(1)}, bf16[496,1024]{1,0:T(8,128)(2,1)S(1)}, u32[]{:S(2)}, u32[]{:S(2)}) collective-permute-start(bf16[496,1024]{1,0:T(8,128)(2,1)S(1)} %fusion.142), channel_id=1, source_target_pairs={{0,16},{16,0},{1,17},{17,1},{2,18},{18,2},{3,19},{19,3},{4,20},{20... | collective-permute-start | bytes 3047432 | tf_op jit(solution)/shard_map/ppermute | solution.py:19
  637.4 25.9 %copy-start.143 = (bf16[128,128]{1,0:T(8,128)(2,1)S(1)}, bf16[128,128]{1,0:T(8,128)(2,1)}, u32[]{:S(2)}) copy-start(bf16[128,128]{1,0:T(8,128)(2,1)} %param.136) | copy-start | bytes 98308
  637.4 51.1 %copy-start.144 = (bf16[128,128]{1,0:T(8,128)(2,1)S(1)}, bf16[128,128]{1,0:T(8,128)(2,1)}, u32[]{:S(2)}) copy-start(bf16[128,128]{1,0:T(8,128)(2,1)} %param.140) | copy-start | bytes 98308
  637.9 71.9 %copy-start.84 = (f32[992,128]{1,0:T(8,128)S(1)}, f32[992,128]{1,0:T(8,128)}, u32[]{:S(2)}) copy-start(f32[992,128]{1,0:T(8,128)} %param.124) | copy-start | bytes 1523716
  637.9 72.3 %collective-permute-start.1 = (bf16[496,1024]{1,0:T(8,128)(2,1)S(1)}, bf16[496,1024]{1,0:T(8,128)(2,1)S(1)}, u32[]{:S(2)}, u32[]{:S(2)}) collective-permute-start(bf16[496,1024]{1,0:T(8,128)(2,1)S(1)} %fusion.143), channel_id=1, source_target_pairs={{0,16},{16,0},{1,17},{17,1},{2,18},{18,2},{3,19},{19,3},{4,20},{20... | collective-permute-start | bytes 3047432 | tf_op jit(solution)/shard_map/ppermute | solution.py:19
  663.3 46.9 %copy-start.52 = (bf16[1024,128]{1,0:T(8,128)(2,1)}, bf16[1024,128]{1,0:T(8,128)(2,1)S(1)}, u32[]{:S(2)}) copy-start(bf16[1024,128]{1,0:T(8,128)(2,1)S(1)} %all_gather.63) | copy-start | bytes 786436
  688.5 22.9 %copy-start.36 = (bf16[1024,128]{1,0:T(8,128)(2,1)}, bf16[1024,128]{1,0:T(8,128)(2,1)S(1)}, u32[]{:S(2)}) copy-start(bf16[1024,128]{1,0:T(8,128)(2,1)S(1)} %all_gather.62) | copy-start | bytes 786436
  715.3 24.0 %copy-start.165 = (bf16[16,16]{1,0:T(8,128)(2,1)S(1)}, bf16[16,16]{1,0:T(8,128)(2,1)}, u32[]{:S(2)}) copy-start(bf16[16,16]{1,0:T(8,128)(2,1)} %param.138) | copy-start | bytes 1540
  715.4 186.5 %all-reduce.25.cloned.1.call-start = ((), (), s32[]{:S(2)}) async-start(), calls=%async_computation.30 | async-start | bytes 139264 | tf_op jit(solution)/shard_map/psum | solution.py:258
  766.8 222.5 %all-reduce.41.cloned.1.call-start = ((), (), s32[]{:S(2)}) async-start(), calls=%async_computation.38 | async-start | bytes 4063232 | tf_op jit(solution)/shard_map/psum | solution.py:297
  900.3 182.1 %all-reduce.39.cloned.1.call-start = ((), (), s32[]{:S(2)}) async-start(), calls=%async_computation.37 | async-start | bytes 4063232 | tf_op jit(solution)/shard_map/psum | solution.py:318
  998.8 249.3 %all-reduce.29.cloned.1.call-start = ((), (), s32[]{:S(2)}) async-start(), calls=%async_computation.32 | async-start | bytes 8126464 | tf_op jit(solution)/shard_map/psum | solution.py:90
  1082.5 3.5 collective-permute-start.3
  1083.8 8.3 collective-permute-start.2
  1097.6 339.2 %all-reduce.27.cloned.1.call-start = ((), (), s32[]{:S(2)}) async-start(), calls=%async_computation.31 | async-start | bytes 8126464 | tf_op jit(solution)/shard_map/psum | solution.py:90
  1286.5 208.3 %reduce-scatter.46.cloned.1.call-start = ((), (), s32[]{:S(2)}) async-start(), calls=%async_computation.26 | async-start | bytes 36864
  1289.4 216.1 %reduce-scatter.48.cloned.1.call-start = ((), (), s32[]{:S(2)}) async-start(), calls=%async_computation.27 | async-start | bytes 36864
  1292.2 250.1 %reduce-scatter.50.cloned.1.call-start = ((), (), s32[]{:S(2)}) async-start(), calls=%async_computation.28 | async-start | bytes 294912
  1296.8 282.0 %reduce-scatter.38.cloned.1.call-start = ((), (), s32[]{:S(2)}) async-start(), calls=%async_computation.22 | async-start | bytes 294912 | tf_op jit(solution)/shard_map/reduce_scatter | solution.py:603
  1300.8 314.8 %reduce-scatter.36.cloned.1.call-start = ((), (), s32[]{:S(2)}) async-start(), calls=%async_computation.21 | async-start | bytes 294912 | tf_op jit(solution)/shard_map/reduce_scatter | solution.py:600
  1303.4 356.8 %reduce-scatter.44.cloned.1.call-start = ((), (), s32[]{:S(2)}) async-start(), calls=%async_computation.25 | async-start | bytes 2359296
  1312.8 392.0 %reduce-scatter.34.cloned.1.call-start = ((), (), s32[]{:S(2)}) async-start(), calls=%async_computation.20 | async-start | bytes 2359296 | tf_op jit(solution)/shard_map/reduce_scatter | solution.py:594
  1318.8 423.3 %reduce-scatter.42.cloned.1.call-start = ((), (), s32[]{:S(2)}) async-start(), calls=%async_computation.24 | async-start | bytes 589824
  1325.1 454.5 %reduce-scatter.32.cloned.1.call-start = ((), (), s32[]{:S(2)}) async-start(), calls=%async_computation.19 | async-start | bytes 589824 | tf_op jit(solution)/shard_map/reduce_scatter | solution.py:582
  1329.2 488.2 %reduce-scatter.30.cloned.1.call-start = ((), (), s32[]{:S(2)}) async-start(), calls=%async_computation.18 | async-start | bytes 589824 | tf_op jit(solution)/shard_map/reduce_scatter | solution.py:579
  1332.7 522.7 %reduce-scatter.28.cloned.1.call-start = ((), (), s32[]{:S(2)}) async-start(), calls=%async_computation.17 | async-start | bytes 589824 | tf_op jit(solution)/shard_map/reduce_scatter | solution.py:576
  1349.2 575.3 %reduce-scatter.52.cloned.1.call-start = ((), (), s32[]{:S(2)}) async-start(), calls=%async_computation.29 | async-start | bytes 7962624
  1375.0 618.9 %reduce-scatter.40.cloned.1.call-start = ((), (), s32[]{:S(2)}) async-start(), calls=%async_computation.23 | async-start | bytes 7962624
  1380.1 56.7 %copy-start.1 = (f32[496,1024]{1,0:T(8,128)S(1)}, f32[496,1024]{1,0:T(8,128)}, u32[]{:S(2)}) copy-start(f32[496,1024]{1,0:T(8,128)} %copy-done) | copy-start | bytes 6094852
  1380.1 56.7 %copy-start.117 = (f32[8,1,128]{2,1,0:T(1,128)S(1)}, f32[8,1,128]{2,1,0:T(1,128)}, u32[]{:S(2)}) copy-start(f32[8,1,128]{2,1,0:T(1,128)} %copy-done.116) | copy-start | bytes 12292
  1380.1 56.7 %copy-start.133 = (f32[496]{0:T(512)S(1)}, f32[496]{0:T(512)}, u32[]{:S(2)}) copy-start(f32[496]{0:T(512)} %copy-done.132) | copy-start | bytes 5956
  1380.1 56.7 %copy-start.137 = (f32[496]{0:T(512)S(1)}, f32[496]{0:T(512)}, u32[]{:S(2)}) copy-start(f32[496]{0:T(512)} %copy-done.136) | copy-start | bytes 5956
  1493.4 213.3 %copy-start.158 = (f32[1024]{0:T(1024)S(1)}, f32[1024]{0:T(1024)}, u32[]{:S(2)}) copy-start(f32[1024]{0:T(1024)} %get-tuple-element.745) | copy-start | bytes 12292
  1493.4 213.3 %copy-start.160 = (f32[1024]{0:T(1024)S(1)}, f32[1024]{0:T(1024)}, u32[]{:S(2)}) copy-start(f32[1024]{0:T(1024)} %get-tuple-element.744) | copy-start | bytes 12292
  1493.4 213.3 %copy-start.157 = (f32[1024]{0:T(1024)S(1)}, f32[1024]{0:T(1024)}, u32[]{:S(2)}) copy-start(f32[1024]{0:T(1024)} %get-tuple-element.734) | copy-start | bytes 12292
  1493.4 213.3 %copy-start.159 = (f32[1024]{0:T(1024)S(1)}, f32[1024]{0:T(1024)}, u32[]{:S(2)}) copy-start(f32[1024]{0:T(1024)} %get-tuple-element.732) | copy-start | bytes 12292
  1493.4 451.3 %collective-permute-start.4 = (bf16[992,3376]{1,0:T(8,128)(2,1)}, bf16[992,3376]{1,0:T(8,128)(2,1)}, u32[]{:S(2)}, u32[]{:S(2)}) collective-permute-start(bf16[992,3376]{1,0:T(8,128)(2,1)} %bitcast.55), channel_id=1, source_target_pairs={{0,16},{16,0},{1,17},{17,1},{2,18},{18,2},{3,19},{19,3},{4,20},{20... | collective-permute-start | bytes 20093960 | tf_op jit(solution)/shard_map/ppermute | solution.py:19
  (154 other events, 451.8 us)
Sparse Core Ops, SparseCore 0:
  9.9 52.1 all-gather.8
  78.7 151.0 all-reduce.36
  267.6 150.1 all-reduce.34
  419.5 26.8 all-gather.10
  448.2 28.1 all-gather.12
  483.4 151.0 all-reduce.32
  636.4 54.4 all-gather.14
  715.5 149.9 all-reduce.30
  868.6 33.2 all-reduce.24
  904.9 84.4 all-reduce.40
  998.9 83.4 all-reduce.38
  1097.7 150.3 all-reduce.28
  1286.6 150.1 all-reduce.26
  1440.5 30.2 reduce-scatter.45
  1474.2 31.2 reduce-scatter.47
  1508.7 33.5 reduce-scatter.49
  1545.2 33.5 reduce-scatter.37
  1582.0 33.5 reduce-scatter.35
  1618.9 41.1 reduce-scatter.43
  1663.6 41.2 reduce-scatter.33
  1708.0 34.1 reduce-scatter.41
  1745.5 34.1 reduce-scatter.31
  1783.3 34.1 reduce-scatter.29
  1821.3 34.1 reduce-scatter.27
  1859.0 65.4 reduce-scatter.51
  1928.3 65.5 reduce-scatter.39
where the time goes:
time: 2010 us; the launch traced here: 2000 us
  waiting for transfers between devices  1280 us (64%)
  blocking collectives  300 us (15%)
  matrix products  222 us (11%)
  other arithmetic  107 us (5%)
  local copies, waits for them, and re-layouts  74 us (4%)
  between operations  20.6 us (1%)
    psum x5, waiting for transfers between devices, reduce_rows(): return lax.psum(partial_value, 'mp')  483 us
    unnamed x33, waiting for transfers between devices  233 us
    psum x2, waiting for transfers between devices, second_forward(): lax.psum((comp_part, post_part, decoder_part), 'mp')  98.6 us
    psum x1, waiting for transfers between devices, second_backward(): lax.psum((mat_nt(grad_means, mean_w) + mat_nt(grad_logs, logvar_w)).astyp...  83.6 us
    dot_general x22, matrix products, mat_tn(): lax.dot_general(left, right, (((0,), (0,)), ((), ())), preferred_element_...  78.2 us
    dot_general x22, matrix products, mat_nn(): return jnp.dot(left, right, preferred_element_type=jnp.float32)  77.2 us
    psum x1, waiting for transfers between devices, second_backward(): lax.psum(mat_nt(grad_rebuilt, genes_w).astype(jnp.bfloat16), 'mp')  62.8 us
    unnamed x391, local copies, waits for them, and re-layouts  61.9 us
  transfers between devices with their start and end apart: 31, of which 25 were waited for; matrix products, arithmetic and copies ran while one was open for 14% of the time, Pallas kernels for 0%

commit v1 on v0

v1 whole, which is shorter than its diff:
```python
import functools
import math

import jax
import jax.numpy as jnp
from jax import lax
from jax.experimental import pallas as pl
from jax.experimental.pallas import tpu as pltpu
from jax.sharding import PartitionSpec as P

HEAD = 64
LATENT = 512
RAMP = 1000
LOG_TWO_PI = 1.8378770664093453
NEG_LARGE = -1e30
FREE_BITS = 1.0
HOP_LAG = 3
F32 = jnp.float32
BF16 = jnp.bfloat16


def mat_nn(left, right):
    return jnp.dot(left, right, preferred_element_type=F32)


def mat_tn(left, right):
    return lax.dot_general(left, right, (((0,), (0,)), ((), ())), preferred_element_type=F32)


def mat_nt(left, right):
    return lax.dot_general(left, right, (((1,), (1,)), ((), ())), preferred_element_type=F32)


def gelu(values):
    return 0.5 * values * (1.0 + lax.erf(values * 0.7071067811865476))


def gelu_slope(values):
    return (
        0.5 * (1.0 + lax.erf(values * 0.7071067811865476))
        + values * jnp.exp(-0.5 * values * values) * 0.3989422804014327
    )


def normalize(values):
    center = values - jnp.mean(values, axis=-1, keepdims=True)
    scale = lax.rsqrt(jnp.mean(center * center, axis=-1, keepdims=True) + 1e-05)
    return center * scale, scale


def norm_back(grad_in, normed, scale, gain):
    scaled = grad_in * gain
    return scale * (
        scaled
        - jnp.mean(scaled, axis=-1, keepdims=True)
        - normed * jnp.mean(scaled * normed, axis=-1, keepdims=True)
    )


def position_code(places, feature_count):
    quarter = feature_count // 4
    frequency = jnp.exp(jnp.arange(quarter, dtype=F32) * (-math.log(10000.0) / quarter))
    along_x = places[0][:, None] * frequency[None, :]
    along_y = places[1][:, None] * frequency[None, :]
    return jnp.concatenate(
        [jnp.sin(along_x), jnp.cos(along_x), jnp.sin(along_y), jnp.cos(along_y)], axis=1
    )


def allowed_pairs(length_row, alive):
    cell_count = alive.shape[0]
    bounds = jnp.cumsum(length_row)[:-1]
    index = jnp.arange(cell_count, dtype=jnp.int32)
    slide = jnp.sum((index[:, None] >= bounds[None, :]).astype(jnp.int32), axis=1)
    return (slide[:, None] == slide[None, :]) & (
        (alive[None, :] == 1) | (index[:, None] == index[None, :])
    )


def heads_of(array):
    return array.reshape(array.shape[0], -1, HEAD)


def attend(queries, keys, values, allowed):
    factor = HEAD ** (-0.5)
    scores = (
        jnp.einsum("qhd,khd->hqk", heads_of(queries), heads_of(keys), preferred_element_type=F32)
        * factor
    )
    scores = jnp.where(allowed[None], scores, NEG_LARGE)
    largest = jnp.max(scores, axis=2, keepdims=True)
    exponents = jnp.exp(scores - largest)
    sums = jnp.sum(exponents, axis=2, keepdims=True)
    probs = (exponents / sums).astype(BF16)
    out = jnp.einsum("hqk,khd->qhd", probs, heads_of(values), preferred_element_type=F32)
    return out.reshape(queries.shape).astype(BF16), largest + jnp.log(sums)


def attend_back(queries, keys, values, grad_out, log_totals, allowed):
    factor = HEAD ** (-0.5)
    q, k, v, g = heads_of(queries), heads_of(keys), heads_of(values), heads_of(grad_out)
    scores = jnp.einsum("qhd,khd->hqk", q, k, preferred_element_type=F32) * factor
    probs = jnp.where(allowed[None], jnp.exp(jnp.minimum(scores - log_totals, 0.0)), 0.0)
    grad_values = jnp.einsum("hqk,qhd->khd", probs.astype(BF16), g, preferred_element_type=F32)
    grad_probs = jnp.einsum("qhd,khd->hqk", g, v, preferred_element_type=F32)
    inner = jnp.sum(probs * grad_probs, axis=2, keepdims=True)
    grad_scores = (probs * (grad_probs - inner)).astype(BF16)
    grad_query = jnp.einsum("hqk,khd->qhd", grad_scores, k, preferred_element_type=F32) * factor
    grad_keys = jnp.einsum("hqk,qhd->khd", grad_scores, q, preferred_element_type=F32) * factor
    return tuple(
        item.reshape(queries.shape).astype(BF16) for item in (grad_query, grad_keys, grad_values)
    )


def part_of(ref, axis, index, size):
    span = pl.ds(index * size, size)
    if axis == 0:
        return ref.at[span, :]
    return ref.at[:, pl.ds(pl.multiple_of(index * size, 128), size)]


def line_sum(part, out, from_left, from_right, to_right, to_left, got_left, got_right, sent_right, sent_left):
    me, count = lax.axis_index("mp"), lax.axis_size("mp")
    pieces, _, width = from_left.shape
    inner_right, inner_left = me < count - 1, me > 0

    def columns(piece):
        return pl.ds(pl.multiple_of(piece * width, width), width)

    def flow(piece, has_source, has_target, source, target, arrived, left, neighbour):
        copy = pltpu.make_async_remote_copy(
            src_ref=target.at[piece],
            dst_ref=source.at[piece],
            send_sem=left.at[piece],
            recv_sem=arrived.at[piece],
            device_id={"mp": neighbour},
        )

        def advance():
            @pl.when(has_source)
            def _():
                copy.wait_recv()

            @pl.when(has_target)
            def _():
                target[piece] = (
                    part[:, columns(piece)] + source[piece].astype(F32)
                ).astype(BF16)
                copy.start()

        return copy, advance

    def rightward(piece):
        return flow(
            piece, inner_left, inner_right, from_left, to_right, got_left, sent_right, me + 1
        )

    def leftward(piece):
        return flow(
            piece, inner_right, inner_left, from_right, to_left, got_right, sent_left, me - 1
        )

    def start():
        @pl.when(me == 0)
        def _():
            from_left[...] = jnp.zeros_like(from_left)

        @pl.when(me == count - 1)
        def _():
            from_right[...] = jnp.zeros_like(from_right)

        def step(moment, carry):
            right_piece = moment - HOP_LAG * me
            left_piece = moment - HOP_LAG * (count - 1 - me)

            @pl.when((right_piece >= 0) & (right_piece < pieces))
            def _():
                rightward(right_piece)[1]()

            @pl.when((left_piece >= 0) & (left_piece < pieces))
            def _():
                leftward(left_piece)[1]()

            return carry

        lax.fori_loop(0, pieces + HOP_LAG * (count - 1), step, 0)

    def finish():
        def step(piece, carry):
            out[:, columns(piece)] = (
                part[:, columns(piece)]
                + from_left[piece].astype(F32)
                + from_right[piece].astype(F32)
            )

            @pl.when(inner_right)
            def _():
                rightward(piece)[0].wait_send()

            @pl.when(inner_left)
            def _():
                leftward(piece)[0].wait_send()

            return carry

        lax.fori_loop(0, pieces, step, 0)

    return start, finish


def comm_kernel(plan, *refs):
    refs = list(refs)

    def take(number):
        taken = refs[:number]
        del refs[:number]
        return taken

    reduces, gathers, swaps, exchanges, shares, pairs = plan
    sources = [take(n) for n in (reduces, len(gathers), len(swaps), len(exchanges), shares, pairs)]
    results = [take(n) for n in (reduces, len(gathers), len(swaps), len(exchanges), shares, pairs)]
    line = take(8) if reduces else None
    sent, got, local_sem = refs

    section, z, dp = (lax.axis_index(name) for name in ("section", "mp", "dp"))
    count_z, count_dp = lax.axis_size("mp"), lax.axis_size("dp")
    row, col = dp // 2, dp % 2
    peers = [row * 2 + (1 - col), (1 - row) * 2 + col, (1 - row) * 2 + (1 - col)]
    partner = {"section": 1 - section}

    barrier = pltpu.get_barrier_semaphore()
    fixed = 0
    if gathers or swaps or pairs:
        pl.semaphore_signal(barrier, inc=1, device_id=partner)
        fixed += 1
    if gathers or exchanges:
        for peer in peers:
            pl.semaphore_signal(barrier, inc=1, device_id={"dp": peer})
        fixed += len(peers)
    if shares:
        for step in range(1, count_z):
            pl.semaphore_signal(barrier, inc=1, device_id={"mp": (z + step) % count_z})
        fixed += count_z - 1
    elif reduces:
        for exists, neighbour in ((z > 0, z - 1), (z < count_z - 1, z + 1)):

            @pl.when(exists)
            def _(neighbour=neighbour):
                pl.semaphore_signal(barrier, inc=1, device_id={"mp": neighbour})

        at_end = (z == 0) | (z == count_z - 1)

        @pl.when(at_end)
        def _():
            pl.semaphore_wait(barrier, fixed + 1)

        @pl.when(jnp.logical_not(at_end))
        def _():
            pl.semaphore_wait(barrier, fixed + 2)

    if fixed and (shares or not reduces):
        pl.semaphore_wait(barrier, fixed)

    used = [0, 0]

    def remote(src, dst, device):
        index = used[0]
        used[0] += 1
        return pltpu.make_async_remote_copy(
            src_ref=src, dst_ref=dst, send_sem=sent.at[index], recv_sem=got.at[index], device_id=device
        )

    def within(src, dst):
        index = used[1]
        used[1] += 1
        return pltpu.make_async_copy(src, dst, local_sem.at[index])

    first, relays, locals_ = [], [], []
    for item, (axis, size) in enumerate(swaps):
        src, dst = sources[2][item], results[2][item]
        first.append(remote(part_of(src, axis, 1 - section, size), dst, partner))
    for item, (axis, size) in enumerate(gathers):
        src, dst = sources[1][item], results[1][item]
        mine = section * count_dp + dp
        locals_.append(within(src, part_of(dst, axis, mine, size)))
        first.append(remote(src, part_of(dst, axis, mine, size), partner))
    for item in range(shares):
        src, dst = sources[4][item], results[4][item]
        locals_.append(within(src, dst.at[z]))
        for step in range(1, count_z):
            first.append(remote(src, dst.at[z], {"mp": (z + step) % count_z}))
    for item in range(pairs):
        src, dst = sources[5][item], results[5][item]
        rows = src.shape[0]
        locals_.append(within(src, part_of(dst, 0, section, rows)))
        first.append(remote(src, part_of(dst, 0, section, rows), partner))
    for peer in peers:
        for item, (axis, size) in enumerate(gathers):
            src, dst = sources[1][item], results[1][item]
            mine = section * count_dp + dp
            copy = remote(src, part_of(dst, axis, mine, size), {"dp": peer})
            held = part_of(dst, axis, section * count_dp + peer, size)
            first.append(copy)
            relays.append((copy, remote(held, held, partner)))
        for item, (axis, size) in enumerate(exchanges):
            src, dst = sources[3][item], results[3][item]
            first.append(remote(part_of(src, axis, peer, size), dst.at[dp], {"dp": peer}))
    for item, (axis, size) in enumerate(exchanges):
        src, dst = sources[3][item], results[3][item]
        locals_.append(within(part_of(src, axis, dp, size), dst.at[dp]))

    for copy in first + locals_:
        copy.start()
    if reduces:
        start, finish = line_sum(sources[0][0], results[0][0], *line)
        start()
    for copy, relay in relays:
        copy.wait_recv()
        relay.start()
    if reduces:
        finish()
    relayed = [copy for copy, _ in relays]
    for copy in first:
        copy.wait_send()
        if not any(copy is other for other in relayed):
            copy.wait_recv()
    for _, relay in relays:
        relay.wait()
    for copy in locals_:
        copy.wait()


def comm(number, reduce=None, gathers=(), swaps=(), exchanges=(), shares=(), pairs=()):
    count_dp, count_z = lax.axis_size("dp"), lax.axis_size("mp")
    sections = lax.axis_size("section")

    def resized(shape, axis, size):
        return shape[:axis] + (size,) + shape[axis + 1 :]

    inputs, outputs, scratch = [], [], []
    plan_gathers, plan_swaps, plan_exchanges = [], [], []
    remote_count = local_count = 0
    if reduce is not None:
        rows, width = reduce.shape
        inputs.append(reduce)
        outputs.append(jax.ShapeDtypeStruct((rows, width), F32))
        buffer = pltpu.VMEM((width // 128, rows, 128), BF16)
        scratch += [buffer] * 4 + [pltpu.SemaphoreType.DMA((width // 128,))] * 4
    for shard, axis in gathers:
        size = shard.shape[axis]
        inputs.append(shard)
        outputs.append(
            jax.ShapeDtypeStruct(resized(shard.shape, axis, size * sections * count_dp), shard.dtype)
        )
        plan_gathers.append((axis, size))
        remote_count += 1 + 2 * (count_dp - 1)
        local_count += 1
    for array, axis in swaps:
        size = array.shape[axis] // sections
        inputs.append(array)
        outputs.append(jax.ShapeDtypeStruct(resized(array.shape, axis, size), array.dtype))
        plan_swaps.append((axis, size))
        remote_count += 1
    for array, axis in exchanges:
        size = array.shape[axis] // count_dp
        inputs.append(array)
        outputs.append(
            jax.ShapeDtypeStruct((count_dp,) + resized(array.shape, axis, size), array.dtype)
        )
        plan_exchanges.append((axis, size))
        remote_count += count_dp - 1
        local_count += 1
    for array in shares:
        inputs.append(array)
        outputs.append(jax.ShapeDtypeStruct((count_z,) + array.shape, array.dtype))
        remote_count += count_z - 1
        local_count += 1
    for array in pairs:
        inputs.append(array)
        outputs.append(
            jax.ShapeDtypeStruct(resized(array.shape, 0, array.shape[0] * sections), array.dtype)
        )
        remote_count += 1
        local_count += 1
    reduces = 0 if reduce is None else 1
    scratch += [
        pltpu.SemaphoreType.DMA((max(remote_count, 1),)),
        pltpu.SemaphoreType.DMA((max(remote_count, 1),)),
        pltpu.SemaphoreType.DMA((max(local_count, 1),)),
    ]
    plan = (reduces, tuple(plan_gathers), tuple(plan_swaps), tuple(plan_exchanges), len(shares), len(pairs))
    vmem, anywhere = pl.BlockSpec(memory_space=pltpu.VMEM), pl.BlockSpec(memory_space=pl.ANY)
    outs = pl.pallas_call(
        functools.partial(comm_kernel, plan),
        out_shape=outputs,
        in_specs=[vmem] * reduces + [anywhere] * (len(inputs) - reduces),
        out_specs=[vmem] * reduces + [anywhere] * (len(inputs) - reduces),
        scratch_shapes=scratch,
        compiler_params=pltpu.CompilerParams(
            collective_id=number, has_side_effects=True, vmem_limit_bytes=48 * 2**20
        ),
        cost_estimate=pl.CostEstimate(flops=1000000, bytes_accessed=90000000, transcendentals=0),
        name="meet",
    )(*inputs)
    outs = list(outs)
    split = []
    for number_of in (reduces, len(gathers), len(swaps), len(exchanges), len(shares), len(pairs)):
        split.append(outs[:number_of])
        outs = outs[number_of:]
    return split


def meet(tiled, number, reduce=None, gathers=(), swaps=(), exchanges=(), shares=(), pairs=()):
    if tiled:
        return comm(number, reduce, gathers, swaps, exchanges, shares, pairs)
    partner = [(i, 1 - i) for i in range(2)]
    section, count_dp = lax.axis_index("section"), lax.axis_size("dp")
    swapped = []
    for array, axis in swaps:
        size = array.shape[axis] // 2
        half = lax.dynamic_slice_in_dim(array, (1 - section) * size, size, axis)
        swapped.append(lax.ppermute(half, "section", partner))
    exchanged = [
        lax.all_to_all(jnp.stack(jnp.split(array, count_dp, axis)), "dp", 0, 0)
        for array, axis in exchanges
    ]
    return [
        [] if reduce is None else comm(number, reduce)[0][0:1],
        [lax.all_gather(shard, ("section", "dp"), axis=axis, tiled=True) for shard, axis in gathers],
        swapped,
        exchanged,
        [lax.all_gather(array, "mp") for array in shares],
        [lax.all_gather(array, "section", axis=0, tiled=True) for array in pairs],
    ]


def half_sum(array, received, axis):
    size = received.shape[axis]
    own = lax.dynamic_slice_in_dim(array, lax.axis_index("section") * size, size, axis)
    return (own.astype(F32) + received.astype(F32)).astype(array.dtype)


def total(parts):
    return jnp.sum(parts.astype(F32), axis=0)


def local(
    expression,
    cell_xy,
    live_mask,
    lengths,
    ramp_step,
    latent_noise,
    gene_embed,
    ln1_gain,
    ln1_bias,
    w_query,
    w_key,
    w_value,
    w_out,
    ln2_gain,
    ln2_bias,
    w_up,
    w_down,
    w_mean,
    w_logvar,
    comp_mean,
    comp_logvar,
    w_dec,
    w_genes,
):
    micro_count = lengths.shape[0]
    cells = expression.shape[0] // micro_count
    micro = lax.axis_index("section")
    latent_cols = w_mean.shape[1]
    comp_count, comp_width = comp_mean.shape
    width = ln1_gain.shape[0]
    shards = 2 * lax.axis_size("dp")
    features = shards * width
    gene_cols = expression.shape[1]
    tiled = width % 128 == 0 and lax.axis_size("dp") == 4
    meeting = functools.partial(meet, tiled)

    def own(array, axis=0):
        return lax.dynamic_slice_in_dim(array, micro * cells, cells, axis)

    genes_in = own(expression)
    alive = own(live_mask)
    alive_float = alive.astype(F32)
    noise = own(latent_noise)
    allowed = allowed_pairs(lax.dynamic_index_in_dim(lengths, micro, 0, False), alive)
    positions = position_code(own(cell_xy, 1), features)

    norm_block = jnp.pad(jnp.stack([ln1_gain, ln1_bias, ln2_gain, ln2_bias]), ((0, 12), (0, 0)))
    comp_block = jnp.pad(
        jnp.concatenate([comp_mean, comp_logvar], axis=0), ((0, 0), (0, width - comp_width))
    )
    small = jnp.concatenate([norm_block, comp_block], axis=0)
    small_rows = small.shape[0]
    _, (embed, small_all), _, _, _, _ = meeting(0, gathers=((gene_embed, 1), (small, 0)))
    small_all = small_all.reshape(shards, small_rows, width).astype(F32)
    norm_params = small_all[:, :4].transpose(1, 0, 2).reshape(4, features)
    gain_one, bias_one, gain_two, bias_two = (norm_params[i : i + 1] for i in range(4))
    comps = small_all[:, 16:, :comp_width].transpose(1, 0, 2).reshape(2 * comp_count, -1)
    centers, spreads = comps[:comp_count], comps[comp_count:]

    qkv_shard = jnp.concatenate([w_query, w_key, w_value], axis=1)
    (summed,), (qkv, out_w, up_w), _, _, _, _ = meeting(
        1, mat_nn(genes_in, embed), gathers=((qkv_shard, 0), (w_out, 1), (w_up, 0))
    )
    start = summed + positions
    normed_one, scale_one = normalize(start)
    first_low = (normed_one * gain_one + bias_one).astype(BF16)
    projected = mat_nn(first_low, qkv).astype(BF16)
    queries, keys, values = jnp.split(projected, 3, axis=1)
    attended, log_totals = attend(queries, keys, values, allowed)
    latent_shard = jnp.concatenate([w_mean, w_logvar], axis=1)
    (summed,), (down_w, latent_w, dec_w), _, _, _, _ = meeting(
        2, mat_nn(attended, out_w), gathers=((w_down, 1), (latent_shard, 0), (w_dec, 1))
    )
    after_attn = start + summed
    normed_two, scale_two = normalize(after_attn)
    second_low = (normed_two * gain_two + bias_two).astype(BF16)
    upper = mat_nn(second_low, up_w)
    activated = gelu(upper).astype(BF16)
    (summed,), (genes_w,), _, _, _, _ = meeting(
        3, mat_nn(activated, down_w), gathers=((w_genes, 0),)
    )
    hidden = (after_attn + summed).astype(BF16)

    stats = mat_nn(hidden, latent_w)
    means, log_vars = stats[:, :latent_cols], stats[:, latent_cols:]
    spread = jnp.exp(0.5 * log_vars) * noise
    latent = means + spread
    latent_low = latent.astype(BF16)
    post_part = jnp.sum(-0.5 * LOG_TWO_PI - 0.5 * log_vars - 0.5 * noise * noise, axis=1)
    precision = jnp.exp(-spreads)
    offsets = latent[None] - centers[:, None, :]
    pulled = offsets * precision[:, None, :]
    comp_part = jnp.sum(
        -0.5 * LOG_TWO_PI - 0.5 * spreads[:, None, :] - 0.5 * offsets * pulled, axis=2
    )
    density_part = jnp.pad(
        jnp.concatenate([comp_part, post_part[None]], axis=0), ((0, 7), (0, -cells % 128))
    )
    (decoder_pre,), _, _, _, (density_parts,), _ = meeting(
        4, mat_nn(latent_low, dec_w), shares=(density_part,)
    )
    densities = jnp.sum(density_parts, axis=0)[:, :cells]
    logits = densities[:comp_count] - math.log(comp_count)
    log_post = densities[comp_count]
    largest = jnp.max(logits, axis=0, keepdims=True)
    log_prior = largest[0] + jnp.log(jnp.sum(jnp.exp(logits - largest), axis=0))
    respons = jnp.exp(logits - log_prior[None, :])
    divergence = jnp.sum((log_post - log_prior) * alive_float)
    decoder_act = gelu(decoder_pre).astype(BF16)
    residual = (mat_nn(decoder_act, genes_w) - genes_in.astype(F32)) * alive_float[:, None]
    grad_rebuilt = residual.astype(BF16)

    grad_genes = mat_tn(decoder_act, grad_rebuilt).astype(BF16)
    counts = jnp.concatenate(
        [jnp.full((1, 128), divergence), jnp.full((7, 128), jnp.sum(alive_float))], axis=0
    )
    (grad_act,), (count_parts,), (genes_other,), _, _, _ = meeting(
        5, mat_nt(grad_rebuilt, genes_w), gathers=((counts, 0),), swaps=((grad_genes, 0),)
    )
    count_parts = jnp.sum(count_parts.reshape(shards, 8, 128)[:, :, 0], axis=0)
    mean_kl = count_parts[0] / (LATENT * count_parts[1])
    ramp_weight = jnp.minimum(1.0, (ramp_step[0] + 1).astype(F32) / RAMP)
    kl_scale = (
        ramp_weight * jax.nn.softplus(mean_kl - FREE_BITS) * jax.nn.sigmoid(mean_kl - FREE_BITS)
    )
    grad_pre = (grad_act * gelu_slope(decoder_pre)).astype(BF16)
    grad_dec = mat_tn(latent_low, grad_pre).astype(BF16)
    cell_weight = kl_scale * alive_float
    weighted = (respons * cell_weight[None, :])[:, :, None]
    grad_latent = mat_nt(grad_pre, dec_w) + jnp.sum(weighted * pulled, axis=0)
    grad_comps = jnp.concatenate(
        [
            -jnp.sum(weighted * pulled, axis=1),
            -jnp.sum(weighted * (0.5 * offsets * pulled - 0.5), axis=1),
        ],
        axis=0,
    )
    grad_means = grad_latent.astype(BF16)
    grad_logs = (grad_latent * (0.5 * spread) - 0.5 * cell_weight[:, None]).astype(BF16)
    grad_stats = jnp.concatenate([grad_means, grad_logs], axis=1)
    grad_latent_w = mat_tn(hidden, grad_stats).astype(BF16)
    cut = gene_cols // 256 * 128
    genes_sum_a = half_sum(grad_genes[:, :cut], genes_other[:, :cut], 0)
    genes_sum_b = half_sum(grad_genes[:, cut:], genes_other[:, cut:], 0)
    (summed,), _, (latent_other, dec_other), (genes_parts_a,), _, _ = meeting(
        6,
        mat_nt(grad_stats, latent_w),
        swaps=((grad_latent_w, 0), (grad_dec, 1)),
        exchanges=((genes_sum_a, 0),),
    )
    grad_hidden = summed.astype(BF16)

    grad_down = mat_tn(activated, grad_hidden).astype(BF16)
    grad_upper = (mat_nt(grad_hidden, down_w) * gelu_slope(upper)).astype(BF16)
    grad_up = mat_tn(second_low, grad_upper).astype(BF16)
    (grad_norm_two,), _, (down_other, up_other), (genes_parts_b, latent_parts, dec_parts), _, _ = (
        meeting(
            7,
            mat_nt(grad_upper, up_w),
            swaps=((grad_down, 1), (grad_up, 0)),
            exchanges=(
                (genes_sum_b, 0),
                (half_sum(grad_latent_w, latent_other, 0), 0),
                (half_sum(grad_dec, dec_other, 1), 1),
            ),
        )
    )
    grad_middle = grad_hidden.astype(F32) + norm_back(
        grad_norm_two, normed_two, scale_two, gain_two
    )
    middle_low = grad_middle.astype(BF16)
    grad_out = mat_tn(attended, middle_low).astype(BF16)
    grad_attended = mat_nt(middle_low, out_w).astype(BF16)
    grad_qkv_act = jnp.concatenate(
        attend_back(queries, keys, values, grad_attended, log_totals, allowed), axis=1
    )
    grad_qkv = mat_tn(first_low, grad_qkv_act).astype(BF16)
    (grad_norm_one,), _, (qkv_other, out_other), (down_parts, up_parts), _, _ = meeting(
        8,
        mat_nt(grad_qkv_act, qkv),
        swaps=((grad_qkv, 0), (grad_out, 1)),
        exchanges=((half_sum(grad_down, down_other, 1), 1), (half_sum(grad_up, up_other, 0), 0)),
    )
    grad_start = grad_middle + norm_back(grad_norm_one, normed_one, scale_one, gain_one)
    start_low = grad_start.astype(BF16)

    norm_grads = jnp.stack(
        [
            jnp.sum(grad_norm_one * normed_one, axis=0),
            jnp.sum(grad_norm_one, axis=0),
            jnp.sum(grad_norm_two * normed_two, axis=0),
            jnp.sum(grad_norm_two, axis=0),
        ]
    )
    norm_grads = norm_grads.reshape(4, shards, width).transpose(1, 0, 2)
    comp_grads = grad_comps.reshape(2 * comp_count, shards, comp_width).transpose(1, 0, 2)
    small_grads = jnp.concatenate(
        [
            jnp.pad(norm_grads, ((0, 0), (0, 12), (0, 0))),
            jnp.pad(comp_grads, ((0, 0), (0, 0), (0, width - comp_width))),
        ],
        axis=1,
    ).reshape(shards * small_rows, width)
    _, _, (start_other, small_other), _, _, _ = meeting(
        9, swaps=((start_low, 1), (small_grads, 0))
    )
    start_mine = lax.dynamic_slice_in_dim(start_low, micro * (features // 2), features // 2, 1)
    start_half = jnp.concatenate(
        [
            jnp.where(micro == 0, start_mine, start_other),
            jnp.where(micro == 0, start_other, start_mine),
        ],
        axis=0,
    )
    grad_embed = mat_tn(expression, start_half).astype(BF16)
    grad_cells = (
        mat_nt(start_low, embed).astype(BF16).astype(F32) + (-residual).astype(BF16).astype(F32)
    ).astype(BF16)
    _, _, _, (embed_parts, qkv_parts, out_parts, small_parts), _, (grad_expression,) = meeting(
        10,
        exchanges=(
            (grad_embed, 1),
            (half_sum(grad_qkv, qkv_other, 0), 0),
            (half_sum(grad_out, out_other, 1), 1),
            (half_sum(small_grads, small_other, 0), 0),
        ),
        pairs=(grad_cells,),
    )
    small_sum = total(small_parts)
    grad_query, grad_key, grad_value = jnp.split(total(qkv_parts), 3, axis=1)
    grad_mean, grad_logvar = jnp.split(total(latent_parts), 2, axis=1)
    return (
        total(embed_parts),
        small_sum[0],
        small_sum[1],
        grad_query,
        grad_key,
        grad_value,
        total(out_parts),
        small_sum[2],
        small_sum[3],
        total(up_parts),
        total(down_parts),
        grad_mean,
        grad_logvar,
        small_sum[16 : 16 + comp_count, :comp_width],
        small_sum[16 + comp_count :, :comp_width],
        total(dec_parts),
        jnp.concatenate([total(genes_parts_a), total(genes_parts_b)], axis=1),
        grad_expression,
    )


def solution(mesh):
    weight_rows = P(("section", "dp"), "mp")
    weight_cols = P("mp", ("section", "dp"))
    vector = P(("section", "dp"))
    comps = P(None, ("mp", "section", "dp"))
    weights = (
        weight_cols, vector, vector, weight_rows, weight_rows, weight_rows, weight_cols,
        vector, vector, weight_rows, weight_cols, weight_rows, weight_rows, comps, comps,
        weight_cols, weight_rows,
    )
    return jax.shard_map(
        local,
        mesh=mesh,
        in_specs=(P("dp", "mp"), P(None, "dp"), P("dp"), P("dp", None), P(), P("dp", "mp"))
        + weights,
        out_specs=weights + (P("dp", "mp"),),
        check_vma=False,
    )
```

time: 2010 us -> 613 us (0.30)
  waiting for transfers between devices: 1280 us -> 0 us
  Pallas kernels: 0 us -> 437 us
  blocking collectives: 300 us -> 0 us
  matrix products: 222 us -> 88.2 us
  other arithmetic: 107 us -> 43.6 us
  local copies, waits for them, and re-layouts: 74 us -> 36.3 us
    psum x9 -> x0, waiting for transfers between devices: 728 us -> none  [the longest x5 483 us: reduce_rows(): return lax.psum(partial_value, 'mp')]
    pallas_call x0 -> x11, Pallas kernels: none -> 437 us  [comm(): pl.pallas_call(functools.partial(comm_kernel, plan), out_shape=outputs, i...]
    all_gather x13 -> x0, blocking collectives: 274 us -> none  [the longest x1 27 us: local(): lax.all_gather(w_key, ('section', 'dp'), axis=0, tiled=True)]
    unnamed x33 -> x0, waiting for transfers between devices: 233 us -> none
    reduce_scatter x6 -> x0, waiting for transfers between devices: 222 us -> none  [the longest x1 42.8 us: local(): lax.psum_scatter(grads_run[9].astype(jnp.bfloat16), ('section', 'dp'), sc...]
    all_gather x4 -> x0, waiting for transfers between devices: 91.7 us -> none  [the longest x1 54.1 us: local(): lax.all_gather(gene_embed, ('section', 'dp'), axis=1, tiled=True)]
    dot_general x34 -> x14, matrix products: 97.9 us -> 34 us  [the longest x8 25.4 us: mat_nn(): return jnp.dot(left, right, preferred_element_type=F32)]
    dot_general x22 -> x8, matrix products: 78.2 us -> 25.5 us  [mat_tn(): lax.dot_general(left, right, (((0,), (0,)), ((), ())), preferred_element_...]
  transfers between devices with their start and end apart: 31 -> 0, of which waited for: 25 -> 0; matrix products, arithmetic and copies ran while one was open for 14% -> 0% of each run, Pallas kernels for 0% -> 0%
where the time goes in v1:
time: 613 us; the launch traced here: 610 us
  Pallas kernels  437 us (71%)
  matrix products  88.2 us (14%)
  other arithmetic  43.6 us (7%)
  local copies, waits for them, and re-layouts  36.3 us (6%)
    pallas_call x11, Pallas kernels, comm(): pl.pallas_call(functools.partial(comm_kernel, plan), out_shape=outputs, i...  437 us
    dot_general x8, matrix products, mat_nt(): lax.dot_general(left, right, (((1,), (1,)), ((), ())), preferred_element_...  28.7 us
    unnamed x218, local copies, waits for them, and re-layouts  26.6 us
    dot_general x8, matrix products, mat_tn(): lax.dot_general(left, right, (((0,), (0,)), ((), ())), preferred_element_...  25.5 us
    dot_general x8, matrix products, mat_nn(): return jnp.dot(left, right, preferred_element_type=F32)  25.4 us

profile of v1, /device:TPU:0, one launch (start us, length us, event | category | flops | bytes accessed | tf_op | source)
XLA Modules:
  0.0 609.7 jit_solution(13789183566158575902)
XLA Ops:
  2.1 1.2 copy-done.20
  3.3 45.5 %meet.11 = (bf16[3376,1024]{1,0:T(8,128)(2,1)}, bf16[384,128]{1,0:T(8,128)(2,1)S(1)}) custom-call(bf16[3376,128]{1,0:T(8,128)(2,1)S(1)} %copy-done.20, bf16[48,128]{1,0:T(8,128)(2,1)S(1)} %pad_maximum_fusion.9.refs_1_), custom_call_target="tpu_custom_call" | custom-call | flops 1000000 | bytes 90000000 | tf_op jit(solution)/shard_map/meet/pallas_call | solution.py:393
  48.8 9.2 %fusion.11.refs_0_ = f32[496,1024]{1,0:T(8,128)} fusion(bf16[3376,1024]{1,0:T(8,128)(2,1)} %get-tuple-element.57, bf16[992,3376]{1,0:T(8,128)(2,1)} %param.23, s32[]{:T(128)S(6)} %select_n.48), kind=kOutput, calls=%fused_computation.32 | convolution fusion | flops 3429367808 | bytes 12374020 | tf_op jit(solution)/shard_map/dot_general | solution.py:23
  58.1 44.7 %meet.12 = (f32[496,1024]{1,0:T(8,128)S(1)}, bf16[1024,768]{1,0:T(8,128)(2,1)S(1)}, bf16[256,1024]{1,0:T(8,128)(2,1)S(1)}, bf16[1024,1024]{1,0:T(8,128)(2,1)}) custom-call(f32[496,1024]{1,0:T(8,128)} %fusion.11.refs_0_, bf16[128,768]{1,0:T(8,128)(2,1)S(1)} %pad_maximum_fusion.5.refs_1_, bf16[256,128]{1,0:T(8,128)(2,1)S(1)} %copy-done.28, ...), custom_call_target="tpu_custom_call" | custom-call | flops 1000000 | bytes 90000000 | tf_op jit(solution)/shard_map/meet/pallas_call | solution.py:393
  102.8 1.3 copy-done.6
  104.2 3.6 multiply_sine_fusion.1
  108.6 1.1 convolution_convert_fusion.6
  111.1 1.0 select_reduce_fusion
  112.1 0.9 fusion.10
  113.1 1.3 fusion.36
  115.5 41.9 %meet.13 = (f32[496,1024]{1,0:T(8,128)S(1)}, bf16[1024,1024]{1,0:T(8,128)(2,1)}, bf16[1024,256]{1,0:T(8,128)(2,1)S(1)}, bf16[128,1024]{1,0:T(8,128)(2,1)S(1)}) custom-call(f32[496,1024]{1,0:T(8,128)S(1)} %fusion.87.refs_0_, bf16[1024,128]{1,0:T(8,128)(2,1)S(1)} %copy-done.23, bf16[128,256]{1,0:T(8,128)(2,1)S(1)} %pad_maximum_fusion.8.refs_2_, ...), custom_call_target="tpu_custom_call" | custom-call | flops 1000000 | bytes 90000000 | tf_op jit(solution)/shard_map/meet/pallas_call | solution.py:393
  158.1 1.6 copy-done.97
  159.8 2.9 multiply_convert_fusion.2
  162.7 0.9 copy-done.101
  163.6 2.5 fusion.88.refs_0_
  166.1 0.9 copy.84.refs_1_
  167.1 1.6 copy-done.5
  168.6 44.7 %meet.14 = (f32[496,1024]{1,0:T(8,128)S(1)}, bf16[1024,3376]{1,0:T(8,128)(2,1)}) custom-call(f32[496,1024]{1,0:T(8,128)S(1)} %copy-done.5, bf16[128,3376]{1,0:T(8,128)(2,1)S(1)} %copy.84.refs_1_), custom_call_target="tpu_custom_call" | custom-call | flops 1000000 | bytes 90000000 | tf_op jit(solution)/shard_map/meet/pallas_call | solution.py:393
  214.3 1.0 copy-done.66
  217.1 2.1 fusion.7
  219.9 40.9 %meet.15 = (f32[496,1024]{1,0:T(8,128)S(1)}, f32[4,24,512]{2,1,0:T(8,128)S(1)}) custom-call(f32[496,1024]{1,0:T(8,128)S(1)} %fusion.49.refs_0_, f32[24,512]{1,0:T(8,128)S(1)} %select_maximum_fusion.1.refs_1_), custom_call_target="tpu_custom_call" | custom-call | flops 1000000 | bytes 90000000 | tf_op jit(solution)/shard_map/meet/pallas_call | solution.py:393
  260.8 1.3 copy-done.2
  262.2 1.4 fusion.77
  264.3 8.4 %subtract_multiply_fusion = f32[496,3376]{1,0:T(8,128)S(1)} fusion(bf16[1024,3376]{1,0:T(8,128)(2,1)} %get-tuple-element.69, f32[496]{0:T(512)S(1)} %get-tuple-element.148, bf16[992,3376]{1,0:T(8,128)(2,1)} %param.23, s32[]{:T(128)S(6)} %select_n.48, f32[496,1024]{1,0:T(8,128)} %copy-done.2), kind=kOutput, calls=%fused_computation.4 | convolution fusion | flops 3436930816 | bytes 18994628 | tf_op jit(solution)/shard_map/dot_general | solution.py:23
  272.7 8.7 %fusion.29.refs_0_ = f32[496,1024]{1,0:T(8,128)S(1)} fusion(bf16[1024,3376]{1,0:T(8,128)(2,1)} %get-tuple-element.69, f32[496,3376]{1,0:T(8,128)S(1)} %subtract_multiply_fusion), kind=kOutput, calls=%fused_computation.77 | convolution fusion | flops 3431042304 | bytes 15643648 | tf_op jit(solution)/shard_map/dot_general | solution.py:31
  281.4 1.3 concatenate.49
  282.8 6.2 %convolution_convert_fusion.refs_2_ = bf16[1024,3376]{1,0:T(8,128)(2,1)} fusion(f32[496,3376]{1,0:T(8,128)S(1)} %subtract_multiply_fusion, f32[496,1024]{1,0:T(8,128)S(1)} %copy-done.3), kind=kOutput, calls=%fused_computation | convolution fusion | flops 3437038848 | bytes 15643648 | tf_op jit(solution)/shard_map/dot_general | solution.py:27
  288.9 38.2 %meet.16 = (f32[496,1024]{1,0:T(8,128)S(1)}, f32[64,128]{1,0:T(8,128)S(1)}, bf16[512,3376]{1,0:T(8,128)(2,1)}) custom-call(f32[496,1024]{1,0:T(8,128)S(1)} %fusion.29.refs_0_, f32[8,128]{1,0:T(8,128)S(1)} %concatenate.50.refs_1_, bf16[1024,3376]{1,0:T(8,128)(2,1)} %convolution_convert_fusion.refs_2_), custom_call_target="tpu_custom_call" | custom-call | flops 1000000 | bytes 90000000 | tf_op jit(solution)/shard_map/meet/pallas_call | solution.py:393
  327.2 1.3 copy-done.4
  330.8 3.2 fusion.3
  334.0 2.2 fusion.18
  336.7 1.8 fusion.47.refs_0_
  339.4 2.0 slice.135
  341.5 2.4 add_convert_fusion.2.refs_3_
  343.8 42.7 %meet.17 = (f32[496,1024]{1,0:T(8,128)}, bf16[512,256]{1,0:T(8,128)(2,1)S(1)}, bf16[128,512]{1,0:T(8,128)(2,1)S(1)}, bf16[4,128,1664]{2,1,0:T(8,128)(2,1)S(1)}) custom-call(f32[496,1024]{1,0:T(8,128)} %fusion.47.refs_0_, bf16[1024,256]{1,0:T(8,128)(2,1)S(1)} %convolution_convert_fusion.8.refs_1_, bf16[128,1024]{1,0:T(8,128)(2,1)S(1)} %convolution_convert_fusion.9.refs_2_, ...), custom_call_target="tpu_custom_call" | custom-call | flops 1000000 | bytes 90000000 | tf_op jit(solution)/shard_map/meet/pallas_call | solution.py:393
  386.6 4.1 fusion.24
  390.7 2.6 fusion.90.refs_0_
  393.4 2.7 convolution_convert_fusion.4.refs_1_
  396.1 2.8 convolution_convert_fusion.3.refs_2_
  398.9 2.0 slice-done.2
  401.0 1.1 copy-done.53
  402.0 1.7 add_convert_fusion.1.refs_3_
  403.9 41.2 %meet.18 = (f32[496,1024]{1,0:T(8,128)}, bf16[1024,512]{1,0:T(8,128)(2,1)S(1)}, bf16[512,1024]{1,0:T(8,128)(2,1)S(1)}, bf16[4,128,1712]{2,1,0:T(8,128)(2,1)S(1)}...) custom-call(f32[496,1024]{1,0:T(8,128)} %fusion.90.refs_0_, ...), custom_call_target="tpu_custom_call" | custom-call | flops 1000000 | bytes 90000000 | tf_op jit(solution)/shard_map/meet/pallas_call | solution.py:393
  445.8 3.9 multiply_reduce_fusion.1
  450.4 1.3 copy-done.40
  452.7 3.4 fusion.31
  456.1 1.8 multiply_reduce_fusion
  457.9 1.3 multiply_convert_fusion
  460.8 2.3 fusion.44.refs_0_
  463.2 2.4 convolution_convert_fusion.5.refs_1_
  466.1 0.7 copy-done.19
  468.4 41.4 %meet.19 = (f32[496,1024]{1,0:T(8,128)}, bf16[512,768]{1,0:T(8,128)(2,1)S(1)}, bf16[256,512]{1,0:T(8,128)(2,1)S(1)}, bf16[4,1024,128]{2,1,0:T(8,128)(2,1)S(1)}, bf16[4,128,1024]{2,1,0:T(8,128)(2,1)S(1)}) custom-call(f32[496,1024]{1,0:T(8,128)} %fusion.44.refs_0_, bf16[1024,768]{1,0:T(8,128)(2,1)} %convolution_convert_fusion.5.refs_1_, ...), custom_call_target="tpu_custom_call" | custom-call | flops 1000000 | bytes 90000000 | tf_op jit(solution)/shard_map/meet/pallas_call | solution.py:393
  509.9 3.3 multiply_reduce_fusion.2
  514.2 2.1 meet.20
  516.5 10.1 %fusion.2.refs_0_ = bf16[3376,512]{1,0:T(8,128)(2,1)} fusion(bf16[992,3376]{1,0:T(8,128)(2,1)} %param.23, bf16[496,512]{1,0:T(8,128)(2,1)S(1)} %get-tuple-element.154, bf16[496,512]{1,0:T(8,128)(2,1)S(1)} %get-tuple-element.153), kind=kOutput, calls=%fused_computation.11 | convolution fusion | flops 3433127936 | bytes 11170816 | tf_op jit(solution)/shard_map/dot_general | solution.py:27
  527.7 8.3 %add_convert_fusion.refs_4_ = bf16[496,3376]{1,0:T(8,128)(2,1)S(1)} fusion(bf16[496,1024]{1,0:T(8,128)(2,1)S(1)} %add_convert_fusion.5.refs_0_, bf16[3376,1024]{1,0:T(8,128)(2,1)} %get-tuple-element.57, f32[496,3376]{1,0:T(8,128)} %copy-done.104), kind=kOutput, calls=%fused_computation.2 | convolution fusion | flops 3441089280 | bytes 17976832 | tf_op jit(solution)/shard_map/dot_general | solution.py:31
  536.0 53.5 %meet.21 = (bf16[4,3376,128]{2,1,0:T(8,128)(2,1)}, bf16[4,128,768]{2,1,0:T(8,128)(2,1)S(1)}, bf16[4,256,128]{2,1,0:T(8,128)(2,1)S(1)}, f32[4,48,128]{2,1,0:T(8,128)S(1)}, bf16[992,3376]{1,0:T(8,128)(2,1)}) custom-call(bf16[3376,512]{1,0:T(8,128)(2,1)} %fusion.2.refs_0_, bf16[512,768]{1,0:T(8,128)(2,1)S(1)} %add_convert_fusion.9.refs_1_, ...), custom_call_target="tpu_custom_call" | custom-call | flops 1000000 | bytes 90000000 | tf_op jit(solution)/shard_map/meet/pallas_call | solution.py:393
  589.6 4.0 convert_reduce_fusion
  594.1 1.3 convert_reduce_fusion.5
  595.5 0.8 fusion.81
  596.9 1.0 convert_reduce_fusion.4
  597.9 0.9 convert_reduce_fusion.3
  601.4 1.7 copy.92
  603.1 6.3 %copy.103 = bf16[992,3376]{1,0:T(8,128)(2,1)} copy(bf16[992,3376]{1,0:T(8,128)(2,1)} %get-tuple-element.233) | data formatting | bytes 13395968
  (294 shorter events, 23.0 us)
Async XLA Ops:
  0.7 109.4 %copy-start = (s32[2,3]{1,0:T(2,128)S(1)}, s32[2,3]{1,0:T(2,128)}, u32[]{:S(2)}) copy-start(s32[2,3]{1,0:T(2,128)} %param.26) | copy-start | bytes 76
  48.7 9.3 %copy-start.72 = (bf16[128,256]{1,0:T(8,128)(2,1)S(1)}, bf16[128,256]{1,0:T(8,128)(2,1)}, u32[]{:S(2)}) copy-start(bf16[128,256]{1,0:T(8,128)(2,1)} %param.34) | copy-start | bytes 196612
  48.8 9.2 %copy-start.73 = (bf16[128,256]{1,0:T(8,128)(2,1)S(1)}, bf16[128,256]{1,0:T(8,128)(2,1)}, u32[]{:S(2)}) copy-start(bf16[128,256]{1,0:T(8,128)(2,1)} %param.33) | copy-start | bytes 196612
  48.8 9.2 %copy-start.74 = (bf16[128,256]{1,0:T(8,128)(2,1)S(1)}, bf16[128,256]{1,0:T(8,128)(2,1)}, u32[]{:S(2)}) copy-start(bf16[128,256]{1,0:T(8,128)(2,1)} %param.32) | copy-start | bytes 196612
  48.8 9.3 %copy-start.22 = (bf16[128,1024]{1,0:T(8,128)(2,1)S(1)}, bf16[128,1024]{1,0:T(8,128)(2,1)}, u32[]{:S(2)}) copy-start(bf16[128,1024]{1,0:T(8,128)(2,1)} %refs_3_.2) | copy-start | bytes 786436
  48.8 9.3 %copy-start.28 = (bf16[256,128]{1,0:T(8,128)(2,1)S(1)}, bf16[256,128]{1,0:T(8,128)(2,1)}, u32[]{:S(2)}) copy-start(bf16[256,128]{1,0:T(8,128)(2,1)} %refs_2_.1) | copy-start | bytes 196612
  58.0 46.1 %copy-start.96 = (f32[2,992]{1,0:T(2,128)S(1)}, f32[2,992]{1,0:T(2,128)}, u32[]{:S(2)}) copy-start(f32[2,992]{1,0:T(2,128)} %param.24) | copy-start | bytes 23812
  104.1 4.5 copy-start.30
  104.1 3.7 copy-start.7
  108.2 49.9 %copy-start.77 = (f32[1,8,128]{2,0,1:T(1,128)}, f32[1,8,128]{2,0,1:T(1,128)S(1)}, u32[]{:S(2)}) copy-start(f32[1,8,128]{2,0,1:T(1,128)S(1)} %get-tuple-element.176) | copy-start | bytes 12292
  108.2 49.9 %copy-start.94 = (f32[1,8,128]{2,0,1:T(1,128)}, f32[1,8,128]{2,0,1:T(1,128)S(1)}, u32[]{:S(2)}) copy-start(f32[1,8,128]{2,0,1:T(1,128)S(1)} %get-tuple-element.177) | copy-start | bytes 12292
  110.0 3.0 copy-start.61
  114.5 43.0 %copy-start.38 = (f32[496,1024]{1,0:T(8,128)S(1)}, f32[496,1024]{1,0:T(8,128)}, u32[]{:S(2)}) copy-start(f32[496,1024]{1,0:T(8,128)} %copy-done.37) | copy-start | bytes 6094852
  157.7 4.9 copy-start.34
  157.8 4.9 copy-start.83
  159.8 2.9 copy-start.87
  159.8 3.8 copy-start.99
  163.6 2.5 copy-start.65
  168.6 44.7 %copy-start.35 = (f32[496,1024]{1,0:T(8,128)S(1)}, f32[496,1024]{1,0:T(8,128)}, u32[]{:S(2)}) copy-start(f32[496,1024]{1,0:T(8,128)} %copy-done.34) | copy-start | bytes 6094852
  213.9 2.6 copy-start.50
  272.7 10.1 %copy-start.104 = (f32[496,3376]{1,0:T(8,128)}, f32[496,3376]{1,0:T(8,128)S(1)}, u32[]{:S(2)}) copy-start(f32[496,3376]{1,0:T(8,128)S(1)} %subtract_multiply_fusion) | copy-start | bytes 20093956
  272.7 10.1 %copy-start.3 = (f32[496,1024]{1,0:T(8,128)S(1)}, f32[496,1024]{1,0:T(8,128)}, u32[]{:S(2)}) copy-start(f32[496,1024]{1,0:T(8,128)} %copy-done.2) | copy-start | bytes 6094852
  288.9 41.8 %copy-start.69 = (f32[24,512]{1,0:T(8,128)S(1)}, f32[24,512]{1,0:T(8,128)}, u32[]{:S(2)}) copy-start(f32[24,512]{1,0:T(8,128)} %copy-done.68) | copy-start | bytes 147460
  288.9 41.8 %copy-start.71 = (f32[16,128]{1,0:T(8,128)S(1)}, f32[16,128]{1,0:T(8,128)}, u32[]{:S(2)}) copy-start(f32[16,128]{1,0:T(8,128)} %copy-done.70) | copy-start | bytes 24580
  330.7 5.5 copy-start.67
  334.0 5.4 slice-start
  336.3 3.1 slice-start.1
  343.8 42.7 %copy-start.100 = (bf16[1024,1024]{1,0:T(8,128)(2,1)S(1)}, bf16[1024,1024]{1,0:T(8,128)(2,1)}, u32[]{:S(2)}) copy-start(bf16[1024,1024]{1,0:T(8,128)(2,1)} %get-tuple-element.64) | copy-start | bytes 6291460
  343.8 42.7 %copy-start.103 = (f32[496,1024]{1,0:T(8,128)S(1)}, f32[496,1024]{1,0:T(8,128)}, u32[]{:S(2)}) copy-start(f32[496,1024]{1,0:T(8,128)} %get-tuple-element.193) | copy-start | bytes 6094852
  386.5 4.2 copy-start.10
  386.6 4.1 copy-start.98
  390.7 2.6 copy-start.60
  390.7 2.6 copy-start.102
  393.3 2.7 copy-start.36
  393.3 2.7 copy-start.78
  393.3 2.7 copy-start.84
  393.4 2.7 copy-start.88
  393.4 2.7 copy-start.95
  398.9 3.1 copy-start.53
  445.8 3.9 copy-start.8
  445.8 3.9 copy-start.16
  445.8 3.9 copy-start.18
  445.8 3.9 copy-start.42
  452.7 3.4 copy-start.33
  452.7 3.4 copy-start.62
  460.8 2.4 copy-start.39
  460.8 2.4 copy-start.76
  460.8 2.4 copy-start.86
  460.8 2.4 copy-start.90
  460.8 2.4 copy-start.93
  463.1 2.5 copy-start.41
  463.1 2.5 copy-start.64
  463.1 2.9 copy-start.49
  509.8 3.3 copy-start.12
  509.8 3.3 copy-start.14
  509.8 3.3 copy-start.26
  509.9 3.3 copy-start.43
  516.5 10.2 %copy-start.52 = (bf16[1024,768]{1,0:T(8,128)(2,1)S(1)}, bf16[1024,768]{1,0:T(8,128)(2,1)}, u32[]{:S(2)}) copy-start(bf16[1024,768]{1,0:T(8,128)(2,1)} %convolution_convert_fusion.5.refs_1_) | copy-start | bytes 4718596
  589.6 4.0 copy-start.21
  593.6 3.3 copy-start.15
  593.6 4.3 copy-start.13
  595.5 3.4 copy-start.25
  596.9 3.9 copy-start.9
  603.1 6.3 %copy-start.1 = (s32[2,3]{1,0:T(2,128)S(1)}, s32[2,3]{1,0:T(2,128)}, u32[]{:S(2)}) copy-start(s32[2,3]{1,0:T(2,128)} %param.26) | copy-start | bytes 76
  (44 other events, 62.5 us)

commit v2 on v1

v2 whole, which is shorter than its diff:
```python
import functools
import math

import jax
import jax.numpy as jnp
from jax import lax
from jax.experimental import pallas as pl
from jax.experimental.pallas import tpu as pltpu
from jax.sharding import PartitionSpec as P

HEAD = 64
LATENT = 512
RAMP = 1000
LOG_TWO_PI = 1.8378770664093453
NEG_LARGE = -1e30
FREE_BITS = 1.0
HOP_LAG = 3
WINDOW = 3
BLOCK_STEP = 4
TILE = 256
LINK_BYTES_PER_US = 92000.0
MOMENT_US = 1.3
SPREAD = 1
SPREAD_FROM = 0
SPREAD_STEP = 1
F32 = jnp.float32
BF16 = jnp.bfloat16


def mat_nn(left, right):
    return jnp.dot(left, right, preferred_element_type=F32)


def mat_tn(left, right):
    return lax.dot_general(left, right, (((0,), (0,)), ((), ())), preferred_element_type=F32)


def mat_nt(left, right):
    return lax.dot_general(left, right, (((1,), (1,)), ((), ())), preferred_element_type=F32)


def gelu(values):
    return 0.5 * values * (1.0 + lax.erf(values * 0.7071067811865476))


def gelu_slope(values):
    return (
        0.5 * (1.0 + lax.erf(values * 0.7071067811865476))
        + values * jnp.exp(-0.5 * values * values) * 0.3989422804014327
    )


def normalize(values):
    center = values - jnp.mean(values, axis=-1, keepdims=True)
    scale = lax.rsqrt(jnp.mean(center * center, axis=-1, keepdims=True) + 1e-05)
    return center * scale, scale


def norm_back(grad_in, normed, scale, gain):
    scaled = grad_in * gain
    return scale * (
        scaled
        - jnp.mean(scaled, axis=-1, keepdims=True)
        - normed * jnp.mean(scaled * normed, axis=-1, keepdims=True)
    )


def position_code(places, feature_count):
    quarter = feature_count // 4
    frequency = jnp.exp(jnp.arange(quarter, dtype=F32) * (-math.log(10000.0) / quarter))
    along_x = places[0][:, None] * frequency[None, :]
    along_y = places[1][:, None] * frequency[None, :]
    return jnp.concatenate(
        [jnp.sin(along_x), jnp.cos(along_x), jnp.sin(along_y), jnp.cos(along_y)], axis=1
    )


def slide_ids(length_row, cell_count):
    bounds = jnp.cumsum(length_row)[:-1]
    index = jnp.arange(cell_count, dtype=jnp.int32)
    return jnp.sum((index[:, None] >= bounds[None, :]).astype(jnp.int32), axis=1)


def allowed_pairs(slide, alive):
    index = jnp.arange(alive.shape[0], dtype=jnp.int32)
    return (slide[:, None] == slide[None, :]) & (
        (alive[None, :] == 1) | (index[:, None] == index[None, :])
    )


def heads_of(array):
    return array.reshape(array.shape[0], -1, HEAD)


def attend(queries, keys, values, allowed):
    factor = HEAD ** (-0.5)
    scores = (
        jnp.einsum("qhd,khd->hqk", heads_of(queries), heads_of(keys), preferred_element_type=F32)
        * factor
    )
    scores = jnp.where(allowed[None], scores, NEG_LARGE)
    largest = jnp.max(scores, axis=2, keepdims=True)
    exponents = jnp.exp(scores - largest)
    sums = jnp.sum(exponents, axis=2, keepdims=True)
    probs = (exponents / sums).astype(BF16)
    out = jnp.einsum("hqk,khd->qhd", probs, heads_of(values), preferred_element_type=F32)
    return out.reshape(queries.shape).astype(BF16), largest + jnp.log(sums)


def attend_back_kernel(middle, out_w, projected, log_totals, slide_keys, slide_queries, alive_keys, out):
    cells, width = out.shape[0], out.shape[1] // 3
    factor = HEAD ** (-0.5)
    shape = (cells, cells)
    own_key = lax.broadcasted_iota(jnp.int32, shape, 0) == lax.broadcasted_iota(jnp.int32, shape, 1)
    allowed = (slide_keys[...] == slide_queries[...]) & ((alive_keys[...] == 1) | own_key)
    grad_out = mat_nt(middle[...], out_w[...]).astype(BF16)
    for head in range(width // HEAD):
        first = head * HEAD
        q = projected[:, first : first + HEAD]
        k = projected[:, width + first : width + first + HEAD]
        v = projected[:, 2 * width + first : 2 * width + first + HEAD]
        g = grad_out[:, first : first + HEAD]
        scores = mat_nt(k, q) * factor - log_totals[head : head + 1, :]
        probs = jnp.where(allowed, jnp.exp(jnp.minimum(scores, 0.0)), 0.0)
        grad_probs = mat_nt(v, g)
        inner = jnp.sum(probs * grad_probs, axis=0, keepdims=True)
        grad_scores = (probs * (grad_probs - inner)).astype(BF16)
        out[:, first : first + HEAD] = (mat_tn(grad_scores, k) * factor).astype(BF16)
        out[:, width + first : width + first + HEAD] = (mat_nn(grad_scores, q) * factor).astype(BF16)
        out[:, 2 * width + first : 2 * width + first + HEAD] = mat_nn(
            probs.astype(BF16), g
        ).astype(BF16)


def attend_back(middle, out_w, projected, log_totals, slide, alive):
    return pl.pallas_call(
        attend_back_kernel,
        out_shape=jax.ShapeDtypeStruct(projected.shape, BF16),
        compiler_params=pltpu.CompilerParams(vmem_limit_bytes=48 * 2**20),
        name="attend_back",
    )(
        middle,
        out_w,
        projected,
        log_totals[:, :, 0],
        slide[:, None],
        slide[None, :],
        alive[:, None],
    )


def part_of(ref, axis, index, size):
    span = pl.ds(index * size, size)
    if axis == 0:
        return ref.at[span, :]
    return ref.at[:, pl.ds(pl.multiple_of(index * size, 128), size)]


def line_sum(produce, hooks, part, out, from_left, from_right, to_right, to_left, got_left, got_right, sent_right, sent_left):
    me, count = lax.axis_index("mp"), lax.axis_size("mp")
    pieces, height, width = from_left.shape
    splits = pieces * width // part.shape[1]
    stride = (part.shape[0] - height) // (splits - 1)
    has_right, has_left = me < count - 1, me > 0

    def place(piece):
        return (
            pl.ds(pl.multiple_of(lax.rem(piece, splits) * stride, 16), height),
            pl.ds(pl.multiple_of(lax.div(piece, splits) * width, width), width),
        )

    def rightward(piece):
        return pltpu.make_async_remote_copy(
            src_ref=to_right.at[piece],
            dst_ref=from_left.at[piece],
            send_sem=sent_right.at[piece],
            recv_sem=got_left.at[piece],
            device_id={"mp": me + 1},
        )

    def leftward(piece):
        return pltpu.make_async_remote_copy(
            src_ref=to_left.at[piece],
            dst_ref=from_right.at[piece],
            send_sem=sent_left.at[piece],
            recv_sem=got_right.at[piece],
            device_id={"mp": me - 1},
        )

    def flow(piece, copy, has_source, has_target, source, target):
        @pl.when((piece >= 0) & (piece < pieces))
        def _():
            @pl.when(has_source)
            def _():
                copy(piece).wait_recv()

            @pl.when(has_target & has_source)
            def _():
                target[piece] = (part[place(piece)] + source[piece].astype(F32)).astype(BF16)

            @pl.when(has_target & jnp.logical_not(has_source))
            def _():
                target[piece] = part[place(piece)].astype(BF16)

            @pl.when(has_target & (piece >= WINDOW))
            def _():
                copy(piece - WINDOW).wait_send()

            @pl.when(has_target)
            def _():
                copy(piece).start()

    moments = pieces + HOP_LAG * (count - 1)
    right_half = lax.div(2 * me + 1, count)
    trail = HOP_LAG * (right_half * me + (1 - right_half) * (count - 1 - me))

    def step(moment, carry):
        produce(moment)
        flow(moment - HOP_LAG * me, rightward, has_left, has_right, from_left, to_right)
        flow(
            moment - HOP_LAG * (count - 1 - me), leftward, has_right, has_left, from_right, to_left
        )
        done = moment - trail
        finished = (done >= 0) & (done < pieces)

        @pl.when(finished & has_left & has_right)
        def _():
            out[place(done)] = (
                part[place(done)] + from_left[done].astype(F32) + from_right[done].astype(F32)
            )

        @pl.when(finished & jnp.logical_not(has_left))
        def _():
            out[place(done)] = part[place(done)] + from_right[done].astype(F32)

        @pl.when(finished & jnp.logical_not(has_right))
        def _():
            out[place(done)] = part[place(done)] + from_left[done].astype(F32)

        return carry

    def finish():
        def step(piece, carry):
            @pl.when(has_right)
            def _():
                rightward(piece).wait_send()

            @pl.when(has_left)
            def _():
                leftward(piece).wait_send()

            return carry

        lax.fori_loop(pieces - WINDOW, pieces, step, 0)

    reached = 0
    for when, hook in hooks:
        if when > reached:
            lax.fori_loop(reached, when, step, 0)
            reached = when
        hook()
    lax.fori_loop(reached, moments, step, 0)
    finish()


PRODUCT_SCRATCH = 5


def start_product(form, left, right, part, left_in, right_in, left_sem, right_sem):
    transposed, sliced = form
    blocks = right_in.shape[0]
    width = part.shape[1] // blocks
    if sliced:
        rows = left_in.shape[0]
        first = pl.multiple_of(lax.axis_index("section") * rows, 16)
        left_copy = pltpu.make_async_copy(left.at[pl.ds(first, rows), :], left_in, left_sem)
        left_copy.start()

    def right_copy(block):
        span = pl.ds(pl.multiple_of(block * width, width), width)
        view = right.at[span, :] if transposed else right.at[:, span]
        return pltpu.make_async_copy(view, right_in.at[block], right_sem.at[block])

    for block in range(blocks):
        right_copy(block).start()
    if sliced:
        left_copy.wait()

    def produce(moment):
        @pl.when((lax.rem(moment, BLOCK_STEP) == 0) & (moment < blocks * BLOCK_STEP))
        def _():
            block = lax.div(moment, BLOCK_STEP)
            right_copy(block).wait()
            contract = (((1,), (1 if transposed else 0,)), ((), ()))
            part[:, pl.ds(pl.multiple_of(block * width, width), width)] = lax.dot_general(
                (left_in if sliced else left)[...],
                right_in[block],
                contract,
                preferred_element_type=F32,
            )

    return produce


def halfway(rows):
    return rows // 32 * 16


def block_of(ref, axis, index, size, start=0, stop=None):
    if axis == 0:
        stop = size if stop is None else stop
        return ref.at[pl.ds(pl.multiple_of(index * size + start, 16), stop - start), :]
    stop = ref.shape[0] if stop is None else stop
    return ref.at[pl.ds(start, stop - start), pl.ds(pl.multiple_of(index * size, 128), size)]


def reaction_moments(travelling):
    third = travelling / LINK_BYTES_PER_US
    last = 2 * len(range(8)) + 3 * HOP_LAG - 1
    return [
        min(last, math.ceil((parts * third + 2.0 + 0.5 * parts) / MOMENT_US)) for parts in (1, 2)
    ]


def comm_kernel(plan, *refs):
    refs = list(refs)

    def take(number):
        taken = refs[:number]
        del refs[:number]
        return taken

    reduces, gathers, swaps, exchanges, shares, pairs, travelling = plan
    groups = (len(gathers), len(swaps), len(exchanges), shares, pairs)
    sources = [take(n) for n in (2 if reduces else 0,) + groups]
    others = [take(1)[0] if paired else None for _, _, paired in exchanges]
    results = [take(n) for n in (1 if reduces else 0,) + groups]
    product = take(PRODUCT_SCRATCH) if reduces else None
    line = take(8) if reduces else None
    staging = [take(4 + paired) for _, _, paired in exchanges]
    sent, got, local_sem = refs

    section, z, dp = (lax.axis_index(name) for name in ("section", "mp", "dp"))
    count_z, count_dp = lax.axis_size("mp"), lax.axis_size("dp")
    row, col = dp // 2, dp % 2
    peer_x, peer_y = row * 2 + (1 - col), (1 - row) * 2 + col
    peer_d = (1 - row) * 2 + (1 - col)
    partner, to_x, to_y = {"section": 1 - section}, {"dp": peer_x}, {"dp": peer_y}

    barrier = pltpu.get_barrier_semaphore()
    fixed = 0
    if gathers or swaps or pairs:
        pl.semaphore_signal(barrier, inc=1, device_id=partner)
        fixed += 1
    if gathers or exchanges:
        pl.semaphore_signal(barrier, inc=1, device_id=to_x)
        pl.semaphore_signal(barrier, inc=1, device_id=to_y)
        fixed += 2
    if shares:
        for step in range(1, count_z):
            pl.semaphore_signal(barrier, inc=1, device_id={"mp": (z + step) % count_z})
        fixed += count_z - 1
    elif reduces:
        for exists, neighbour in ((z > 0, z - 1), (z < count_z - 1, z + 1)):

            @pl.when(exists)
            def _(neighbour=neighbour):
                pl.semaphore_signal(barrier, inc=1, device_id={"mp": neighbour})

        at_end = (z == 0) | (z == count_z - 1)

        @pl.when(at_end)
        def _():
            pl.semaphore_wait(barrier, fixed + 1)

        @pl.when(jnp.logical_not(at_end))
        def _():
            pl.semaphore_wait(barrier, fixed + 2)

    if fixed and (shares or not reduces):
        pl.semaphore_wait(barrier, fixed)

    used = [0, 0]

    def remote(src, dst, device):
        index = used[0]
        used[0] += 1
        return pltpu.make_async_remote_copy(
            src_ref=src, dst_ref=dst, send_sem=sent.at[index], recv_sem=got.at[index], device_id=device
        )

    def within(src, dst):
        index = used[1]
        used[1] += 1
        return pltpu.make_async_copy(src, dst, local_sem.at[index])

    locals_, early, first, second = [], [], [], []
    after_one, after_two, after_three = [], [], []
    receives, loads = [], []
    starts_d, starts_xy, conclusions = [], [], []
    for item, (axis, size) in enumerate(swaps):
        src, dst = sources[2][item], results[2][item]
        copy = remote(part_of(src, axis, 1 - section, size), dst, partner)
        early.append(copy)
        receives.append(copy)
    for item in range(pairs):
        copy = remote(sources[5][item], results[5][item], partner)
        early.append(copy)
        receives.append(copy)
    for item in range(shares):
        src, dst = sources[4][item], results[4][item]
        locals_.append(within(src, dst.at[z]))
        for step in range(1, count_z):
            copy = remote(src, dst.at[z], {"mp": (z + step) % count_z})
            early.append(copy)
            receives.append(copy)
    for item, (axis, size) in enumerate(gathers):
        src, dst = sources[1][item], results[1][item]
        rows = src.shape[0]
        cut = halfway(rows)

        def shard_of(index, start=0, stop=rows, dst=dst, axis=axis, size=size):
            return block_of(dst, axis, section * count_dp + index, size, start, stop)

        upper, lower = src.at[pl.ds(0, cut), :], src.at[pl.ds(cut, rows - cut), :]
        locals_.append(within(src, shard_of(dp)))
        own = remote(src, shard_of(dp), partner)
        x_upper = remote(upper, shard_of(dp, 0, cut), to_x)
        y_lower = remote(lower, shard_of(dp, cut), to_y)
        x_lower = remote(lower, shard_of(dp, cut), to_x)
        y_upper = remote(upper, shard_of(dp, 0, cut), to_y)
        pass_y = remote(shard_of(peer_x, 0, cut), shard_of(peer_x, 0, cut), to_y)
        pass_x = remote(shard_of(peer_y, cut), shard_of(peer_y, cut), to_x)
        relay_x = remote(shard_of(peer_x), shard_of(peer_x), partner)
        relay_y = remote(shard_of(peer_y), shard_of(peer_y), partner)
        relay_upper = remote(shard_of(peer_d, 0, cut), shard_of(peer_d, 0, cut), partner)
        relay_lower = remote(shard_of(peer_d, cut), shard_of(peer_d, cut), partner)
        early.append(own)
        first += [x_upper, y_lower]
        second += [x_lower, y_upper]
        after_one += [([x_upper], None, pass_y), ([y_lower], None, pass_x)]
        after_two += [([x_lower], None, relay_x), ([y_upper], None, relay_y)]
        after_three += [([pass_y], None, relay_upper), ([pass_x], None, relay_lower)]
        receives += [own, relay_x, relay_y, relay_upper, relay_lower]
    for item, (axis, size, paired) in enumerate(exchanges):
        src, dst = sources[3][item], results[3][item]
        mine, from_x, from_y, inbound = staging[item][:4]
        rows, dtype = from_x.shape[0], from_x.dtype
        cut = halfway(rows)
        rest = rows - cut
        half = section * count_dp if paired else 0
        fetched = []
        for role, index in enumerate((peer_d, peer_x, peer_y, dp)):
            copies = [within(block_of(src, axis, half + index, size), mine.at[role])]
            if paired:
                copies.append(
                    within(block_of(others[item], axis, index, size), staging[item][4].at[role])
                )
            fetched.append(copies)
            loads += copies

        def merge(role, mine=mine, other=staging[item][-1] if paired else None):
            def run():
                if other is not None:
                    mine[role] = (mine[role].astype(F32) + other[role].astype(F32)).astype(mine.dtype)

            return run

        top, bottom = pl.ds(0, cut), pl.ds(cut, rest)
        d_upper = remote(mine.at[0, top, :], inbound.at[top, :], to_x)
        d_lower = remote(mine.at[0, bottom, :], inbound.at[bottom, :], to_y)
        x_upper = remote(mine.at[1, top, :], from_x.at[top, :], to_x)
        y_lower = remote(mine.at[2, bottom, :], from_y.at[bottom, :], to_y)
        y_upper = remote(mine.at[2, top, :], from_y.at[top, :], to_y)
        x_lower = remote(mine.at[1, bottom, :], from_x.at[bottom, :], to_x)

        def add(role, span, mine=mine, term=inbound):
            def run():
                mine[role, span, :] = (
                    mine[role, span, :].astype(F32) + term[span, :].astype(F32)
                ).astype(mine.dtype)

            return run

        def conclude(mine=mine, from_x=from_x, from_y=from_y, dst=dst):
            dst[...] = mine[3].astype(F32) + from_x[...].astype(F32) + from_y[...].astype(F32)

        starts_d += [(fetched[0], merge(0), [d_upper, d_lower])]
        starts_xy += [
            (fetched[1], merge(1), [x_upper]),
            (fetched[2], merge(2), [y_lower]),
            (fetched[3], merge(3), []),
        ]
        after_one += [
            ([d_upper], add(2, top), y_upper),
            ([d_lower], add(1, bottom), x_lower),
        ]
        receives += [x_upper, y_lower, y_upper, x_lower]
        conclusions.append(conclude)

    remotes = early + first + second

    def begin():
        for copy in loads + remotes + locals_:
            copy.start()

    def send_parts():
        for copies, compute, targets in starts_d + starts_xy:
            for copy in copies:
                copy.wait()
            compute()
            for copy in targets:
                copy.start()

    def react(items):
        def run():
            for waits, compute, copy in items:
                for wait in waits:
                    wait.wait_recv()
                if compute is not None:
                    compute()
                copy.start()

        return run

    if reduces:
        produce = start_product(reduces, *sources[0], *product)
        moments = reaction_moments(travelling)
        hooks = [(0, begin), (2, send_parts), (moments[0], react(after_one)), (moments[1], react(after_two))]
        line_sum(produce, hooks, product[0], results[0][0], *line)
    else:
        begin()
        send_parts()
        react(after_one)()
        react(after_two)()
    react(after_three)()
    for copy in receives:
        copy.wait_recv()
    for conclude in conclusions:
        conclude()
    started = remotes + [copy for _, _, copies in starts_d + starts_xy for copy in copies]
    started += [copy for _, _, copy in after_one + after_two + after_three]
    for copy in started:
        copy.wait_send()
    for copy in locals_:
        copy.wait()


def comm(number, reduce=None, gathers=(), swaps=(), exchanges=(), shares=(), pairs=(), name="meet"):
    count_dp, count_z = lax.axis_size("dp"), lax.axis_size("mp")
    sections = lax.axis_size("section")

    def resized(shape, axis, size):
        return shape[:axis] + (size,) + shape[axis + 1 :]

    inputs, outputs, scratch = [], [], []
    plan_gathers, plan_swaps, plan_exchanges = [], [], []
    remote_count = local_count = travelling = 0
    reduces = None
    if reduce is not None:
        left, right, transposed, sliced = reduce
        reduces = (transposed, sliced)
        rows, depth = left.shape[0] // (sections if sliced else 1), left.shape[1]
        width = right.shape[0 if transposed else 1]
        blocks = width // 256
        inputs += [left, right]
        outputs.append(jax.ShapeDtypeStruct((rows, width), F32))
        scratch += [
            pltpu.VMEM((rows, width), F32),
            pltpu.VMEM((rows, depth) if sliced else (16, 128), BF16),
            pltpu.VMEM((blocks, 256, depth) if transposed else (blocks, depth, 256), BF16),
            pltpu.SemaphoreType.DMA,
            pltpu.SemaphoreType.DMA((blocks,)),
        ]
        buffer = pltpu.VMEM((width // 64, 256, 128), BF16)
        scratch += [buffer] * 4 + [pltpu.SemaphoreType.DMA((width // 64,))] * 4
    for shard, axis in gathers:
        size = shard.shape[axis]
        inputs.append(shard)
        outputs.append(
            jax.ShapeDtypeStruct(resized(shard.shape, axis, size * sections * count_dp), shard.dtype)
        )
        plan_gathers.append((axis, size))
        travelling += shard.size * shard.dtype.itemsize
        remote_count += 11
        local_count += 1
    for array, axis in swaps:
        size = array.shape[axis] // sections
        inputs.append(array)
        outputs.append(jax.ShapeDtypeStruct(resized(array.shape, axis, size), array.dtype))
        plan_swaps.append((axis, size))
        remote_count += 1
    other_inputs = []
    for array, other, axis in exchanges:
        paired = other is not None
        size = array.shape[axis] // (count_dp * (sections if paired else 1))
        piece = resized(array.shape, axis, size)
        inputs.append(array)
        outputs.append(jax.ShapeDtypeStruct(piece, F32))
        plan_exchanges.append((axis, size, paired))
        roles, one = pltpu.VMEM((4,) + piece, array.dtype), pltpu.VMEM(piece, array.dtype)
        scratch += [roles, one, one, one]
        if paired:
            other_inputs.append(other)
            scratch.append(roles)
        travelling += piece[0] * piece[1] * array.dtype.itemsize
        remote_count += 6
        local_count += 8
    for array in shares:
        inputs.append(array)
        outputs.append(jax.ShapeDtypeStruct((count_z,) + array.shape, array.dtype))
        remote_count += count_z - 1
        local_count += 1
    for array in pairs:
        inputs.append(array)
        outputs.append(jax.ShapeDtypeStruct(array.shape, array.dtype))
        remote_count += 1
    inputs += other_inputs
    scratch += [
        pltpu.SemaphoreType.DMA((max(remote_count, 1),)),
        pltpu.SemaphoreType.DMA((max(remote_count, 1),)),
        pltpu.SemaphoreType.DMA((max(local_count, 1),)),
    ]
    plan = (reduces, tuple(plan_gathers), tuple(plan_swaps), tuple(plan_exchanges), len(shares), len(pairs), travelling)
    placed = [True] * (reduces is not None) + [False] * (len(gathers) + len(swaps))
    placed += [True] * len(exchanges) + [False] * (len(shares) + len(pairs))
    vmem, anywhere = pl.BlockSpec(memory_space=pltpu.VMEM), pl.BlockSpec(memory_space=pl.ANY)
    outs = pl.pallas_call(
        functools.partial(comm_kernel, plan),
        out_shape=outputs,
        in_specs=([] if reduces is None else [anywhere if reduces[1] else vmem])
        + [anywhere] * (len(inputs) - (0 if reduces is None else 1)),
        out_specs=[vmem if in_vmem else anywhere for in_vmem in placed],
        scratch_shapes=scratch,
        compiler_params=pltpu.CompilerParams(
            collective_id=number, has_side_effects=True, vmem_limit_bytes=48 * 2**20
        ),
        cost_estimate=pl.CostEstimate(flops=1000000, bytes_accessed=90000000, transcendentals=0),
        name=name,
    )(*inputs)
    outs = list(outs)
    split = []
    for number_of in (1 if reduces else 0, len(gathers), len(swaps), len(exchanges), len(shares), len(pairs)):
        split.append(outs[:number_of])
        outs = outs[number_of:]
    return split


def trade(remote, mine, indices, from_x, from_y, inbound, to_x, to_y):
    rows = from_x.shape[0]
    cut = halfway(rows)
    top, bottom = pl.ds(0, cut), pl.ds(cut, rows - cut)
    d, x, y, own = indices
    d_upper = remote(mine.at[d, top, :], inbound.at[top, :], to_x)
    d_lower = remote(mine.at[d, bottom, :], inbound.at[bottom, :], to_y)
    x_upper = remote(mine.at[x, top, :], from_x.at[top, :], to_x)
    y_lower = remote(mine.at[y, bottom, :], from_y.at[bottom, :], to_y)
    y_upper = remote(mine.at[y, top, :], from_y.at[top, :], to_y)
    x_lower = remote(mine.at[x, bottom, :], from_x.at[bottom, :], to_x)

    def pass_on():
        for copy, index, span, onward in (
            (d_upper, y, top, y_upper),
            (d_lower, x, bottom, x_lower),
        ):
            copy.wait_recv()
            mine[index, span, :] = (
                mine[index, span, :].astype(F32) + inbound[span, :].astype(F32)
            ).astype(mine.dtype)
            onward.start()

    def conclude():
        for copy in (x_upper, y_lower, y_upper, x_lower):
            copy.wait_recv()
        for copy in (d_upper, d_lower, x_upper, y_lower, y_upper, x_lower):
            copy.wait_send()
        return mine[own].astype(F32) + from_x[...].astype(F32) + from_y[...].astype(F32)

    return (d_upper, d_lower), (x_upper, y_lower), pass_on, conclude


def tail_kernel(
    start, expression, embed, grad_rebuilt, qkv, out, small, qkv_other, out_other,
    embed_sum, qkv_sum, out_sum, small_sum, cells_own, cells_other,
    start_other, start_turned, x_own, x_other, embed_in, cells, embed_parts, embed_x, embed_y, embed_in_d,
    qkv_parts, qkv_x, qkv_y, qkv_in_d, qkv_partner, out_parts, out_x, out_y, out_in_d, out_partner,
    small_parts, small_x, small_y, small_in_d, small_partner, sent, got, local_sem,
):
    section, dp = lax.axis_index("section"), lax.axis_index("dp")
    count_dp = lax.axis_size("dp")
    row, col = dp // 2, dp % 2
    peer_x, peer_y = row * 2 + (1 - col), (1 - row) * 2 + col
    peer_d = (1 - row) * 2 + (1 - col)
    partner, to_x, to_y = {"section": 1 - section}, {"dp": peer_x}, {"dp": peer_y}
    rows, genes = cells.shape
    half = start_other.shape[1]
    width = half // count_dp

    barrier = pltpu.get_barrier_semaphore()
    for device in (partner, to_x, to_y):
        pl.semaphore_signal(barrier, inc=1, device_id=device)
    pl.semaphore_wait(barrier, 3)

    used = [0, 0]

    def remote(src, dst, device):
        index = used[0]
        used[0] += 1
        return pltpu.make_async_remote_copy(
            src_ref=src, dst_ref=dst, send_sem=sent.at[index], recv_sem=got.at[index], device_id=device
        )

    def within(src, dst):
        index = used[1]
        used[1] += 1
        return pltpu.make_async_copy(src, dst, local_sem.at[index])

    def half_of(index):
        return pl.ds(pl.multiple_of(index * half, 128), half)

    def rows_of(index):
        return pl.ds(pl.multiple_of(index * rows, 16), rows)

    swaps = [
        remote(start.at[:, half_of(1 - section)], start_other, partner),
        remote(small.at[1 - section], small_partner, partner),
    ]
    for copy in swaps:
        copy.start()
    roles = (peer_d, peer_x, peer_y, dp)
    fetches = []
    for src, other, axis, parts, parts_other in (
        (qkv, qkv_other, 0, qkv_parts, qkv_partner),
        (out, out_other, 1, out_parts, out_partner),
    ):
        size = src.shape[axis] // (2 * count_dp)
        for role, index in enumerate(roles):
            fetches.append(
                within(block_of(src, axis, section * count_dp + index, size), parts.at[role])
            )
            fetches.append(within(block_of(other, axis, index, size), parts_other.at[role]))
    fetches.append(within(small.at[section], small_parts))
    load_own = within(expression.at[rows_of(section), :], x_own)
    load_other = within(expression.at[rows_of(1 - section), :], x_other)
    load_embed = within(embed, embed_in)
    load_cells = within(grad_rebuilt, cells)
    for copy in fetches + [load_own, load_other, load_embed, load_cells]:
        copy.start()

    trades = [
        trade(remote, parts, indices, *buffers, to_x, to_y)
        for parts, indices, buffers in (
            (qkv_parts, (0, 1, 2, 3), (qkv_x, qkv_y, qkv_in_d)),
            (out_parts, (0, 1, 2, 3), (out_x, out_y, out_in_d)),
            (small_parts, roles, (small_x, small_y, small_in_d)),
            (embed_parts, roles, (embed_x, embed_y, embed_in_d)),
        )
    ]

    for copy in fetches:
        copy.wait()
    swaps[1].wait_recv()
    for parts, other in (
        (qkv_parts, qkv_partner),
        (out_parts, out_partner),
        (small_parts, small_partner),
    ):
        parts[...] = (parts[...].astype(F32) + other[...].astype(F32)).astype(parts.dtype)
    for first, second, _, _ in trades[:3]:
        for copy in first + second:
            copy.start()

    load_own.wait()
    load_other.wait()
    swaps[0].wait_recv()
    start_turned[0] = start[:, half_of(section)].T
    start_turned[1] = start_other[...].T

    def embed_tile(span, size):
        tile = mat_nn(start_turned[0], x_own[:, span]) + mat_nn(start_turned[1], x_other[:, span])
        embed_parts[:, :, span] = tile.reshape(count_dp, width, size).astype(BF16)

    whole = genes // TILE

    def embed_step(index, carry):
        embed_tile(pl.ds(pl.multiple_of(index * TILE, TILE), TILE), TILE)
        return carry

    lax.fori_loop(0, whole, embed_step, 0)
    if genes % TILE:
        embed_tile(pl.ds(whole * TILE, genes % TILE), genes % TILE)
    for copy in trades[3][0] + trades[3][1]:
        copy.start()

    load_embed.wait()
    load_cells.wait()

    def cells_tile(span):
        tile = mat_nt(start[...], embed_in[span, :]).astype(BF16)
        cells[:, span] = (tile.astype(F32) - cells[:, span].astype(F32)).astype(BF16)

    def cells_step(index, carry):
        cells_tile(pl.ds(pl.multiple_of(index * TILE, TILE), TILE))
        return carry

    lax.fori_loop(0, whole, cells_step, 0)
    if genes % TILE:
        cells_tile(pl.ds(whole * TILE, genes % TILE))
    give = remote(cells, cells_other, partner)
    give.start()
    keep = within(cells, cells_own)
    keep.start()

    for _, _, pass_on, _ in trades:
        pass_on()
    qkv_sum[...] = trades[0][3]()
    out_sum[...] = trades[1][3]()
    small_sum[...] = trades[2][3]()
    embed_sum[...] = trades[3][3]().T
    for copy in swaps:
        copy.wait_send()
    give.wait()
    keep.wait()


def assemble_kernel(own, other, whole, held, arrived, left):
    section = lax.axis_index("section")
    rows = own.shape[0]
    spans = [(start, min(128, rows - start)) for start in range(0, rows, 128)]
    loads, stores = [], []
    for place, (src, index) in enumerate(((own, section), (other, 1 - section))):
        for part, (start, size) in enumerate(spans):
            span = pl.ds(start, size)
            target = pl.ds(pl.multiple_of(index * rows + start, 16), size)
            number = place * len(spans) + part
            loads.append(
                pltpu.make_async_copy(src.at[span, :], held.at[place, span, :], arrived.at[number])
            )
            stores.append(
                pltpu.make_async_copy(held.at[place, span, :], whole.at[target, :], left.at[number])
            )
    for load in loads:
        load.start()
    for load, store in zip(loads, stores):
        load.wait()
        store.start()
    for store in stores:
        store.wait()


def tail(number, start, expression, embed, grad_rebuilt, qkv, qkv_other, out, out_other, small):
    rows, features = start.shape
    genes, count_dp = embed.shape[0], lax.axis_size("dp")
    half = features // 2
    width = half // count_dp
    vmem, anywhere = pl.BlockSpec(memory_space=pltpu.VMEM), pl.BlockSpec(memory_space=pl.ANY)

    def buffers(shape, dtype, paired):
        parts, one = pltpu.VMEM((count_dp,) + shape, dtype), pltpu.VMEM(shape, dtype)
        return [parts, one, one, one] + ([parts] if paired else [])

    qkv_piece = (qkv.shape[0] // (2 * count_dp), qkv.shape[1])
    out_piece = (out.shape[0], out.shape[1] // (2 * count_dp))
    small_piece = small.shape[2:]
    cells = jax.ShapeDtypeStruct((rows, genes), BF16)
    results = pl.pallas_call(
        tail_kernel,
        out_shape=[
            jax.ShapeDtypeStruct((genes, width), F32),
            jax.ShapeDtypeStruct(qkv_piece, F32),
            jax.ShapeDtypeStruct(out_piece, F32),
            jax.ShapeDtypeStruct(small_piece, F32),
            cells,
            cells,
        ],
        in_specs=[vmem] + [anywhere] * 8,
        out_specs=[vmem] * 4 + [anywhere] * 2,
        scratch_shapes=[
            pltpu.VMEM((rows, half), BF16),
            pltpu.VMEM((2, half, rows), BF16),
            pltpu.VMEM((rows, genes), BF16),
            pltpu.VMEM((rows, genes), BF16),
            pltpu.VMEM((genes, features), BF16),
            pltpu.VMEM((rows, genes), BF16),
        ]
        + buffers((width, genes), BF16, False)
        + buffers(qkv_piece, BF16, True)
        + buffers(out_piece, BF16, True)
        + buffers(small_piece, F32, True)
        + [
            pltpu.SemaphoreType.DMA((27,)),
            pltpu.SemaphoreType.DMA((27,)),
            pltpu.SemaphoreType.DMA((22,)),
        ],
        compiler_params=pltpu.CompilerParams(
            collective_id=number, has_side_effects=True, vmem_limit_bytes=56 * 2**20
        ),
        name="tail",
    )(start, expression, embed, grad_rebuilt, qkv, out, small, qkv_other, out_other)
    whole = pl.pallas_call(
        assemble_kernel,
        out_shape=jax.ShapeDtypeStruct((2 * rows, genes), BF16),
        in_specs=[anywhere] * 2,
        out_specs=anywhere,
        scratch_shapes=[pltpu.VMEM((2, rows, genes), BF16)]
        + [pltpu.SemaphoreType.DMA((2 * (-(-rows // 128)),))] * 2,
        compiler_params=pltpu.CompilerParams(vmem_limit_bytes=56 * 2**20),
        name="assemble",
    )(results[4], results[5])
    return list(results[:4]) + [whole]


def meet(tiled, number, reduce=None, gathers=(), swaps=(), exchanges=(), shares=(), pairs=()):
    if tiled:
        return comm(number, reduce, gathers, swaps, exchanges, shares, pairs)
    partner = [(i, 1 - i) for i in range(2)]
    section, count_dp = lax.axis_index("section"), lax.axis_size("dp")
    swapped = []
    for array, axis in swaps:
        size = array.shape[axis] // 2
        half = lax.dynamic_slice_in_dim(array, (1 - section) * size, size, axis)
        swapped.append(lax.ppermute(half, "section", partner))
    exchanged = []
    for array, other, axis in exchanges:
        if other is not None:
            array = half_sum(array, other, axis)
        parts = lax.all_to_all(jnp.stack(jnp.split(array, count_dp, axis)), "dp", 0, 0)
        exchanged.append(total(parts))
    return [
        [] if reduce is None else comm(number, reduce)[0][0:1],
        [lax.all_gather(shard, ("section", "dp"), axis=axis, tiled=True) for shard, axis in gathers],
        swapped,
        exchanged,
        [lax.all_gather(array, "mp") for array in shares],
        [lax.ppermute(array, "section", partner) for array in pairs],
    ]


def half_sum(array, received, axis):
    size = received.shape[axis]
    own = lax.dynamic_slice_in_dim(array, lax.axis_index("section") * size, size, axis)
    return (own.astype(F32) + received.astype(F32)).astype(array.dtype)


def total(parts):
    return jnp.sum(parts.astype(F32), axis=0)


def local(
    expression,
    cell_xy,
    live_mask,
    lengths,
    ramp_step,
    latent_noise,
    gene_embed,
    ln1_gain,
    ln1_bias,
    w_query,
    w_key,
    w_value,
    w_out,
    ln2_gain,
    ln2_bias,
    w_up,
    w_down,
    w_mean,
    w_logvar,
    comp_mean,
    comp_logvar,
    w_dec,
    w_genes,
):
    micro_count = lengths.shape[0]
    cells = expression.shape[0] // micro_count
    micro = lax.axis_index("section")
    latent_cols = w_mean.shape[1]
    comp_count, comp_width = comp_mean.shape
    width = ln1_gain.shape[0]
    shards = 2 * lax.axis_size("dp")
    features = shards * width
    tiled = width % 128 == 0 and lax.axis_size("dp") == 4
    meeting = functools.partial(meet, tiled)

    def own(array, axis=0):
        return lax.dynamic_slice_in_dim(array, micro * cells, cells, axis)

    genes_in = own(expression)
    alive = own(live_mask)
    alive_float = alive.astype(F32)
    noise = own(latent_noise)
    slide = slide_ids(lax.dynamic_index_in_dim(lengths, micro, 0, False), cells)
    allowed = allowed_pairs(slide, alive)
    positions = position_code(own(cell_xy, 1), features)

    norm_block = jnp.pad(jnp.stack([ln1_gain, ln1_bias, ln2_gain, ln2_bias]), ((0, 12), (0, 0)))
    comp_block = jnp.pad(
        jnp.concatenate([comp_mean, comp_logvar], axis=0), ((0, 0), (0, width - comp_width))
    )
    small = jnp.concatenate([norm_block, comp_block], axis=0)
    small_rows = small.shape[0]
    _, (embed, small_all), _, _, _, _ = meeting(0, gathers=((gene_embed, 1), (small, 0)))
    small_all = small_all.reshape(shards, small_rows, width).astype(F32)
    norm_params = small_all[:, :4].transpose(1, 0, 2).reshape(4, features)
    gain_one, bias_one, gain_two, bias_two = (norm_params[i : i + 1] for i in range(4))
    comps = small_all[:, 16:, :comp_width].transpose(1, 0, 2).reshape(2 * comp_count, -1)
    centers, spreads = comps[:comp_count], comps[comp_count:]

    qkv_shard = jnp.concatenate([w_query, w_key, w_value], axis=1)
    (summed,), (qkv, out_w, up_w), _, _, _, _ = meeting(
        1, (expression, embed, False, True), gathers=((qkv_shard, 0), (w_out, 1), (w_up, 0))
    )
    start = summed + positions
    normed_one, scale_one = normalize(start)
    first_low = (normed_one * gain_one + bias_one).astype(BF16)
    projected = mat_nn(first_low, qkv).astype(BF16)
    queries, keys, values = jnp.split(projected, 3, axis=1)
    attended, log_totals = attend(queries, keys, values, allowed)
    latent_shard = jnp.concatenate([w_mean, w_logvar], axis=1)
    (summed,), (down_w, latent_w, dec_w), _, _, _, _ = meeting(
        2, (attended, out_w, False, False), gathers=((w_down, 1), (latent_shard, 0), (w_dec, 1))
    )
    after_attn = start + summed
    normed_two, scale_two = normalize(after_attn)
    second_low = (normed_two * gain_two + bias_two).astype(BF16)
    upper = mat_nn(second_low, up_w)
    activated = gelu(upper).astype(BF16)
    (summed,), (genes_w,), _, _, _, _ = meeting(
        3, (activated, down_w, False, False), gathers=((w_genes, 0),)
    )
    hidden = (after_attn + summed).astype(BF16)

    stats = mat_nn(hidden, latent_w)
    means, log_vars = stats[:, :latent_cols], stats[:, latent_cols:]
    spread = jnp.exp(0.5 * log_vars) * noise
    latent = means + spread
    latent_low = latent.astype(BF16)
    post_part = jnp.sum(-0.5 * LOG_TWO_PI - 0.5 * log_vars - 0.5 * noise * noise, axis=1)
    precision = jnp.exp(-spreads)
    offsets = latent[None] - centers[:, None, :]
    pulled = offsets * precision[:, None, :]
    comp_part = jnp.sum(
        -0.5 * LOG_TWO_PI - 0.5 * spreads[:, None, :] - 0.5 * offsets * pulled, axis=2
    )
    density_part = jnp.pad(
        jnp.concatenate([comp_part, post_part[None]], axis=0), ((0, 7), (0, -cells % 128))
    )
    (decoder_pre,), _, _, _, (density_parts,), _ = meeting(
        4, (latent_low, dec_w, False, False), shares=(density_part,)
    )
    densities = jnp.sum(density_parts, axis=0)[:, :cells]
    logits = densities[:comp_count] - math.log(comp_count)
    log_post = densities[comp_count]
    largest = jnp.max(logits, axis=0, keepdims=True)
    log_prior = largest[0] + jnp.log(jnp.sum(jnp.exp(logits - largest), axis=0))
    respons = jnp.exp(logits - log_prior[None, :])
    divergence = jnp.sum((log_post - log_prior) * alive_float)
    decoder_act = lax.optimization_barrier(gelu(decoder_pre).astype(BF16))
    residual = (mat_nn(decoder_act, genes_w) - genes_in.astype(F32)) * alive_float[:, None]
    grad_rebuilt = residual.astype(BF16)

    grad_genes = mat_tn(decoder_act, grad_rebuilt).astype(BF16)
    counts = jnp.concatenate(
        [jnp.full((1, 128), divergence), jnp.full((31, 128), jnp.sum(alive_float))], axis=0
    )
    (grad_act,), (count_parts,), (genes_other,), _, _, _ = meeting(
        5, (grad_rebuilt, genes_w, True, False), gathers=((counts, 0),), swaps=((grad_genes, 0),)
    )
    count_parts = jnp.sum(count_parts.reshape(shards, 32, 128)[:, :, 0], axis=0)
    mean_kl = count_parts[0] / (LATENT * count_parts[1])
    ramp_weight = jnp.minimum(1.0, (ramp_step[0] + 1).astype(F32) / RAMP)
    kl_scale = (
        ramp_weight * jax.nn.softplus(mean_kl - FREE_BITS) * jax.nn.sigmoid(mean_kl - FREE_BITS)
    )
    grad_pre = (grad_act * gelu_slope(decoder_pre)).astype(BF16)
    grad_dec = mat_tn(latent_low, grad_pre).astype(BF16)
    cell_weight = kl_scale * alive_float
    weighted = (respons * cell_weight[None, :])[:, :, None]
    grad_latent = mat_nt(grad_pre, dec_w) + jnp.sum(weighted * pulled, axis=0)
    grad_comps = jnp.concatenate(
        [
            -jnp.sum(weighted * pulled, axis=1),
            -jnp.sum(weighted * (0.5 * offsets * pulled - 0.5), axis=1),
        ],
        axis=0,
    )
    grad_means = grad_latent.astype(BF16)
    grad_logs = (grad_latent * (0.5 * spread) - 0.5 * cell_weight[:, None]).astype(BF16)
    grad_stats = jnp.concatenate([grad_means, grad_logs], axis=1)
    grad_latent_w = mat_tn(hidden, grad_stats).astype(BF16)
    (summed,), _, (latent_other, dec_other), (genes_parts,), _, _ = meeting(
        6,
        (grad_stats, latent_w, True, False),
        swaps=((grad_latent_w, 0), (grad_dec, 1)),
        exchanges=((grad_genes, genes_other, 0),),
    )
    grad_hidden = summed.astype(BF16)

    grad_down = mat_tn(activated, grad_hidden).astype(BF16)
    grad_upper = (mat_nt(grad_hidden, down_w) * gelu_slope(upper)).astype(BF16)
    grad_up = mat_tn(second_low, grad_upper).astype(BF16)
    (grad_norm_two,), _, (down_other, up_other), (latent_parts, dec_parts), _, _ = (
        meeting(
            7,
            (grad_upper, up_w, True, False),
            swaps=((grad_down, 1), (grad_up, 0)),
            exchanges=(
                (grad_latent_w, latent_other, 0),
                (grad_dec, dec_other, 1),
            ),
        )
    )
    grad_middle = grad_hidden.astype(F32) + norm_back(
        grad_norm_two, normed_two, scale_two, gain_two
    )
    middle_low = grad_middle.astype(BF16)
    grad_out = mat_tn(attended, middle_low).astype(BF16)
    grad_qkv_act = attend_back(middle_low, out_w, projected, log_totals, slide, alive)
    grad_qkv = mat_tn(first_low, grad_qkv_act).astype(BF16)
    (grad_norm_one,), _, (qkv_other, out_other), (down_parts, up_parts), _, _ = meeting(
        8,
        (grad_qkv_act, qkv, True, False),
        swaps=((grad_qkv, 0), (grad_out, 1)),
        exchanges=((grad_down, down_other, 1), (grad_up, up_other, 0)),
    )
    grad_start = grad_middle + norm_back(grad_norm_one, normed_one, scale_one, gain_one)
    start_low = grad_start.astype(BF16)

    norm_grads = jnp.stack(
        [
            jnp.sum(grad_norm_one * normed_one, axis=0),
            jnp.sum(grad_norm_one, axis=0),
            jnp.sum(grad_norm_two * normed_two, axis=0),
            jnp.sum(grad_norm_two, axis=0),
        ]
    )
    norm_grads = norm_grads.reshape(4, shards, width).transpose(1, 0, 2)
    comp_grads = grad_comps.reshape(2 * comp_count, shards, comp_width).transpose(1, 0, 2)
    small_grads = jnp.concatenate(
        [
            jnp.pad(norm_grads, ((0, 0), (0, 12), (0, 0))),
            jnp.pad(comp_grads, ((0, 0), (0, 0), (0, width - comp_width))),
        ],
        axis=1,
    ).reshape(shards * small_rows, width)
    if tiled:
        embed_parts, qkv_parts, out_parts, small_sum, grad_expression = tail(
            9,
            start_low,
            expression,
            embed,
            grad_rebuilt,
            grad_qkv,
            qkv_other,
            grad_out,
            out_other,
            small_grads.reshape(2, shards // 2, small_rows, width),
        )
    else:
        start_all = lax.all_gather(start_low, "section", axis=0, tiled=True)
        start_half = lax.dynamic_slice_in_dim(start_all, micro * (features // 2), features // 2, 1)
        grad_embed = mat_tn(expression, start_half).astype(BF16)
        grad_cells = (
            mat_nt(start_low, embed).astype(BF16).astype(F32) - grad_rebuilt.astype(F32)
        ).astype(BF16)
        grad_expression = lax.all_gather(grad_cells, "section", axis=0, tiled=True)
        small_other = lax.ppermute(
            lax.dynamic_slice_in_dim(
                small_grads, (1 - micro) * (shards // 2 * small_rows), shards // 2 * small_rows, 0
            ),
            "section",
            [(0, 1), (1, 0)],
        )
        _, _, _, (embed_parts, qkv_parts, out_parts, small_sum), _, _ = meeting(
            9,
            exchanges=(
                (grad_embed, None, 1),
                (grad_qkv, qkv_other, 0),
                (grad_out, out_other, 1),
                (small_grads, small_other, 0),
            ),
        )
    grad_query, grad_key, grad_value = jnp.split(qkv_parts, 3, axis=1)
    grad_mean, grad_logvar = jnp.split(latent_parts, 2, axis=1)
    return (
        embed_parts,
        small_sum[0],
        small_sum[1],
        grad_query,
        grad_key,
        grad_value,
        out_parts,
        small_sum[2],
        small_sum[3],
        up_parts,
        down_parts,
        grad_mean,
        grad_logvar,
        small_sum[16 : 16 + comp_count, :comp_width],
        small_sum[16 + comp_count :, :comp_width],
        dec_parts,
        genes_parts,
        grad_expression,
    )


def solution(mesh):
    weight_rows = P(("section", "dp"), "mp")
    weight_cols = P("mp", ("section", "dp"))
    vector = P(("section", "dp"))
    comps = P(None, ("mp", "section", "dp"))
    weights = (
        weight_cols, vector, vector, weight_rows, weight_rows, weight_rows, weight_cols,
        vector, vector, weight_rows, weight_cols, weight_rows, weight_rows, comps, comps,
        weight_cols, weight_rows,
    )
    return jax.shard_map(
        local,
        mesh=mesh,
        in_specs=(P("dp", "mp"), P(None, "dp"), P("dp"), P("dp", None), P(), P("dp", "mp"))
        + weights,
        out_specs=weights + (P("dp", "mp"),),
        check_vma=False,
    )
```

time: 613 us -> 503 us (0.82)
  matrix products: 88.2 us -> 36.3 us
  Pallas kernels: 437 us -> 395 us
  other arithmetic: 43.6 us -> 33.6 us
  local copies, waits for them, and re-layouts: 36.3 us -> 28.1 us
    pallas_call x11 -> x9, Pallas kernels: 437 us -> 337 us  [comm(): pl.pallas_call(functools.partial(comm_kernel, plan), out_shape=outputs, i...]
    pallas_call x0 -> x3, Pallas kernels: none -> 58.5 us  [the longest x1 47.8 us: tail(): pl.pallas_call(tail_kernel, out_shape=[jax.ShapeDtypeStruct((genes, width...]
    dot_general x8 -> x2, matrix products: 28.7 us -> 3.31 us  [mat_nt(): lax.dot_general(left, right, (((1,), (1,)), ((), ())), preferred_element_...]
    dot_general x8 -> x4, matrix products: 25.4 us -> 12.5 us  [mat_nn(): return jnp.dot(left, right, preferred_element_type=F32)]
    reduce_sum x13 -> x2, other arithmetic: 10.1 us -> 0.2 us  [the longest x1 0.12 us: local(): count_parts = jnp.sum(count_parts.reshape(shards, 32, 128)[:, :, 0], axis=0)]
    dot_general x8 -> x7, matrix products: 25.5 us -> 16.1 us  [mat_tn(): lax.dot_general(left, right, (((0,), (0,)), ((), ())), preferred_element_...]
    unnamed x218 -> x216, local copies, waits for them, and re-layouts: 26.6 us -> 19.3 us
    dot_general x4 -> x0, matrix products: 6.35 us -> none  [the longest x1 3.4 us: attend_back(): jnp.einsum('hqk,qhd->khd', probs.astype(BF16), g, preferred_element_type=...]
where the time goes in v2:
time: 503 us; the launch traced here: 498 us
  Pallas kernels  395 us (79%)
  matrix products  36.3 us (7%)
  other arithmetic  33.6 us (7%)
  local copies, waits for them, and re-layouts  28.1 us (6%)
    pallas_call x9, Pallas kernels, comm(): pl.pallas_call(functools.partial(comm_kernel, plan), out_shape=outputs, i...  337 us
    pallas_call x1, Pallas kernels, tail(): pl.pallas_call(tail_kernel, out_shape=[jax.ShapeDtypeStruct((genes, width...  47.8 us
    unnamed x216, local copies, waits for them, and re-layouts  19.3 us
    dot_general x7, matrix products, mat_tn(): lax.dot_general(left, right, (((0,), (0,)), ((), ())), preferred_element_...  16.1 us
    dot_general x4, matrix products, mat_nn(): return jnp.dot(left, right, preferred_element_type=F32)  12.5 us

profile of v2, /device:TPU:0, one launch (start us, length us, event | category | flops | bytes accessed | tf_op | source)
XLA Modules:
  0.0 498.3 jit_solution(3212385541167545814)
XLA Ops:
  0.8 0.9 constant_dynamic-slice_fusion
  1.7 3.6 multiply_sine_fusion.1
  5.4 35.9 %meet.9 = (bf16[3376,1024]{1,0:T(8,128)(2,1)}, bf16[384,128]{1,0:T(8,128)(2,1)S(1)}) custom-call(bf16[3376,128]{1,0:T(8,128)(2,1)S(1)} %copy-done.27, bf16[48,128]{1,0:T(8,128)(2,1)S(1)} %pad_maximum_fusion.3.refs_1_), custom_call_target="tpu_custom_call" | custom-call | flops 1000000 | bytes 90000000 | tf_op jit(solution)/shard_map/meet/pallas_call | solution.py:628
  41.4 42.8 %meet.10 = (f32[496,1024]{1,0:T(8,128)S(1)}, bf16[1024,768]{1,0:T(8,128)(2,1)S(1)}, bf16[256,1024]{1,0:T(8,128)(2,1)S(1)}, bf16[1024,1024]{1,0:T(8,128)(2,1)}) custom-call(bf16[992,3376]{1,0:T(8,128)(2,1)} %expression.1, bf16[3376,1024]{1,0:T(8,128)(2,1)} %get-tuple-element.55.refs_1_.embed, bf16[128,768]{1,0:T(8,128)(2,1)S(1)} %pad_maximum_fusion.1.refs_2_, ...), custom_call_target="tpu_custom_call" | custom-call | flops 1000000 | bytes 90000000 | tf_op jit(solution)/shard_map/meet/pallas_call | solution.py:628
  85.0 1.0 copy-done.16
  86.0 1.1 convolution_convert_fusion.4.projected
  87.2 0.9 copy-done.6
  88.4 0.7 fusion.48
  89.7 0.6 copy-done.36
  90.5 1.0 fusion.9
  91.5 1.9 copy-done.44
  93.4 0.9 fusion.10
  94.5 3.5 fusion.24
  98.0 0.8 copy.65.refs_0_
  98.9 0.9 copy-done.26
  99.9 0.9 copy-done.33
  100.8 36.9 %meet.11 = (f32[496,1024]{1,0:T(8,128)S(1)}, bf16[1024,1024]{1,0:T(8,128)(2,1)S(1)}, bf16[1024,256]{1,0:T(8,128)(2,1)S(1)}, bf16[128,1024]{1,0:T(8,128)(2,1)S(1)}) custom-call(bf16[496,256]{1,0:T(8,128)(2,1)S(1)} %copy-done.26, bf16[256,1024]{1,0:T(8,128)(2,1)S(1)} %get-tuple-element.59.refs_1_.out_w, bf16[1024,128]{1,0:T(8,128)(2,1)S(1)} %copy-done.33, ...), custom_call_target="tpu_custom_call" | custom-call | flops 1000000 | bytes 90000000 | tf_op jit(solution)/shard_map/meet/pallas_call | solution.py:628
  137.8 3.1 fusion.50
  141.3 3.1 multiply_convert_fusion.2
  144.4 1.6 copy.66.refs_2_
  146.0 1.2 copy-done.24
  147.2 37.5 %meet.12 = (f32[496,1024]{1,0:T(8,128)S(1)}, bf16[1024,3376]{1,0:T(8,128)(2,1)}) custom-call(bf16[496,1024]{1,0:T(8,128)(2,1)S(1)} %copy-done.24, bf16[1024,1024]{1,0:T(8,128)(2,1)S(1)} %get-tuple-element.62.refs_1_, bf16[128,3376]{1,0:T(8,128)(2,1)S(1)} %copy.66.refs_2_), custom_call_target="tpu_custom_call" | custom-call | flops 1000000 | bytes 90000000 | tf_op jit(solution)/shard_map/meet/pallas_call | solution.py:628
  185.7 0.9 copy-done.55
  187.2 1.2 fusion.6
  188.4 37.4 %meet.13 = (f32[496,1024]{1,0:T(8,128)S(1)}, f32[4,24,512]{2,1,0:T(8,128)S(1)}) custom-call(bf16[496,128]{1,0:T(8,128)(2,1)S(1)} %get-tuple-element.166.refs_0_, bf16[128,1024]{1,0:T(8,128)(2,1)S(1)} %copy-done.22, f32[24,512]{1,0:T(8,128)S(1)} %select_maximum_fusion.1.refs_2_), custom_call_target="tpu_custom_call" | custom-call | flops 1000000 | bytes 90000000 | tf_op jit(solution)/shard_map/meet/pallas_call | solution.py:628
  226.3 8.0 %multiply_convert_fusion.refs_0_.grad_rebuilt = bf16[496,3376]{1,0:T(8,128)(2,1)S(1)} fusion(bf16[496,1024]{1,0:T(8,128)(2,1)S(1)} %multiply_convert_fusion.1, bf16[1024,3376]{1,0:T(8,128)(2,1)} %get-tuple-element.67.refs_1_, f32[496]{0:T(512)} %get-tuple-element.164, bf16[992,3376]{1,0:T(8,128)(2,1)} %expression.1, s32[]{:T(128)S(6)} %select_n.18), kind=kOutput, calls=%fused_computation.1 | convolution fusion | flops 3436065792 | bytes 14629828 | tf_op jit(solution)/shard_map/dot_general | solution.py:31
  234.3 6.1 %convolution_convert_fusion.refs_3_.refs_4_ = bf16[1024,3376]{1,0:T(8,128)(2,1)} fusion(bf16[496,1024]{1,0:T(8,128)(2,1)S(1)} %multiply_convert_fusion.1, bf16[496,3376]{1,0:T(8,128)(2,1)S(1)} %multiply_convert_fusion.refs_0_.grad_rebuilt), kind=kOutput, calls=%fused_computation | convolution fusion | flops 3432824832 | bytes 11278848 | tf_op jit(solution)/shard_map/dot_general | solution.py:35
  240.5 1.6 reduce_sum.224
  242.0 0.8 fusion.29
  242.8 0.8 exponential_reduce_fusion
  243.6 0.7 slice.116
  244.3 1.8 convert_reduce_fusion
  246.1 1.3 concatenate.40
  247.5 37.0 %meet.14 = (f32[496,1024]{1,0:T(8,128)S(1)}, f32[256,128]{1,0:T(8,128)S(1)}, bf16[512,3376]{1,0:T(8,128)(2,1)}) custom-call(bf16[496,3376]{1,0:T(8,128)(2,1)S(1)} %multiply_convert_fusion.refs_0_.grad_rebuilt, bf16[1024,3376]{1,0:T(8,128)(2,1)} %get-tuple-element.67.refs_1_, f32[32,128]{1,0:T(8,128)S(1)} %concatenate.41.refs_2_, ...), custom_call_target="tpu_custom_call" | custom-call | flops 1000000 | bytes 90000000 | tf_op jit(solution)/shard_map/meet/pallas_call | solution.py:628
  284.6 0.9 fusion.16
  285.9 0.6 fusion.58
  288.8 2.4 fusion.2
  291.1 1.4 fusion.54
  292.6 0.5 convolution_convert_fusion.6.refs_2_.refs_4_
  293.6 36.0 %meet.15 = (f32[496,1024]{1,0:T(8,128)S(1)}, bf16[512,256]{1,0:T(8,128)(2,1)S(1)}, bf16[128,512]{1,0:T(8,128)(2,1)S(1)}, f32[128,3376]{1,0:T(8,128)S(1)}) custom-call(bf16[496,256]{1,0:T(8,128)(2,1)S(1)} %pad_maximum_fusion.refs_0_, bf16[1024,256]{1,0:T(8,128)(2,1)S(1)} %copy-done.13, bf16[1024,256]{1,0:T(8,128)(2,1)S(1)} %convolution_convert_fusion.6.refs_2_.refs_4_, ...), custom_call_target="tpu_custom_call" | custom-call | flops 1000000 | bytes 90000000 | tf_op jit(solution)/shard_map/meet/pallas_call | solution.py:628
  329.7 1.9 fusion.22.refs_0_
  331.9 2.8 convolution_convert_fusion.1.refs_3_.refs_5_
  334.7 2.7 convolution_convert_fusion.2.refs_2_.refs_4_
  337.3 36.6 %meet.16 = (f32[496,1024]{1,0:T(8,128)}, bf16[1024,512]{1,0:T(8,128)(2,1)S(1)}, bf16[512,1024]{1,0:T(8,128)(2,1)S(1)}, f32[128,256]{1,0:T(8,128)S(1)}, f32[128,128]{1,0:T(8,128)S(1)}) custom-call(bf16[496,1024]{1,0:T(8,128)(2,1)S(1)} %fusion.22.refs_0_, bf16[1024,1024]{1,0:T(8,128)(2,1)} %get-tuple-element.61.refs_1_, ...), custom_call_target="tpu_custom_call" | custom-call | flops 1000000 | bytes 90000000 | tf_op jit(solution)/shard_map/meet/pallas_call | solution.py:628
  374.0 3.8 multiply_reduce_fusion
  377.8 2.1 fusion.47
  381.2 4.7 attend_back.1.refs_0_
  385.9 3.2 convolution_convert_fusion.3.refs_2_.qkv
  389.2 36.8 %meet.17 = (f32[496,1024]{1,0:T(8,128)}, bf16[512,768]{1,0:T(8,128)(2,1)S(1)}, bf16[256,512]{1,0:T(8,128)(2,1)S(1)}, f32[1024,128]{1,0:T(8,128)S(1)}, f32[128,1024]{1,0:T(8,128)S(1)}) custom-call(bf16[496,768]{1,0:T(8,128)(2,1)S(1)} %attend_back.1.refs_0_, bf16[1024,768]{1,0:T(8,128)(2,1)} %copy-done.16, ...), custom_call_target="tpu_custom_call" | custom-call | flops 1000000 | bytes 90000000 | tf_op jit(solution)/shard_map/meet/pallas_call | solution.py:628
  426.0 2.8 multiply_reduce_fusion.1
  429.1 0.7 copy.71
  429.8 4.4 add_convert_fusion.start
  434.2 47.8 %tail.1 = (f32[3376,128]{1,0:T(8,128)}, f32[128,768]{1,0:T(8,128)}, f32[256,128]{1,0:T(8,128)}, f32[48,128]{1,0:T(8,128)}, bf16[496,3376]{1,0:T(8,128)(2,1)}, /*index=5*/bf16[496,3376]{1,0:T(8,128)(2,1)}) custom-call(bf16[496,1024]{1,0:T(8,128)(2,1)} %add_convert_fusion.start, bf16[992,3376]{1,0:T(8,128)(2,1)} %expression.1, ...), custom_call_target="tpu_custom_call" | custom-call | tf_op jit(solution)/shard_map/tail/pallas_call | solution.py:866
  482.1 6.0 %assemble.1 = bf16[992,3376]{1,0:T(8,128)(2,1)} custom-call(bf16[496,3376]{1,0:T(8,128)(2,1)} %get-tuple-element.90.own, bf16[496,3376]{1,0:T(8,128)(2,1)} %get-tuple-element.91.other), custom_call_target="tpu_custom_call" | custom-call | tf_op jit(solution)/shard_map/assemble/pallas_call | solution.py:900
  488.1 0.8 fusion.53
  488.9 0.6 fusion.56
  489.5 0.5 slice_bitcast_fusion.1
  490.0 0.7 fusion.55
  490.7 1.7 copy.72
  492.3 2.8 copy.84
  495.1 0.7 copy.85
  495.8 0.8 copy.86
  496.6 0.8 copy.87
  497.4 0.6 copy.88
  (257 shorter events, 7.3 us)
Async XLA Ops:
  0.7 88.4 %copy-start = (s32[2,3]{1,0:T(2,128)S(1)}, s32[2,3]{1,0:T(2,128)}, u32[]{:S(2)}) copy-start(s32[2,3]{1,0:T(2,128)} %param.26) | copy-start | bytes 76
  0.7 4.6 copy-start.93
  0.7 4.6 copy-start.92
  0.7 4.7 copy-start.102
  0.7 4.7 copy-start.101
  0.7 4.7 copy-start.100
  0.7 4.7 copy-start.99
  0.7 4.7 copy-start.27
  0.7 40.6 %copy-start.67 = (bf16[128,256]{1,0:T(8,128)(2,1)S(1)}, bf16[128,256]{1,0:T(8,128)(2,1)}, u32[]{:S(2)}) copy-start(bf16[128,256]{1,0:T(8,128)(2,1)} %param.32) | copy-start | bytes 196612
  0.8 40.6 %copy-start.66 = (bf16[128,256]{1,0:T(8,128)(2,1)S(1)}, bf16[128,256]{1,0:T(8,128)(2,1)}, u32[]{:S(2)}) copy-start(bf16[128,256]{1,0:T(8,128)(2,1)} %param.33) | copy-start | bytes 196612
  0.8 40.6 %copy-start.65 = (bf16[128,256]{1,0:T(8,128)(2,1)S(1)}, bf16[128,256]{1,0:T(8,128)(2,1)}, u32[]{:S(2)}) copy-start(bf16[128,256]{1,0:T(8,128)(2,1)} %param.34) | copy-start | bytes 196612
  0.8 40.6 %copy-start.35 = (bf16[256,128]{1,0:T(8,128)(2,1)S(1)}, bf16[256,128]{1,0:T(8,128)(2,1)}, u32[]{:S(2)}) copy-start(bf16[256,128]{1,0:T(8,128)(2,1)} %refs_3_.1) | copy-start | bytes 196612
  0.8 40.6 %copy-start.31 = (bf16[128,1024]{1,0:T(8,128)(2,1)S(1)}, bf16[128,1024]{1,0:T(8,128)(2,1)}, u32[]{:S(2)}) copy-start(bf16[128,1024]{1,0:T(8,128)(2,1)} %refs_4_.2) | copy-start | bytes 786436
  41.3 43.6 %copy-start.29 = (bf16[384,128]{1,0:T(8,128)(2,1)}, bf16[384,128]{1,0:T(8,128)(2,1)S(1)}, u32[]{:S(2)}) copy-start(bf16[384,128]{1,0:T(8,128)(2,1)S(1)} %get-tuple-element.57) | copy-start | bytes 294916
  84.2 14.7 %copy-start.8 = (bf16[256,1024]{1,0:T(8,128)(2,1)}, bf16[256,1024]{1,0:T(8,128)(2,1)S(1)}, u32[]{:S(2)}) copy-start(bf16[256,1024]{1,0:T(8,128)(2,1)S(1)} %get-tuple-element.59.refs_1_.out_w) | copy-start | bytes 1572868
  85.0 56.3 %copy-start.71 = (f32[1,8,128]{2,0,1:T(1,128)}, f32[1,8,128]{2,0,1:T(1,128)S(1)}, u32[]{:S(2)}) copy-start(f32[1,8,128]{2,0,1:T(1,128)S(1)} %get-tuple-element.192) | copy-start | bytes 12292
  85.0 56.3 %copy-start.96 = (f32[1,8,128]{2,0,1:T(1,128)}, f32[1,8,128]{2,0,1:T(1,128)S(1)}, u32[]{:S(2)}) copy-start(f32[1,8,128]{2,0,1:T(1,128)S(1)} %get-tuple-element.193) | copy-start | bytes 12292
  94.3 3.7 copy-start.75
  94.5 4.4 copy-start.78
  94.5 4.4 copy-start.79
  94.5 4.4 copy-start.38
  137.8 3.1 copy-start.21
  137.8 8.2 %copy-start.10 = (bf16[1024,1024]{1,0:T(8,128)(2,1)}, bf16[1024,1024]{1,0:T(8,128)(2,1)S(1)}, u32[]{:S(2)}) copy-start(bf16[1024,1024]{1,0:T(8,128)(2,1)S(1)} %get-tuple-element.62.refs_1_) | copy-start | bytes 6291460
  137.8 47.5 %copy-start.12 = (bf16[1024,256]{1,0:T(8,128)(2,1)}, bf16[1024,256]{1,0:T(8,128)(2,1)S(1)}, u32[]{:S(2)}) copy-start(bf16[1024,256]{1,0:T(8,128)(2,1)S(1)} %get-tuple-element.64.refs_1_) | copy-start | bytes 1572868
  137.8 3.5 copy-start.52
  140.9 3.5 copy-start.39
  140.9 3.5 copy-start.80
  141.3 3.1 copy-start.84
  147.2 37.5 %copy-start.40 = (f32[496,1024]{1,0:T(8,128)S(1)}, f32[496,1024]{1,0:T(8,128)}, u32[]{:S(2)}) copy-start(f32[496,1024]{1,0:T(8,128)} %copy-done.39) | copy-start | bytes 6094852
  185.3 3.2 copy-start.22
  186.6 39.6 %copy-start.48 = (f32[496,256]{1,0:T(8,128)}, f32[496,256]{1,0:T(8,128)S(1)}, u32[]{:S(2)}) copy-start(f32[496,256]{1,0:T(8,128)S(1)} %fusion.59) | copy-start | bytes 1523716
  186.8 39.5 %copy-start.50 = (f32[496,128]{1,0:T(8,128)}, f32[496,128]{1,0:T(8,128)S(1)}, u32[]{:S(2)}) copy-start(f32[496,128]{1,0:T(8,128)S(1)} %get-tuple-element.167) | copy-start | bytes 761860
  187.1 39.2 %copy-start.61 = (f32[16,128]{1,0:T(8,128)}, f32[16,128]{1,0:T(8,128)S(1)}, u32[]{:S(2)}) copy-start(f32[16,128]{1,0:T(8,128)S(1)} %exp.48) | copy-start | bytes 24580
  187.1 39.2 %copy-start.63 = (f32[16,128]{1,0:T(8,128)}, f32[16,128]{1,0:T(8,128)S(1)}, u32[]{:S(2)}) copy-start(f32[16,128]{1,0:T(8,128)S(1)} %sub.146) | copy-start | bytes 24580
  225.9 8.4 %copy-start.3 = (f32[496,1024]{1,0:T(8,128)}, f32[496,1024]{1,0:T(8,128)S(1)}, u32[]{:S(2)}) copy-start(f32[496,1024]{1,0:T(8,128)S(1)} %get-tuple-element.66) | copy-start | bytes 6094852
  225.9 8.4 %copy-start.34 = (f32[4,24,512]{2,1,0:T(8,128)}, f32[4,24,512]{2,1,0:T(8,128)S(1)}, u32[]{:S(2)}) copy-start(f32[4,24,512]{2,1,0:T(8,128)S(1)} %get-tuple-element.68) | copy-start | bytes 589828
  234.3 13.2 %copy-start.2 = (bf16[496,3376]{1,0:T(8,128)(2,1)}, bf16[496,3376]{1,0:T(8,128)(2,1)S(1)}, u32[]{:S(2)}) copy-start(bf16[496,3376]{1,0:T(8,128)(2,1)S(1)} %multiply_convert_fusion.refs_0_.grad_rebuilt) | copy-start | bytes 10046980
  247.5 37.0 %copy-start.4 = (f32[496,1024]{1,0:T(8,128)S(1)}, f32[496,1024]{1,0:T(8,128)}, u32[]{:S(2)}) copy-start(f32[496,1024]{1,0:T(8,128)} %copy-done.3) | copy-start | bytes 6094852
  284.5 4.2 copy-start.69
  284.5 4.2 copy-start.56
  284.5 4.2 copy-start.91
  284.5 4.2 copy-start.51
  284.5 4.2 copy-start.62
  284.6 4.2 copy-start.64
  285.5 5.7 %copy-start.23 = (bf16[128,1024]{1,0:T(8,128)(2,1)S(1)}, bf16[128,1024]{1,0:T(8,128)(2,1)}, u32[]{:S(2)}) copy-start(bf16[128,1024]{1,0:T(8,128)(2,1)} %copy-done.21) | copy-start | bytes 786436
  285.5 5.7 %copy-start.49 = (f32[496,256]{1,0:T(8,128)S(1)}, f32[496,256]{1,0:T(8,128)}, u32[]{:S(2)}) copy-start(f32[496,256]{1,0:T(8,128)} %copy-done.48) | copy-start | bytes 1523716
  285.5 7.1 %copy-start.47 = (bf16[496,1024]{1,0:T(8,128)(2,1)S(1)}, bf16[496,1024]{1,0:T(8,128)(2,1)}, u32[]{:S(2)}) copy-start(bf16[496,1024]{1,0:T(8,128)(2,1)} %copy-done.46) | copy-start | bytes 3047428
  293.6 36.0 %copy-start.11 = (bf16[1024,1024]{1,0:T(8,128)(2,1)S(1)}, bf16[1024,1024]{1,0:T(8,128)(2,1)}, u32[]{:S(2)}) copy-start(bf16[1024,1024]{1,0:T(8,128)(2,1)} %copy-done.10) | copy-start | bytes 6291460
  293.6 36.0 %copy-start.103 = (f32[496,1024]{1,0:T(8,128)S(1)}, f32[496,1024]{1,0:T(8,128)}, u32[]{:S(2)}) copy-start(f32[496,1024]{1,0:T(8,128)} %get-tuple-element.209) | copy-start | bytes 6094852
  373.9 3.8 copy-start.17
  374.0 3.8 copy-start.19
  374.0 3.8 copy-start.45
  380.4 8.7 %copy-start.5 = (bf16[256,1024]{1,0:T(8,128)(2,1)}, bf16[256,1024]{1,0:T(8,128)(2,1)S(1)}, u32[]{:S(2)}) copy-start(bf16[256,1024]{1,0:T(8,128)(2,1)S(1)} %convolution_convert_fusion.5.refs_3_.out) | copy-start | bytes 1572868
  380.4 5.5 %copy-start.74 = (f32[1,8,128]{2,0,1:T(1,128)S(1)}, f32[1,8,128]{2,0,1:T(1,128)}, u32[]{:S(2)}) copy-start(f32[1,8,128]{2,0,1:T(1,128)} %copy-done.73) | copy-start | bytes 12292
  380.7 5.2 %copy-start.43 = (f32[496,1024]{1,0:T(8,128)S(1)}, f32[496,1024]{1,0:T(8,128)}, u32[]{:S(2)}) copy-start(f32[496,1024]{1,0:T(8,128)} %copy-done.42) | copy-start | bytes 6094852
  380.8 5.2 %copy-start.95 = (f32[1,8,128]{2,0,1:T(1,128)S(1)}, f32[1,8,128]{2,0,1:T(1,128)}, u32[]{:S(2)}) copy-start(f32[1,8,128]{2,0,1:T(1,128)} %copy-done.94) | copy-start | bytes 12292
  385.9 3.2 copy-start.18
  385.9 3.2 copy-start.20
  389.1 36.8 %copy-start.83 = (f32[496]{0:T(512)S(1)}, f32[496]{0:T(512)}, u32[]{:S(2)}) copy-start(f32[496]{0:T(512)} %copy-done.82) | copy-start | bytes 5956
  389.2 36.8 %copy-start.87 = (f32[496]{0:T(512)S(1)}, f32[496]{0:T(512)}, u32[]{:S(2)}) copy-start(f32[496]{0:T(512)} %copy-done.86) | copy-start | bytes 5956
  482.1 6.0 %copy-start.57 = (f32[128,768]{1,0:T(8,128)S(1)}, f32[128,768]{1,0:T(8,128)}, u32[]{:S(2)}) copy-start(f32[128,768]{1,0:T(8,128)} %get-tuple-element.83) | copy-start | bytes 1179652
  482.1 6.8 %copy-start.90 = (f32[48,128]{1,0:T(8,128)S(1)}, f32[48,128]{1,0:T(8,128)}, u32[]{:S(2)}) copy-start(f32[48,128]{1,0:T(8,128)} %get-tuple-element.82) | copy-start | bytes 73732
  482.1 8.6 %copy-start.15 = (f32[128,3376]{1,0:T(8,128)S(1)}, f32[128,3376]{1,0:T(8,128)}, u32[]{:S(2)}) copy-start(f32[128,3376]{1,0:T(8,128)} %copy-done.14) | copy-start | bytes 5185540
  492.3 5.7 %copy-start.1 = (s32[2,3]{1,0:T(2,128)S(1)}, s32[2,3]{1,0:T(2,128)}, u32[]{:S(2)}) copy-start(s32[2,3]{1,0:T(2,128)} %param.26) | copy-start | bytes 76
  (40 other events, 74.9 us)

commit v3 on v2

--- a/solution.py
+++ b/solution.py
@@ -156,7 +156,11 @@
     return ref.at[:, pl.ds(pl.multiple_of(index * size, 128), size)]
 
 
-def line_sum(produce, hooks, part, out, from_left, from_right, to_right, to_left, got_left, got_right, sent_right, sent_left):
+def settle_plain(out, place, value):
+    out[place] = value
+
+
+def line_sum(produce, hooks, settle, part, out, from_left, from_right, to_right, to_left, got_left, got_right, sent_right, sent_left):
     me, count = lax.axis_index("mp"), lax.axis_size("mp")
     pieces, height, width = from_left.shape
     splits = pieces * width // part.shape[1]
@@ -225,17 +229,19 @@
 
         @pl.when(finished & has_left & has_right)
         def _():
-            out[place(done)] = (
-                part[place(done)] + from_left[done].astype(F32) + from_right[done].astype(F32)
+            settle(
+                out,
+                place(done),
+                part[place(done)] + from_left[done].astype(F32) + from_right[done].astype(F32),
             )
 
         @pl.when(finished & jnp.logical_not(has_left))
         def _():
-            out[place(done)] = part[place(done)] + from_right[done].astype(F32)
+            settle(out, place(done), part[place(done)] + from_right[done].astype(F32))
 
         @pl.when(finished & jnp.logical_not(has_right))
         def _():
-            out[place(done)] = part[place(done)] + from_left[done].astype(F32)
+            settle(out, place(done), part[place(done)] + from_left[done].astype(F32))
 
         return carry
 
@@ -527,7 +533,7 @@
         produce = start_product(reduces, *sources[0], *product)
         moments = reaction_moments(travelling)
         hooks = [(0, begin), (2, send_parts), (moments[0], react(after_one)), (moments[1], react(after_two))]
-        line_sum(produce, hooks, product[0], results[0][0], *line)
+        line_sum(produce, hooks, settle_plain, product[0], results[0][0], *line)
     else:
         begin()
         send_parts()
@@ -646,6 +652,283 @@
     return split
 
 
+def spread(remote, src, dst, axis, size, section, dp, peers, partner, to_x, to_y):
+    count_dp = lax.axis_size("dp")
+    rows = src.shape[0]
+    cut = halfway(rows)
+    peer_x, peer_y, peer_d = peers
+
+    def shard_of(index, start=0, stop=rows):
+        return block_of(dst, axis, section * count_dp + index, size, start, stop)
+
+    def still(*place):
+        return (shard_of(*place), shard_of(*place))
+
+    upper, lower = src.at[pl.ds(0, cut), :], src.at[pl.ds(cut, rows - cut), :]
+    return {
+        "own": remote(src, shard_of(dp), partner),
+        "x_upper": remote(upper, shard_of(dp, 0, cut), to_x),
+        "y_lower": remote(lower, shard_of(dp, cut), to_y),
+        "x_lower": remote(lower, shard_of(dp, cut), to_x),
+        "y_upper": remote(upper, shard_of(dp, 0, cut), to_y),
+        "pass_y": remote(*still(peer_x, 0, cut), to_y),
+        "pass_x": remote(*still(peer_y, cut), to_x),
+        "relay_x": remote(*still(peer_x), partner),
+        "relay_y": remote(*still(peer_y), partner),
+        "relay_upper": remote(*still(peer_d, 0, cut), partner),
+        "relay_lower": remote(*still(peer_d, cut), partner),
+    }
+
+
+def spread_steps(copies):
+    def begin():
+        for name in ("own", "x_upper", "y_lower", "x_lower", "y_upper"):
+            copies[name].start()
+
+    def follow(pairs):
+        def run():
+            for arrived, onward in pairs:
+                copies[arrived].wait_recv()
+                copies[onward].start()
+
+        return run
+
+    one = follow((("x_upper", "pass_y"), ("y_lower", "pass_x")))
+    two = follow((("x_lower", "relay_x"), ("y_upper", "relay_y")))
+    three = follow((("pass_y", "relay_upper"), ("pass_x", "relay_lower")))
+    return begin, one, two, three
+
+
+def head_kernel(plan, *refs):
+    refs = list(refs)
+
+    def take(number):
+        taken = refs[:number]
+        del refs[:number]
+        return taken
+
+    count = len(plan)
+    places, frequency, expression, embed = take(4)
+    shards = take(count)
+    start, embed_all = take(2)
+    gathered = take(count)
+    part, codes, cells_in, columns_in, cells_sem, columns_sem = take(6)
+    held = take(count)
+    line = take(8)
+    sent, got, local_sem = refs
+
+    section, z, dp = (lax.axis_index(name) for name in ("section", "mp", "dp"))
+    count_z, count_dp = lax.axis_size("mp"), lax.axis_size("dp")
+    row, col = dp // 2, dp % 2
+    peer_x, peer_y = row * 2 + (1 - col), (1 - row) * 2 + col
+    peer_d = (1 - row) * 2 + (1 - col)
+    peers = (peer_x, peer_y, peer_d)
+    partner, to_x, to_y = {"section": 1 - section}, {"dp": peer_x}, {"dp": peer_y}
+    rows, width = cells_in.shape[0], embed.shape[1]
+
+    barrier = pltpu.get_barrier_semaphore()
+    for device in (partner, to_x, to_y):
+        pl.semaphore_signal(barrier, inc=1, device_id=device)
+    for exists, neighbour in ((z > 0, z - 1), (z < count_z - 1, z + 1)):
+
+        @pl.when(exists)
+        def _(neighbour=neighbour):
+            pl.semaphore_signal(barrier, inc=1, device_id={"mp": neighbour})
+
+    at_end = (z == 0) | (z == count_z - 1)
+
+    @pl.when(at_end)
+    def _():
+        pl.semaphore_wait(barrier, 4)
+
+    @pl.when(jnp.logical_not(at_end))
+    def _():
+        pl.semaphore_wait(barrier, 5)
+
+    used = [0, 0]
+
+    def remote(src, dst, device):
+        index = used[0]
+        used[0] += 1
+        return pltpu.make_async_remote_copy(
+            src_ref=src, dst_ref=dst, send_sem=sent.at[index], recv_sem=got.at[index], device_id=device
+        )
+
+    def within(src, dst):
+        index = used[1]
+        used[1] += 1
+        return pltpu.make_async_copy(src, dst, local_sem.at[index])
+
+    place = (section, dp, peers, partner, to_x, to_y)
+    main = spread(remote, embed, embed_all, 1, width, *place)
+    begin, one, two, three = spread_steps(main)
+    rest = [
+        spread(remote, src, dst, axis, size, *place)
+        for src, dst, (axis, size) in zip(shards, gathered, plan)
+    ]
+    rest_steps = [spread_steps(copies) for copies in rest]
+    loads = [within(src, room) for src, room in zip(shards, held)]
+    kept = [within(columns_in.at[0], block_of(embed_all, 1, section * count_dp + dp, width))]
+    kept += [
+        within(room, block_of(dst, axis, section * count_dp + dp, size))
+        for room, dst, (axis, size) in zip(held, gathered, plan)
+    ]
+
+    order = [
+        section * count_dp + dp,
+        (1 - section) * count_dp + dp,
+        section * count_dp + peer_x,
+        section * count_dp + peer_y,
+        (1 - section) * count_dp + peer_x,
+        (1 - section) * count_dp + peer_y,
+        section * count_dp + peer_d,
+        (1 - section) * count_dp + peer_d,
+    ]
+
+    first = pl.multiple_of(section * rows, 16)
+    cells_copy = pltpu.make_async_copy(expression.at[pl.ds(first, rows), :], cells_in, cells_sem)
+
+    def fetch(turn):
+        src = embed if turn == 0 else block_of(embed_all, 1, order[turn], width)
+        return pltpu.make_async_copy(src, columns_in.at[turn], columns_sem.at[turn])
+
+    begin()
+    cells_copy.start()
+    fetch(0).start()
+    for copy in loads:
+        copy.start()
+
+    quarter = frequency.shape[1]
+    for axis in range(2):
+        along = places[:, axis : axis + 1] * frequency[...]
+        codes[:, 2 * axis * quarter : (2 * axis + 1) * quarter] = jnp.sin(along)
+        codes[:, (2 * axis + 1) * quarter : (2 * axis + 2) * quarter] = jnp.cos(along)
+    cells_copy.wait()
+
+    def keep():
+        for copy in loads:
+            copy.wait()
+        for copy in kept:
+            copy.start()
+
+    def produce(moment):
+        turn = lax.div(moment, 2)
+
+        @pl.when((lax.rem(moment, 2) == 0) & (turn < len(order)))
+        def _():
+            pltpu.make_async_copy(embed, columns_in.at[turn], columns_sem.at[turn]).wait()
+            part[:, pl.ds(pl.multiple_of(turn * width, width), width)] = mat_nn(
+                cells_in[...], columns_in[turn]
+            )
+
+    def settle(out, where, value):
+        span, columns = where
+        turn = lax.div(columns.start, width)
+        block = sum(jnp.where(turn == index, target, 0) for index, target in enumerate(order))
+        columns = pl.ds(pl.multiple_of(block * width, width), width)
+        out[span, columns] = value + codes[span, columns]
+
+    def arrived(names, turns):
+        def run():
+            for name in names:
+                main[name].wait_recv()
+            for turn in turns:
+                fetch(turn).start()
+
+        return run
+
+    def neighbours():
+        one()
+        for steps in rest_steps:
+            steps[0]()
+        two()
+        for turn in (2, 3):
+            fetch(turn).start()
+
+    def diagonal():
+        three()
+        fetch(6).start()
+
+    def later(number):
+        def run():
+            for steps in rest_steps:
+                steps[number]()
+
+        return run
+
+    hooks = [
+        (1, keep),
+        (2, arrived(("own",), (1,))),
+        (4, neighbours),
+        (8, arrived(("relay_x", "relay_y"), (4, 5))),
+        (12, diagonal),
+        (14, arrived(("relay_upper", "relay_lower"), (7,))),
+        (17, later(1)),
+        (21, later(2)),
+    ]
+    line_sum(produce, hooks, settle, part, start, *line)
+    for steps in rest_steps:
+        steps[3]()
+    for copies in rest:
+        for name in ("own", "relay_x", "relay_y", "relay_upper", "relay_lower"):
+            copies[name].wait_recv()
+    for copies in [main] + rest:
+        for copy in copies.values():
+            copy.wait_send()
+    for copy in kept:
+        copy.wait()
+
+
+def head(number, places, expression, embed, gathers):
+    sections, count_dp = lax.axis_size("section"), lax.axis_size("dp")
+    rows, genes = places.shape[0], expression.shape[1]
+    width = embed.shape[1]
+    total_parts = sections * count_dp
+    features = total_parts * width
+    quarter = features // 4
+    frequency = jnp.exp(jnp.arange(quarter, dtype=F32) * (-math.log(10000.0) / quarter))[None, :]
+    vmem, anywhere = pl.BlockSpec(memory_space=pltpu.VMEM), pl.BlockSpec(memory_space=pl.ANY)
+    plan = tuple((axis, shard.shape[axis]) for shard, axis in gathers)
+    shapes = [
+        shard.shape[:axis] + (shard.shape[axis] * total_parts,) + shard.shape[axis + 1 :]
+        for shard, axis in gathers
+    ]
+    pieces = features // 64
+    buffer = pltpu.VMEM((pieces, 256, 128), BF16)
+    copies = 11 * (1 + len(gathers))
+    results = pl.pallas_call(
+        functools.partial(head_kernel, plan),
+        out_shape=[
+            jax.ShapeDtypeStruct((rows, features), F32),
+            jax.ShapeDtypeStruct((genes, features), BF16),
+        ]
+        + [jax.ShapeDtypeStruct(shape, shard.dtype) for shape, (shard, _) in zip(shapes, gathers)],
+        in_specs=[vmem] * 2 + [anywhere] * (2 + len(gathers)),
+        out_specs=[vmem] + [anywhere] * (1 + len(gathers)),
+        scratch_shapes=[
+            pltpu.VMEM((rows, features), F32),
+            pltpu.VMEM((rows, features), F32),
+            pltpu.VMEM((rows, genes), BF16),
+            pltpu.VMEM((total_parts, genes, width), BF16),
+            pltpu.SemaphoreType.DMA,
+            pltpu.SemaphoreType.DMA((total_parts,)),
+        ]
+        + [pltpu.VMEM(shard.shape, shard.dtype) for shard, _ in gathers]
+        + [buffer] * 4
+        + [pltpu.SemaphoreType.DMA((pieces,))] * 4
+        + [
+            pltpu.SemaphoreType.DMA((copies,)),
+            pltpu.SemaphoreType.DMA((copies,)),
+            pltpu.SemaphoreType.DMA((1 + 2 * len(gathers),)),
+        ],
+        compiler_params=pltpu.CompilerParams(
+            collective_id=number, has_side_effects=True, vmem_limit_bytes=48 * 2**20
+        ),
+        name="head",
+    )(places, frequency, expression, embed, *[shard for shard, _ in gathers])
+    return results[0], results[1], results[2:]
+
+
 def trade(remote, mine, indices, from_x, from_y, inbound, to_x, to_y):
     rows = from_x.shape[0]
     cut = halfway(rows)
@@ -910,6 +1193,355 @@
     return list(results[:4]) + [whole]
 
 
+def line_pipe(produce, hooks, items, spacing, part, total, from_left, from_right, to_right, to_left, got_left, got_right, sent_right, sent_left):
+    me, count = lax.axis_index("mp"), lax.axis_size("mp")
+    pieces = part.shape[2] // 128
+    has_right, has_left = me < count - 1, me > 0
+
+    def place(slot):
+        column = lax.rem(slot, spacing) * 128
+        return (lax.rem(lax.div(slot, spacing), 2), slice(None), pl.ds(pl.multiple_of(column, 128), 128))
+
+    def rightward(slot):
+        return pltpu.make_async_remote_copy(
+            src_ref=to_right.at[slot],
+            dst_ref=from_left.at[slot],
+            send_sem=sent_right.at[slot],
+            recv_sem=got_left.at[slot],
+            device_id={"mp": me + 1},
+        )
+
+    def leftward(slot):
+        return pltpu.make_async_remote_copy(
+            src_ref=to_left.at[slot],
+            dst_ref=from_right.at[slot],
+            send_sem=sent_left.at[slot],
+            recv_sem=got_right.at[slot],
+            device_id={"mp": me - 1},
+        )
+
+    def used(slot):
+        return (slot >= 0) & (slot < items * spacing) & (lax.rem(slot, spacing) < pieces)
+
+    def flow(slot, copy, has_source, has_target, source, target):
+        @pl.when(used(slot))
+        def _():
+            @pl.when(has_source)
+            def _():
+                copy(slot).wait_recv()
+
+            @pl.when(has_target & has_source)
+            def _():
+                target[slot] = (part[place(slot)] + source[slot].astype(F32)).astype(BF16)
+
+            @pl.when(has_target & jnp.logical_not(has_source))
+            def _():
+                target[slot] = part[place(slot)].astype(BF16)
+
+            @pl.when(has_target)
+            def _():
+                copy(slot).start()
+
+    right_half = lax.div(2 * me + 1, count)
+    trail = HOP_LAG * (right_half * me + (1 - right_half) * (count - 1 - me))
+
+    def step(moment, carry):
+        for when, hook in hooks:
+            pl.when(moment == when)(hook)
+        produce(moment)
+        flow(moment - HOP_LAG * me, rightward, has_left, has_right, from_left, to_right)
+        flow(
+            moment - HOP_LAG * (count - 1 - me), leftward, has_right, has_left, from_right, to_left
+        )
+        done = moment - trail
+
+        @pl.when(used(done) & has_left & has_right)
+        def _():
+            total[place(done)] = (
+                part[place(done)] + from_left[done].astype(F32) + from_right[done].astype(F32)
+            )
+
+        @pl.when(used(done) & jnp.logical_not(has_left))
+        def _():
+            total[place(done)] = part[place(done)] + from_right[done].astype(F32)
+
+        @pl.when(used(done) & jnp.logical_not(has_right))
+        def _():
+            total[place(done)] = part[place(done)] + from_left[done].astype(F32)
+
+        return carry
+
+    lax.fori_loop(0, (items + 1) * spacing, step, 0)
+
+    def finish(slot, carry):
+        @pl.when(used(slot) & has_right)
+        def _():
+            rightward(slot).wait_send()
+
+        @pl.when(used(slot) & has_left)
+        def _():
+            leftward(slot).wait_send()
+
+        return carry
+
+    lax.fori_loop(0, items * spacing, finish, 0)
+
+
+def pipe_spacing(pieces, count):
+    return max(pieces + 1, (pieces - 1 + HOP_LAG * (count - 1)) // 2 + 1)
+
+
+def middle_kernel(
+    plan, spacing, attended, start, gain, bias, out_w, noise, centers, spreads, *refs
+):
+    refs = list(refs)
+
+    def take(number):
+        taken = refs[:number]
+        del refs[:number]
+        return taken
+
+    count = len(plan)
+    shards = take(count)
+    (normed_out, scale_out, second_out, upper_out, active_out, hidden_out, log_vars_out,
+     latent_out, spread_out, latent_low_out, decoder_out, density_all) = take(12)
+    gathered = take(count)
+    part, total, kept_rows, density = take(4)
+    up_in, down_in, latent_in, dec_in = take(4)
+    held = take(count)
+    line = take(8)
+    sent, got, local_sem = refs
+
+    section, z, dp = (lax.axis_index(name) for name in ("section", "mp", "dp"))
+    count_z, count_dp = lax.axis_size("mp"), lax.axis_size("dp")
+    row, col = dp // 2, dp % 2
+    peer_x, peer_y = row * 2 + (1 - col), (1 - row) * 2 + col
+    peers = (peer_x, peer_y, (1 - row) * 2 + (1 - col))
+    partner, to_x, to_y = {"section": 1 - section}, {"dp": peer_x}, {"dp": peer_y}
+    cells, latents = noise.shape
+    half_rows = part.shape[1]
+    comp_count = centers.shape[0]
+
+    barrier = pltpu.get_barrier_semaphore()
+    for device in (partner, to_x, to_y):
+        pl.semaphore_signal(barrier, inc=1, device_id=device)
+    for step in range(1, count_z):
+        pl.semaphore_signal(barrier, inc=1, device_id={"mp": (z + step) % count_z})
+    pl.semaphore_wait(barrier, 3 + count_z - 1)
+
+    used = [0, 0]
+
+    def remote(src, dst, device):
+        index = used[0]
+        used[0] += 1
+        return pltpu.make_async_remote_copy(
+            src_ref=src, dst_ref=dst, send_sem=sent.at[index], recv_sem=got.at[index], device_id=device
+        )
+
+    def within(src, dst):
+        index = used[1]
+        used[1] += 1
+        return pltpu.make_async_copy(src, dst, local_sem.at[index])
+
+    around = (section, dp, peers, partner, to_x, to_y)
+    spreads_of = [
+        spread(remote, src, dst, axis, size, *around)
+        for src, dst, (axis, size) in zip(shards, gathered, plan)
+    ]
+    steps_of = [spread_steps(copies) for copies in spreads_of]
+    loads = [within(src, room) for src, room in zip(shards, held)]
+    keeps = [
+        within(room, block_of(dst, axis, section * count_dp + dp, size))
+        for room, dst, (axis, size) in zip(held, gathered, plan)
+    ]
+    fetches = [
+        within(src, dst) for src, dst in zip(gathered, (up_in, down_in, latent_in, dec_in))
+    ]
+    density_sends = [
+        remote(density, density_all.at[z], {"mp": (z + step) % count_z})
+        for step in range(1, count_z)
+    ]
+    density_keep = within(density, density_all.at[z])
+
+    def run_steps(items, number):
+        def run():
+            for item in items:
+                steps_of[item][number]()
+
+        return run
+
+    def keep():
+        for load in loads:
+            load.wait()
+        for copy in keeps:
+            copy.start()
+
+    near, far = list(range(count - 1)), [count - 1]
+
+    def fetch():
+        for item in near:
+            for name in ("own", "relay_x", "relay_y", "relay_upper", "relay_lower"):
+                spreads_of[item][name].wait_recv()
+            keeps[item].wait()
+        for copy in fetches:
+            copy.start()
+        for copy in fetches:
+            copy.wait()
+
+    def share():
+        for copy in density_sends + [density_keep]:
+            copy.start()
+
+    for load in loads:
+        load.start()
+
+    def rows_of(half):
+        return pl.ds(pl.multiple_of(half * (cells - half_rows), 16), half_rows)
+
+    def out_product(half):
+        part[half] = mat_nn(attended[rows_of(half), :], out_w[...])
+
+    def feed_forward(half):
+        rows = rows_of(half)
+        values = start[rows, :] + total[half]
+        kept_rows[half] = values
+        normed, scale = normalize(values)
+        second = (normed * gain[...] + bias[...]).astype(BF16)
+        upper = mat_nn(second, up_in[...])
+        active = gelu(upper).astype(BF16)
+        part[half] = mat_nn(active, down_in[...])
+        normed_out[rows, :] = normed
+        scale_out[rows, :] = scale
+        second_out[rows, :] = second
+        upper_out[rows, :] = upper
+        active_out[rows, :] = active
+
+    def latents_of(half):
+        rows = rows_of(half)
+        hidden = (kept_rows[half] + total[half]).astype(BF16)
+        hidden_out[rows, :] = hidden
+        stats = mat_nn(hidden, latent_in[...])
+        means, log_vars = stats[:, :latents], stats[:, latents:]
+        own_noise = noise[rows, :]
+        scaled = jnp.exp(0.5 * log_vars) * own_noise
+        latent = means + scaled
+        low = latent.astype(BF16)
+        part[half] = mat_nn(low, dec_in[...])
+        log_vars_out[rows, :] = log_vars
+        spread_out[rows, :] = scaled
+        latent_out[rows, :] = latent
+        latent_low_out[rows, :] = low
+        lane = lax.broadcasted_iota(jnp.int32, (half_rows, 128), 1)
+        columns = jnp.sum(
+            -0.5 * LOG_TWO_PI - 0.5 * log_vars - 0.5 * own_noise * own_noise, axis=1, keepdims=True
+        )
+        table = jnp.where(lane == comp_count, columns, 0.0)
+        for index in range(comp_count):
+            log_spread = spreads[index : index + 1, :]
+            offset = latent - centers[index : index + 1, :]
+            columns = jnp.sum(
+                -0.5 * LOG_TWO_PI - 0.5 * log_spread - 0.5 * offset * offset * jnp.exp(-log_spread),
+                axis=1,
+                keepdims=True,
+            )
+            table = jnp.where(lane == index, columns, table)
+        density[:, pl.ds(pl.multiple_of(half * half_rows, 128), half_rows)] = table.T[
+            : density.shape[0], :
+        ]
+
+    def conclude(half):
+        decoder_out[rows_of(half), :] = total[half]
+
+    def produce(moment):
+        item = lax.div(moment, spacing)
+        half, stage = lax.rem(item, 2), lax.div(item, 2)
+        begins = lax.rem(moment, spacing) == 0
+        for number, work in enumerate((out_product, feed_forward, latents_of, conclude)):
+            pl.when(begins & (stage == number))(functools.partial(work, half))
+
+    hooks = [
+        (0, run_steps(near, 0)),
+        (1, keep),
+        (7, run_steps(near, 1)),
+        (13, run_steps(near, 2)),
+        (16, run_steps(near, 3)),
+        (2 * spacing, fetch),
+        (2 * spacing + 1, run_steps(far, 0)),
+        (2 * spacing + 10, run_steps(far, 1)),
+        (2 * spacing + 18, run_steps(far, 2)),
+        (2 * spacing + 26, run_steps(far, 3)),
+        (5 * spacing + 1, share),
+    ]
+    line_pipe(produce, hooks, 6, spacing, part, total, *line)
+    conclude(1)
+    for item in far:
+        for name in ("own", "relay_x", "relay_y", "relay_upper", "relay_lower"):
+            spreads_of[item][name].wait_recv()
+        keeps[item].wait()
+    for copies in spreads_of:
+        for copy in copies.values():
+            copy.wait_send()
+    for copy in density_sends:
+        copy.wait()
+    density_keep.wait()
+
+
+def middle(number, attended, start, gain, bias, out_w, noise, centers, spreads, gathers):
+    sections, count_dp, count_z = (lax.axis_size(name) for name in ("section", "dp", "mp"))
+    cells, features = start.shape
+    latents = noise.shape[1]
+    total_parts = sections * count_dp
+    pieces = features // 128
+    spacing = pipe_spacing(pieces, count_z)
+    slots = 6 * spacing
+    half_rows = 256
+    plan = tuple((axis, shard.shape[axis]) for shard, axis in gathers)
+    shapes = [
+        shard.shape[:axis] + (shard.shape[axis] * total_parts,) + shard.shape[axis + 1 :]
+        for shard, axis in gathers
+    ]
+    units = shapes[0][1]
+    vmem, anywhere = pl.BlockSpec(memory_space=pltpu.VMEM), pl.BlockSpec(memory_space=pl.ANY)
+    outputs = [
+        ((cells, features), F32),
+        ((cells, 1), F32),
+        ((cells, features), BF16),
+        ((cells, units), F32),
+        ((cells, units), BF16),
+        ((cells, features), BF16),
+        ((cells, latents), F32),
+        ((cells, latents), F32),
+        ((cells, latents), F32),
+        ((cells, latents), BF16),
+        ((cells, features), F32),
+        ((count_z, 24, 2 * half_rows), F32),
+    ] + [(shape, BF16) for shape in shapes]
+    buffer = pltpu.VMEM((slots, half_rows, 128), BF16)
+    copies = 11 * len(gathers) + count_z - 1
+    halves = pltpu.VMEM((2, half_rows, features), F32)
+    results = pl.pallas_call(
+        functools.partial(middle_kernel, plan, spacing),
+        out_shape=[jax.ShapeDtypeStruct(*item) for item in outputs],
+        in_specs=[vmem] * 8 + [anywhere] * len(gathers),
+        out_specs=[vmem] * 11 + [anywhere] * (1 + len(gathers)),
+        scratch_shapes=[halves, halves, halves, pltpu.VMEM((24, 2 * half_rows), F32)]
+        + [pltpu.VMEM(shape, BF16) for shape in shapes[:-1]]
+        + [pltpu.VMEM(shard.shape, BF16) for shard, _ in gathers]
+        + [buffer] * 4
+        + [pltpu.SemaphoreType.DMA((slots,))] * 4
+        + [
+            pltpu.SemaphoreType.DMA((copies,)),
+            pltpu.SemaphoreType.DMA((copies,)),
+            pltpu.SemaphoreType.DMA((3 * len(gathers),)),
+        ],
+        compiler_params=pltpu.CompilerParams(
+            collective_id=number, has_side_effects=True, vmem_limit_bytes=60 * 2**20
+        ),
+        name="middle",
+    )(attended, start, gain, bias, out_w, noise, centers, spreads, *[shard for shard, _ in gathers])
+    return results[:12], results[12:]
+
+
 def meet(tiled, number, reduce=None, gathers=(), swaps=(), exchanges=(), shares=(), pairs=()):
     if tiled:
         return comm(number, reduce, gathers, swaps, exchanges, shares, pairs)
@@ -991,7 +1623,6 @@
     noise = own(latent_noise)
     slide = slide_ids(lax.dynamic_index_in_dim(lengths, micro, 0, False), cells)
     allowed = allowed_pairs(slide, alive)
-    positions = position_code(own(cell_xy, 1), features)
 
     norm_block = jnp.pad(jnp.stack([ln1_gain, ln1_bias, ln2_gain, ln2_bias]), ((0, 12), (0, 0)))
     comp_block = jnp.pad(
@@ -999,56 +1630,82 @@
     )
     small = jnp.concatenate([norm_block, comp_block], axis=0)
     small_rows = small.shape[0]
-    _, (embed, small_all), _, _, _, _ = meeting(0, gathers=((gene_embed, 1), (small, 0)))
+    qkv_shard = jnp.concatenate([w_query, w_key, w_value], axis=1)
+    places = own(cell_xy, 1)
+    weights = ((small, 0), (qkv_shard, 0), (w_out, 1))
+    if tiled:
+        start, embed, (small_all, qkv, out_w) = head(
+            0, places.T, expression, gene_embed, weights
+        )
+    else:
+        _, (embed, small_all, qkv, out_w), _, _, _, _ = meeting(
+            0, gathers=((gene_embed, 1),) + weights
+        )
+        (summed,), _, _, _, _, _ = meeting(1, (expression, embed, False, True))
+        start = summed + position_code(places, features)
     small_all = small_all.reshape(shards, small_rows, width).astype(F32)
     norm_params = small_all[:, :4].transpose(1, 0, 2).reshape(4, features)
     gain_one, bias_one, gain_two, bias_two = (norm_params[i : i + 1] for i in range(4))
     comps = small_all[:, 16:, :comp_width].transpose(1, 0, 2).reshape(2 * comp_count, -1)
     centers, spreads = comps[:comp_count], comps[comp_count:]
 
-    qkv_shard = jnp.concatenate([w_query, w_key, w_value], axis=1)
-    (summed,), (qkv, out_w, up_w), _, _, _, _ = meeting(
-        1, (expression, embed, False, True), gathers=((qkv_shard, 0), (w_out, 1), (w_up, 0))
-    )
-    start = summed + positions
     normed_one, scale_one = normalize(start)
     first_low = (normed_one * gain_one + bias_one).astype(BF16)
     projected = mat_nn(first_low, qkv).astype(BF16)
     queries, keys, values = jnp.split(projected, 3, axis=1)
     attended, log_totals = attend(queries, keys, values, allowed)
     latent_shard = jnp.concatenate([w_mean, w_logvar], axis=1)
-    (summed,), (down_w, latent_w, dec_w), _, _, _, _ = meeting(
-        2, (attended, out_w, False, False), gathers=((w_down, 1), (latent_shard, 0), (w_dec, 1))
-    )
-    after_attn = start + summed
-    normed_two, scale_two = normalize(after_attn)
-    second_low = (normed_two * gain_two + bias_two).astype(BF16)
-    upper = mat_nn(second_low, up_w)
-    activated = gelu(upper).astype(BF16)
-    (summed,), (genes_w,), _, _, _, _ = meeting(
-        3, (activated, down_w, False, False), gathers=((w_genes, 0),)
-    )
-    hidden = (after_attn + summed).astype(BF16)
-
-    stats = mat_nn(hidden, latent_w)
-    means, log_vars = stats[:, :latent_cols], stats[:, latent_cols:]
-    spread = jnp.exp(0.5 * log_vars) * noise
-    latent = means + spread
-    latent_low = latent.astype(BF16)
-    post_part = jnp.sum(-0.5 * LOG_TWO_PI - 0.5 * log_vars - 0.5 * noise * noise, axis=1)
     precision = jnp.exp(-spreads)
-    offsets = latent[None] - centers[:, None, :]
-    pulled = offsets * precision[:, None, :]
-    comp_part = jnp.sum(
-        -0.5 * LOG_TWO_PI - 0.5 * spreads[:, None, :] - 0.5 * offsets * pulled, axis=2
-    )
-    density_part = jnp.pad(
-        jnp.concatenate([comp_part, post_part[None]], axis=0), ((0, 7), (0, -cells % 128))
-    )
-    (decoder_pre,), _, _, _, (density_parts,), _ = meeting(
-        4, (latent_low, dec_w, False, False), shares=(density_part,)
-    )
-    densities = jnp.sum(density_parts, axis=0)[:, :cells]
+    if tiled:
+        states, (up_w, down_w, latent_w, dec_w, genes_w) = middle(
+            1,
+            attended,
+            start,
+            gain_two,
+            bias_two,
+            out_w,
+            noise,
+            centers,
+            spreads,
+            ((w_up, 0), (w_down, 1), (latent_shard, 0), (w_dec, 1), (w_genes, 0)),
+        )
+        (normed_two, scale_two, second_low, upper, activated, hidden, log_vars, latent, spread_latent,
+         latent_low, decoder_pre, density_parts) = states
+        density = jnp.sum(density_parts, axis=0)
+        rows = density.shape[1] // 2
+        densities = jnp.concatenate([density[:, :rows], density[:, 3 * rows - cells :]], axis=1)
+    else:
+        (summed,), (up_w, down_w, latent_w, dec_w), _, _, _, _ = meeting(
+            2, (attended, out_w, False, False), gathers=((w_up, 0), (w_down, 1), (latent_shard, 0), (w_dec, 1))
+        )
+        after_attn = start + summed
+        normed_two, scale_two = normalize(after_attn)
+        second_low = (normed_two * gain_two + bias_two).astype(BF16)
+        upper = mat_nn(second_low, up_w)
+        activated = gelu(upper).astype(BF16)
+        (summed,), (genes_w,), _, _, _, _ = meeting(
+            3, (activated, down_w, False, False), gathers=((w_genes, 0),)
+        )
+        hidden = (after_attn + summed).astype(BF16)
+
+        stats = mat_nn(hidden, latent_w)
+        means, log_vars = stats[:, :latent_cols], stats[:, latent_cols:]
+        spread_latent = jnp.exp(0.5 * log_vars) * noise
+        latent = means + spread_latent
+        latent_low = latent.astype(BF16)
+        post_part = jnp.sum(-0.5 * LOG_TWO_PI - 0.5 * log_vars - 0.5 * noise * noise, axis=1)
+        offsets = latent[None] - centers[:, None, :]
+        pulled = offsets * precision[:, None, :]
+        comp_part = jnp.sum(
+            -0.5 * LOG_TWO_PI - 0.5 * spreads[:, None, :] - 0.5 * offsets * pulled, axis=2
+        )
+        density_part = jnp.pad(
+            jnp.concatenate([comp_part, post_part[None]], axis=0), ((0, 7), (0, -cells % 128))
+        )
+        (decoder_pre,), _, _, _, (density_parts,), _ = meeting(
+            4, (latent_low, dec_w, False, False), shares=(density_part,)
+        )
+        densities = jnp.sum(density_parts, axis=0)[:, :cells]
     logits = densities[:comp_count] - math.log(comp_count)
     log_post = densities[comp_count]
     largest = jnp.max(logits, axis=0, keepdims=True)
@@ -1075,6 +1732,8 @@
     grad_pre = (grad_act * gelu_slope(decoder_pre)).astype(BF16)
     grad_dec = mat_tn(latent_low, grad_pre).astype(BF16)
     cell_weight = kl_scale * alive_float
+    offsets = latent[None] - centers[:, None, :]
+    pulled = offsets * precision[:, None, :]
     weighted = (respons * cell_weight[None, :])[:, :, None]
     grad_latent = mat_nt(grad_pre, dec_w) + jnp.sum(weighted * pulled, axis=0)
     grad_comps = jnp.concatenate(
@@ -1085,7 +1744,7 @@
         axis=0,
     )
     grad_means = grad_latent.astype(BF16)
-    grad_logs = (grad_latent * (0.5 * spread) - 0.5 * cell_weight[:, None]).astype(BF16)
+    grad_logs = (grad_latent * (0.5 * spread_latent) - 0.5 * cell_weight[:, None]).astype(BF16)
     grad_stats = jnp.concatenate([grad_means, grad_logs], axis=1)
     grad_latent_w = mat_tn(hidden, grad_stats).astype(BF16)
     (summed,), _, (latent_other, dec_other), (genes_parts,), _, _ = meeting(

time: 503 us -> 470 us (0.934)
  Pallas kernels: 395 us -> 369 us
  other arithmetic: 33.6 us -> 27.4 us
    pallas_call x9 -> x4, Pallas kernels: 337 us -> 146 us  [comm(): pl.pallas_call(functools.partial(comm_kernel, plan), out_shape=outputs, i...]
    pallas_call x0 -> x2, Pallas kernels: none -> 165 us  [the longest x1 106 us: middle(): pl.pallas_call(functools.partial(middle_kernel, plan, spacing), out_shape...]
    dot_general x4 -> x2, matrix products: 12.5 us -> 8.73 us  [mat_nn(): return jnp.dot(left, right, preferred_element_type=F32)]
    unnamed x216 -> x158, local copies, waits for them, and re-layouts: 19.3 us -> 21 us
where the time goes in v3:
time: 470 us; the launch traced here: 465 us
  Pallas kernels  369 us (79%)
  local copies, waits for them, and re-layouts  32.3 us (7%)
  matrix products  31.4 us (7%)
  other arithmetic  27.4 us (6%)
    pallas_call x4, Pallas kernels, comm(): pl.pallas_call(functools.partial(comm_kernel, plan), out_shape=outputs, i...  146 us
    pallas_call x1, Pallas kernels, middle(): pl.pallas_call(functools.partial(middle_kernel, plan, spacing), out_shape...  106 us
    pallas_call x1, Pallas kernels, head(): pl.pallas_call(functools.partial(head_kernel, plan), out_shape=[jax.Shape...  59 us
    pallas_call x1, Pallas kernels, tail(): pl.pallas_call(tail_kernel, out_shape=[jax.ShapeDtypeStruct((genes, width...  48.4 us
    unnamed x158, local copies, waits for them, and re-layouts  21 us
    dot_general x7, matrix products, mat_tn(): lax.dot_general(left, right, (((0,), (0,)), ((), ())), preferred_element_...  15.8 us

profile of v3, /device:TPU:0, one launch (start us, length us, event | category | flops | bytes accessed | tf_op | source)
XLA Modules:
  0.0 464.5 jit_solution(18141641236415377796)
XLA Ops:
  0.7 0.8 constant_dynamic-slice_fusion.2
  1.7 0.9 pad_maximum_fusion.1.refs_5_
  2.6 0.7 fusion.28
  3.3 0.7 fusion.36
  4.0 1.2 copy-done.20
  5.2 0.8 copy-done.28
  6.0 59.0 %head.1 = (f32[496,1024]{1,0:T(8,128)S(1)}, bf16[3376,1024]{1,0:T(8,128)(2,1)}, bf16[384,128]{1,0:T(8,128)(2,1)S(1)}, bf16[1024,768]{1,0:T(8,128)(2,1)S(1)}, bf16[256,1024]{1,0:T(8,128)(2,1)S(1)}) custom-call(f32[496,2]{1,0:T(8,128)S(1)} %bitcast.76, f32[1,256]{1,0:T(1,128)S(1)} %multiply_exponential_fusion.refs_1_, bf16[992,3376]{1,0:T(8,128)(2,1)} %expression.1, ...), custom_call_target="tpu_custom_call" | custom-call | tf_op jit(solution)/shard_map/head/pallas_call | solution.py:899
  65.1 0.8 copy-done.8
  65.9 1.1 copy-done.14
  67.6 0.6 slice_bitcast_fusion.7
  68.4 0.8 copy-done.15
  69.2 1.1 convolution_convert_fusion.4.projected
  70.4 0.9 copy-done.6
  72.2 1.0 fusion.7
  73.2 2.0 copy-done.34
  75.1 0.9 fusion.8
  76.2 3.5 fusion.22
  79.7 0.8 copy.73.attended
  80.7 0.7 slice.91.centers
  81.4 0.7 slice.93.spreads
  82.0 0.7 constant_dynamic-slice_fusion.noise
  82.8 1.7 copy.74.refs_4_
  84.5 0.6 pad_maximum_fusion.2.refs_2_
  85.1 105.6 %middle.1 = (f32[496,1024]{1,0:T(8,128)}, f32[496,1]{1,0:T(8,128)}, bf16[496,1024]{1,0:T(8,128)(2,1)}, f32[496,1024]{1,0:T(8,128)}, bf16[496,1024]{1,0:T(8,128)(...) custom-call(bf16[496,256]{1,0:T(8,128)(2,1)} %copy.73.attended, ...), custom_call_target="tpu_custom_call" | custom-call | tf_op jit(solution)/shard_map/middle/pallas_call | solution.py:1522
  190.7 1.9 multiply_convert_fusion.1
  192.7 7.7 %multiply_convert_fusion.refs_0_.grad_rebuilt = bf16[496,3376]{1,0:T(8,128)(2,1)S(1)} fusion(bf16[496,1024]{1,0:T(8,128)(2,1)S(1)} %multiply_convert_fusion.1, bf16[1024,3376]{1,0:T(8,128)(2,1)} %get-tuple-element.67.refs_1_, f32[496]{0:T(512)S(1)} %get-tuple-element.178, bf16[992,3376]{1,0:T(8,128)(2,1)} %expression.1, s32[]{:T(128)S(6)} %select_n.18), kind=kOutput, calls=%fused_computation.1 | convolution fusion | flops 3436065792 | bytes 14629828 | tf_op jit(solution)/shard_map/dot_general | solution.py:31
  200.3 6.1 %convolution_convert_fusion.refs_3_.refs_4_ = bf16[1024,3376]{1,0:T(8,128)(2,1)} fusion(bf16[496,1024]{1,0:T(8,128)(2,1)S(1)} %multiply_convert_fusion.1, bf16[496,3376]{1,0:T(8,128)(2,1)S(1)} %multiply_convert_fusion.refs_0_.grad_rebuilt), kind=kOutput, calls=%fused_computation | convolution fusion | flops 3432824832 | bytes 11278848 | tf_op jit(solution)/shard_map/dot_general | solution.py:35
  206.5 0.9 reduce_sum.184
  207.6 0.6 convert_reduce_fusion
  208.2 1.3 concatenate.36
  209.6 37.0 %meet.4 = (f32[496,1024]{1,0:T(8,128)S(1)}, f32[256,128]{1,0:T(8,128)S(1)}, bf16[512,3376]{1,0:T(8,128)(2,1)}) custom-call(bf16[496,3376]{1,0:T(8,128)(2,1)S(1)} %multiply_convert_fusion.refs_0_.grad_rebuilt, bf16[1024,3376]{1,0:T(8,128)(2,1)} %get-tuple-element.67.refs_1_, f32[32,128]{1,0:T(8,128)S(1)} %concatenate.37.refs_2_, ...), custom_call_target="tpu_custom_call" | custom-call | flops 1000000 | bytes 90000000 | tf_op jit(solution)/shard_map/meet/pallas_call | solution.py:634
  246.6 0.9 fusion.14
  250.8 2.4 fusion.2
  254.2 35.5 %meet.5 = (f32[496,1024]{1,0:T(8,128)S(1)}, bf16[512,256]{1,0:T(8,128)(2,1)S(1)}, bf16[128,512]{1,0:T(8,128)(2,1)S(1)}, f32[128,3376]{1,0:T(8,128)S(1)}) custom-call(bf16[496,256]{1,0:T(8,128)(2,1)S(1)} %pad_maximum_fusion.refs_0_, bf16[1024,256]{1,0:T(8,128)(2,1)S(1)} %copy-done.24, bf16[1024,256]{1,0:T(8,128)(2,1)S(1)} %convolution_convert_fusion.6.refs_2_.refs_4_, ...), custom_call_target="tpu_custom_call" | custom-call | flops 1000000 | bytes 90000000 | tf_op jit(solution)/shard_map/meet/pallas_call | solution.py:634
  289.8 1.9 fusion.20.refs_0_
  291.7 2.7 convolution_convert_fusion.1.refs_3_.refs_5_
  294.4 2.6 convolution_convert_fusion.2.refs_2_.refs_4_
  297.1 36.5 %meet.6 = (f32[496,1024]{1,0:T(8,128)}, bf16[1024,512]{1,0:T(8,128)(2,1)S(1)}, bf16[512,1024]{1,0:T(8,128)(2,1)S(1)}, f32[128,256]{1,0:T(8,128)S(1)}, f32[128,128]{1,0:T(8,128)S(1)}) custom-call(bf16[496,1024]{1,0:T(8,128)(2,1)S(1)} %fusion.20.refs_0_, bf16[1024,1024]{1,0:T(8,128)(2,1)} %get-tuple-element.82.refs_1_, ...), custom_call_target="tpu_custom_call" | custom-call | flops 1000000 | bytes 90000000 | tf_op jit(solution)/shard_map/meet/pallas_call | solution.py:634
  333.7 3.7 multiply_reduce_fusion
  337.5 4.1 fusion.43
  341.7 1.2 convolution_convert_fusion.5.refs_3_.out
  342.9 0.6 log_add_fusion.log_totals
  343.7 0.9 copy.76.slide_keys
  344.6 1.1 copy-done.7
  345.7 1.0 copy-done.9
  346.8 0.7 copy-done.32
  347.5 0.7 copy-done.33
  348.2 4.7 %attend_back.1.refs_0_ = bf16[496,768]{1,0:T(8,128)(2,1)S(1)} custom-call(bf16[496,1024]{1,0:T(8,128)(2,1)S(1)} %get-tuple-element.173.middle, bf16[256,1024]{1,0:T(8,128)(2,1)S(1)} %copy-done.9, bf16[496,768]{1,0:T(8,128)(2,1)S(1)} %copy-done.7, f32[4,496]{1,0:T(4,128)S(1)} %copy-done.33, s32[496,1]{1,0:T(8,128)S(1)} %copy.76.slide_keys, ...), custom_call_target="tpu_custom_call" | custom-call | tf_op jit(solution)/shard_map/attend_back/pallas_call | solution.py:136
  352.9 2.3 convolution_convert_fusion.3.refs_2_.qkv
  355.3 36.6 %meet.7 = (f32[496,1024]{1,0:T(8,128)}, bf16[512,768]{1,0:T(8,128)(2,1)S(1)}, bf16[256,512]{1,0:T(8,128)(2,1)S(1)}, f32[1024,128]{1,0:T(8,128)S(1)}, f32[128,1024]{1,0:T(8,128)S(1)}) custom-call(bf16[496,768]{1,0:T(8,128)(2,1)S(1)} %attend_back.1.refs_0_, bf16[1024,768]{1,0:T(8,128)(2,1)} %copy-done.14, ...), custom_call_target="tpu_custom_call" | custom-call | flops 1000000 | bytes 90000000 | tf_op jit(solution)/shard_map/meet/pallas_call | solution.py:634
  392.0 3.0 multiply_reduce_fusion.1
  395.3 0.7 copy.78
  396.1 3.8 add_convert_fusion.start
  399.9 48.4 %tail.1 = (f32[3376,128]{1,0:T(8,128)}, f32[128,768]{1,0:T(8,128)}, f32[256,128]{1,0:T(8,128)}, f32[48,128]{1,0:T(8,128)}, bf16[496,3376]{1,0:T(8,128)(2,1)}, /*index=5*/bf16[496,3376]{1,0:T(8,128)(2,1)}) custom-call(bf16[496,1024]{1,0:T(8,128)(2,1)} %add_convert_fusion.start, bf16[992,3376]{1,0:T(8,128)(2,1)} %expression.1, ...), custom_call_target="tpu_custom_call" | custom-call | tf_op jit(solution)/shard_map/tail/pallas_call | solution.py:1149
  448.3 6.0 %assemble.1 = bf16[992,3376]{1,0:T(8,128)(2,1)} custom-call(bf16[496,3376]{1,0:T(8,128)(2,1)} %get-tuple-element.104.own, bf16[496,3376]{1,0:T(8,128)(2,1)} %get-tuple-element.105.other), custom_call_target="tpu_custom_call" | custom-call | tf_op jit(solution)/shard_map/assemble/pallas_call | solution.py:1183
  454.3 0.8 fusion.46
  455.1 0.6 fusion.50
  456.2 0.7 fusion.48
  456.9 1.7 copy.79
  458.6 2.9 copy.95
  461.4 0.7 copy.96
  462.1 0.8 copy.97
  462.9 0.8 copy.98
  463.7 0.6 copy.99
  (188 shorter events, 5.7 us)
Async XLA Ops:
  0.7 81.4 %copy-start = (f32[992,128]{1,0:T(8,128)S(1)}, f32[992,128]{1,0:T(8,128)}, u32[]{:S(2)}) copy-start(f32[992,128]{1,0:T(8,128)} %param.28) | copy-start | bytes 1523716
  4.0 1.2 copy-start.20
  67.0 1.4 copy-start.2
  67.2 2.0 copy-start.15
  67.2 3.1 copy-start.56
  67.6 2.7 copy-start.59
  68.2 2.1 copy-start.49
  68.2 2.1 copy-start.65
  70.3 1.3 copy-start.67
  70.3 1.3 copy-start.73
  71.9 7.7 %copy-start.31 = (s32[496]{0:T(512)}, s32[496]{0:T(512)S(1)}, u32[]{:S(2)}) copy-start(s32[496]{0:T(512)S(1)} %fusion.33) | copy-start | bytes 5956
  73.2 2.0 copy-start.34
  79.7 111.1 %copy-start.37 = (bf16[4,64,496]{2,1,0:T(8,128)(2,1)}, bf16[4,64,496]{2,1,0:T(8,128)(2,1)S(1)}, u32[]{:S(2)}) copy-start(bf16[4,64,496]{2,1,0:T(8,128)(2,1)S(1)} %fusion.22) | copy-start | bytes 761860
  79.7 3.1 copy-start.39
  79.7 4.8 %copy-start.54 = (bf16[128,128]{1,0:T(8,128)(2,1)S(1)}, bf16[128,128]{1,0:T(8,128)(2,1)}, u32[]{:S(2)}) copy-start(bf16[128,128]{1,0:T(8,128)(2,1)} %param.41) | copy-start | bytes 98308
  79.7 4.8 %copy-start.55 = (bf16[128,128]{1,0:T(8,128)(2,1)S(1)}, bf16[128,128]{1,0:T(8,128)(2,1)}, u32[]{:S(2)}) copy-start(bf16[128,128]{1,0:T(8,128)(2,1)} %param.40) | copy-start | bytes 98308
  200.3 9.2 %copy-start.4 = (bf16[496,3376]{1,0:T(8,128)(2,1)}, bf16[496,3376]{1,0:T(8,128)(2,1)S(1)}, u32[]{:S(2)}) copy-start(bf16[496,3376]{1,0:T(8,128)(2,1)S(1)} %multiply_convert_fusion.refs_0_.grad_rebuilt) | copy-start | bytes 10046980
  209.6 37.0 %copy-start.35 = (f32[496,1024]{1,0:T(8,128)S(1)}, f32[496,1024]{1,0:T(8,128)}, u32[]{:S(2)}) copy-start(f32[496,1024]{1,0:T(8,128)} %get-tuple-element.66) | copy-start | bytes 6094852
  246.6 4.2 copy-start.48
  246.6 4.2 copy-start.44
  246.6 4.2 copy-start.47
  247.5 5.7 %copy-start.41 = (bf16[128,1024]{1,0:T(8,128)(2,1)S(1)}, bf16[128,1024]{1,0:T(8,128)(2,1)}, u32[]{:S(2)}) copy-start(bf16[128,1024]{1,0:T(8,128)(2,1)} %get-tuple-element.70) | copy-start | bytes 786436
  247.5 5.7 %copy-start.42 = (f32[496,128]{1,0:T(8,128)S(1)}, f32[496,128]{1,0:T(8,128)}, u32[]{:S(2)}) copy-start(f32[496,128]{1,0:T(8,128)} %get-tuple-element.73) | copy-start | bytes 761860
  247.5 6.1 %copy-start.72 = (bf16[496,1024]{1,0:T(8,128)(2,1)S(1)}, bf16[496,1024]{1,0:T(8,128)(2,1)}, u32[]{:S(2)}) copy-start(bf16[496,1024]{1,0:T(8,128)(2,1)} %get-tuple-element.75) | copy-start | bytes 3047428
  254.2 35.5 %copy-start.68 = (bf16[1024,1024]{1,0:T(8,128)(2,1)S(1)}, bf16[1024,1024]{1,0:T(8,128)(2,1)}, u32[]{:S(2)}) copy-start(bf16[1024,1024]{1,0:T(8,128)(2,1)} %get-tuple-element.80) | copy-start | bytes 6291460
  254.2 35.5 %copy-start.69 = (f32[496,1024]{1,0:T(8,128)S(1)}, f32[496,1024]{1,0:T(8,128)}, u32[]{:S(2)}) copy-start(f32[496,1024]{1,0:T(8,128)} %get-tuple-element.81) | copy-start | bytes 6094852
  289.7 2.0 copy-start.12
  289.7 4.7 %copy-start.10 = (f32[496,1024]{1,0:T(8,128)}, f32[496,1024]{1,0:T(8,128)S(1)}, u32[]{:S(2)}) copy-start(f32[496,1024]{1,0:T(8,128)S(1)} %get-tuple-element.78) | copy-start | bytes 6094852
  289.8 2.0 copy-start.71
  291.7 2.7 copy-start.70
  297.1 36.6 %copy-start.36 = (f32[496,1024]{1,0:T(8,128)S(1)}, f32[496,1024]{1,0:T(8,128)}, u32[]{:S(2)}) copy-start(f32[496,1024]{1,0:T(8,128)} %get-tuple-element.88) | copy-start | bytes 6094852
  333.6 3.7 copy-start.16
  333.6 3.7 copy-start.18
  333.6 3.7 copy-start.26
  333.6 3.7 copy-start.29
  333.7 3.7 copy-start.43
  333.7 3.8 copy-start.11
  337.5 4.1 copy-start.38
  343.5 9.4 %copy-start.3 = (f32[496,1024]{1,0:T(8,128)S(1)}, f32[496,1024]{1,0:T(8,128)}, u32[]{:S(2)}) copy-start(f32[496,1024]{1,0:T(8,128)} %copy-done.2) | copy-start | bytes 6094852
  348.2 4.7 %copy-start.50 = (f32[1024]{0:T(1024)S(1)}, f32[1024]{0:T(1024)}, u32[]{:S(2)}) copy-start(f32[1024]{0:T(1024)} %copy-done.49) | copy-start | bytes 12292
  348.2 4.7 %copy-start.57 = (f32[496]{0:T(512)S(1)}, f32[496]{0:T(512)}, u32[]{:S(2)}) copy-start(f32[496]{0:T(512)} %copy-done.56) | copy-start | bytes 5956
  348.2 4.7 %copy-start.60 = (f32[496]{0:T(512)S(1)}, f32[496]{0:T(512)}, u32[]{:S(2)}) copy-start(f32[496]{0:T(512)} %copy-done.59) | copy-start | bytes 5956
  348.2 4.7 %copy-start.66 = (f32[1024]{0:T(1024)S(1)}, f32[1024]{0:T(1024)}, u32[]{:S(2)}) copy-start(f32[1024]{0:T(1024)} %copy-done.65) | copy-start | bytes 12292
  352.9 2.4 copy-start.5
  352.9 2.4 copy-start.17
  352.9 2.4 copy-start.19
  391.9 3.1 copy-start.21
  391.9 3.1 copy-start.22
  391.9 3.1 copy-start.25
  391.9 3.1 copy-start.62
  391.9 3.1 copy-start.63
  392.0 3.1 copy-start.53
  392.0 3.2 copy-start.52
  392.0 4.1 copy-start.51
  392.0 4.1 copy-start.58
  392.0 4.0 copy-start.61
  448.3 6.0 %copy-start.40 = (f32[128,768]{1,0:T(8,128)S(1)}, f32[128,768]{1,0:T(8,128)}, u32[]{:S(2)}) copy-start(f32[128,768]{1,0:T(8,128)} %get-tuple-element.97) | copy-start | bytes 1179652
  448.3 6.8 %copy-start.64 = (f32[48,128]{1,0:T(8,128)S(1)}, f32[48,128]{1,0:T(8,128)}, u32[]{:S(2)}) copy-start(f32[48,128]{1,0:T(8,128)} %get-tuple-element.96) | copy-start | bytes 73732
  448.3 7.9 %copy-start.27 = (f32[128,256]{1,0:T(8,128)S(1)}, f32[128,256]{1,0:T(8,128)}, u32[]{:S(2)}) copy-start(f32[128,256]{1,0:T(8,128)} %copy-done.26) | copy-start | bytes 393220
  448.3 8.6 %copy-start.13 = (f32[128,3376]{1,0:T(8,128)S(1)}, f32[128,3376]{1,0:T(8,128)}, u32[]{:S(2)}) copy-start(f32[128,3376]{1,0:T(8,128)} %copy-done.12) | copy-start | bytes 5185540
  458.6 2.9 copy-start.45
  458.6 3.5 copy-start.23
  458.6 5.7 %copy-start.1 = (f32[992,128]{1,0:T(8,128)S(1)}, f32[992,128]{1,0:T(8,128)}, u32[]{:S(2)}) copy-start(f32[992,128]{1,0:T(8,128)} %param.28) | copy-start | bytes 1523716
  461.4 2.2 copy-start.30
  (10 other events, 9.2 us)

commit v4 on v3

--- a/solution.py
+++ b/solution.py
@@ -81,33 +81,115 @@
     return jnp.sum((index[:, None] >= bounds[None, :]).astype(jnp.int32), axis=1)
 
 
-def allowed_pairs(slide, alive):
-    index = jnp.arange(alive.shape[0], dtype=jnp.int32)
-    return (slide[:, None] == slide[None, :]) & (
-        (alive[None, :] == 1) | (index[:, None] == index[None, :])
-    )
-
-
-def heads_of(array):
-    return array.reshape(array.shape[0], -1, HEAD)
-
-
-def attend(queries, keys, values, allowed):
+def attend_kernel(start, gain, bias, weights, slide_keys, slide_queries, alive_keys, *outs):
+    normed_out, scale_out, low_out, projected_out, attended_out, totals_out = outs
+    cells, width = attended_out.shape
     factor = HEAD ** (-0.5)
-    scores = (
-        jnp.einsum("qhd,khd->hqk", heads_of(queries), heads_of(keys), preferred_element_type=F32)
-        * factor
-    )
-    scores = jnp.where(allowed[None], scores, NEG_LARGE)
-    largest = jnp.max(scores, axis=2, keepdims=True)
-    exponents = jnp.exp(scores - largest)
-    sums = jnp.sum(exponents, axis=2, keepdims=True)
-    probs = (exponents / sums).astype(BF16)
-    out = jnp.einsum("hqk,khd->qhd", probs, heads_of(values), preferred_element_type=F32)
-    return out.reshape(queries.shape).astype(BF16), largest + jnp.log(sums)
-
-
-def attend_back_kernel(middle, out_w, projected, log_totals, slide_keys, slide_queries, alive_keys, out):
+    normed, scale = normalize(start[...])
+    normed_out[...] = normed
+    scale_out[...] = scale
+    low = (normed * gain[...] + bias[...]).astype(BF16)
+    low_out[...] = low
+    projected = mat_nn(low, weights[...]).astype(BF16)
+    projected_out[...] = projected
+    shape = (cells, cells)
+    own_key = lax.broadcasted_iota(jnp.int32, shape, 0) == lax.broadcasted_iota(jnp.int32, shape, 1)
+    allowed = (slide_keys[...] == slide_queries[...]) & ((alive_keys[...] == 1) | own_key)
+    for head_index in range(width // HEAD):
+        first = head_index * HEAD
+        q = projected[:, first : first + HEAD]
+        k = projected[:, width + first : width + first + HEAD]
+        v = projected[:, 2 * width + first : 2 * width + first + HEAD]
+        scores = jnp.where(allowed, mat_nt(k, q) * factor, NEG_LARGE)
+        largest = jnp.max(scores, axis=0, keepdims=True)
+        exponents = jnp.exp(scores - largest)
+        sums = jnp.sum(exponents, axis=0, keepdims=True)
+        probs = (exponents / sums).astype(BF16)
+        attended_out[:, first : first + HEAD] = mat_tn(probs, v).astype(BF16)
+        totals_out[head_index : head_index + 1, :] = largest + jnp.log(sums)
+
+
+def attend(start, gain, bias, weights, slide, alive):
+    cells, features = start.shape
+    width = weights.shape[1] // 3
+    return pl.pallas_call(
+        attend_kernel,
+        out_shape=[
+            jax.ShapeDtypeStruct((cells, features), F32),
+            jax.ShapeDtypeStruct((cells, 1), F32),
+            jax.ShapeDtypeStruct((cells, features), BF16),
+            jax.ShapeDtypeStruct((cells, 3 * width), BF16),
+            jax.ShapeDtypeStruct((cells, width), BF16),
+            jax.ShapeDtypeStruct((width // HEAD, cells), F32),
+        ],
+        compiler_params=pltpu.CompilerParams(vmem_limit_bytes=48 * 2**20),
+        name="attend",
+    )(start, gain, bias, weights, slide[:, None], slide[None, :], alive[:, None])
+
+
+def decode_kernel(section, pre, weights, cells, alive, residual, grad, act, act_turned):
+    @pl.when(pl.program_id(0) == 0)
+    def _():
+        value = gelu(pre[...]).astype(BF16)
+        act[...] = value
+        act_turned[...] = value.T
+
+    rebuilt = mat_nn(act[...], weights[...])
+    difference = ((rebuilt - cells[...].astype(F32)) * alive[...]).astype(BF16)
+    residual[...] = difference
+    grad[...] = mat_nn(act_turned[...], difference).astype(BF16)
+
+
+def decode(micro, pre, weights, expression, alive):
+    rows, features = pre.shape
+    genes = weights.shape[1]
+    block = 512
+    return pl.pallas_call(
+        decode_kernel,
+        grid_spec=pltpu.PrefetchScalarGridSpec(
+            num_scalar_prefetch=1,
+            grid=(pl.cdiv(genes, block),),
+            in_specs=[
+                pl.BlockSpec((rows, features), lambda step, section: (0, 0)),
+                pl.BlockSpec((features, block), lambda step, section: (0, step)),
+                pl.BlockSpec((rows, block), lambda step, section: (section[0], step)),
+                pl.BlockSpec((rows, 1), lambda step, section: (0, 0)),
+            ],
+            out_specs=[
+                pl.BlockSpec((rows, block), lambda step, section: (0, step)),
+                pl.BlockSpec((features, block), lambda step, section: (0, step)),
+            ],
+            scratch_shapes=[pltpu.VMEM((rows, features), BF16), pltpu.VMEM((features, rows), BF16)],
+        ),
+        out_shape=[
+            jax.ShapeDtypeStruct((rows, genes), BF16),
+            jax.ShapeDtypeStruct((features, genes), BF16),
+        ],
+        compiler_params=pltpu.CompilerParams(vmem_limit_bytes=48 * 2**20),
+        name="decode",
+    )(micro.astype(jnp.int32).reshape(1), pre, weights, expression, alive[:, None])
+
+
+def attend_back_kernel(plan, middle, out_w, projected, log_totals, slide_keys, slide_queries, alive_keys, *refs):
+    swapped, out, received = refs[: len(plan)], refs[len(plan)], refs[len(plan) + 1 : 2 * len(plan) + 1]
+    sent, got = refs[2 * len(plan) + 1 :]
+    section = lax.axis_index("section")
+    partner = {"section": 1 - section}
+    barrier = pltpu.get_barrier_semaphore()
+    pl.semaphore_signal(barrier, inc=1, device_id=partner)
+    pl.semaphore_wait(barrier, 1)
+    copies = [
+        pltpu.make_async_remote_copy(
+            src_ref=part_of(src, axis, 1 - section, size),
+            dst_ref=dst,
+            send_sem=sent.at[item],
+            recv_sem=got.at[item],
+            device_id=partner,
+        )
+        for item, (src, dst, (axis, size)) in enumerate(zip(swapped, received, plan))
+    ]
+    for copy in copies:
+        copy.start()
     cells, width = out.shape[0], out.shape[1] // 3
     factor = HEAD ** (-0.5)
     shape = (cells, cells)
@@ -130,23 +212,40 @@
         out[:, 2 * width + first : 2 * width + first + HEAD] = mat_nn(
             probs.astype(BF16), g
         ).astype(BF16)
-
-
-def attend_back(middle, out_w, projected, log_totals, slide, alive):
-    return pl.pallas_call(
-        attend_back_kernel,
-        out_shape=jax.ShapeDtypeStruct(projected.shape, BF16),
-        compiler_params=pltpu.CompilerParams(vmem_limit_bytes=48 * 2**20),
+    for copy in copies:
+        copy.wait()
+
+
+def attend_back(number, middle, out_w, projected, log_totals, slide, alive, swaps):
+    plan = tuple((axis, array.shape[axis] // 2) for array, axis in swaps)
+    halves = [
+        array.shape[:axis] + (array.shape[axis] // 2,) + array.shape[axis + 1 :]
+        for array, axis in swaps
+    ]
+    vmem, anywhere = pl.BlockSpec(memory_space=pltpu.VMEM), pl.BlockSpec(memory_space=pl.ANY)
+    count = len(swaps)
+    results = pl.pallas_call(
+        functools.partial(attend_back_kernel, plan),
+        out_shape=[jax.ShapeDtypeStruct(projected.shape, BF16)]
+        + [jax.ShapeDtypeStruct(half, BF16) for half in halves],
+        in_specs=[vmem] * 7 + [anywhere] * count,
+        out_specs=[vmem] + [anywhere] * count,
+        scratch_shapes=[pltpu.SemaphoreType.DMA((max(count, 1),))] * 2,
+        compiler_params=pltpu.CompilerParams(
+            collective_id=number, has_side_effects=True, vmem_limit_bytes=48 * 2**20
+        ),
         name="attend_back",
     )(
         middle,
         out_w,
         projected,
-        log_totals[:, :, 0],
+        log_totals,
         slide[:, None],
         slide[None, :],
         alive[:, None],
+        *[array for array, _ in swaps],
     )
+    return results[0], results[1:]
 
 
 def part_of(ref, axis, index, size):
@@ -1202,21 +1301,28 @@
         column = lax.rem(slot, spacing) * 128
         return (lax.rem(lax.div(slot, spacing), 2), slice(None), pl.ds(pl.multiple_of(column, 128), 128))
 
+    rooms = from_left.shape[0]
+
+    def room_of(slot):
+        return lax.rem(slot, rooms)
+
     def rightward(slot):
+        room = room_of(slot)
         return pltpu.make_async_remote_copy(
-            src_ref=to_right.at[slot],
-            dst_ref=from_left.at[slot],
-            send_sem=sent_right.at[slot],
-            recv_sem=got_left.at[slot],
+            src_ref=to_right.at[room],
+            dst_ref=from_left.at[room],
+            send_sem=sent_right.at[room],
+            recv_sem=got_left.at[room],
             device_id={"mp": me + 1},
         )
 
     def leftward(slot):
+        room = room_of(slot)
         return pltpu.make_async_remote_copy(
-            src_ref=to_left.at[slot],
-            dst_ref=from_right.at[slot],
-            send_sem=sent_left.at[slot],
-            recv_sem=got_right.at[slot],
+            src_ref=to_left.at[room],
+            dst_ref=from_right.at[room],
+            send_sem=sent_left.at[room],
+            recv_sem=got_right.at[room],
             device_id={"mp": me - 1},
         )
 
@@ -1226,17 +1332,23 @@
     def flow(slot, copy, has_source, has_target, source, target):
         @pl.when(used(slot))
         def _():
+            room = room_of(slot)
+
             @pl.when(has_source)
             def _():
                 copy(slot).wait_recv()
 
+            @pl.when(has_target & (slot >= rooms))
+            def _():
+                copy(slot).wait_send()
+
             @pl.when(has_target & has_source)
             def _():
-                target[slot] = (part[place(slot)] + source[slot].astype(F32)).astype(BF16)
+                target[room] = (part[place(slot)] + source[room].astype(F32)).astype(BF16)
 
             @pl.when(has_target & jnp.logical_not(has_source))
             def _():
-                target[slot] = part[place(slot)].astype(BF16)
+                target[room] = part[place(slot)].astype(BF16)
 
             @pl.when(has_target)
             def _():
@@ -1255,19 +1367,21 @@
         )
         done = moment - trail
 
+        room = room_of(done)
+
         @pl.when(used(done) & has_left & has_right)
         def _():
             total[place(done)] = (
-                part[place(done)] + from_left[done].astype(F32) + from_right[done].astype(F32)
+                part[place(done)] + from_left[room].astype(F32) + from_right[room].astype(F32)
             )
 
         @pl.when(used(done) & jnp.logical_not(has_left))
         def _():
-            total[place(done)] = part[place(done)] + from_right[done].astype(F32)
+            total[place(done)] = part[place(done)] + from_right[room].astype(F32)
 
         @pl.when(used(done) & jnp.logical_not(has_right))
         def _():
-            total[place(done)] = part[place(done)] + from_left[done].astype(F32)
+            total[place(done)] = part[place(done)] + from_left[room].astype(F32)
 
         return carry
 
@@ -1284,7 +1398,7 @@
 
         return carry
 
-    lax.fori_loop(0, items * spacing, finish, 0)
+    lax.fori_loop(items * spacing - rooms, items * spacing, finish, 0)
 
 
 def pipe_spacing(pieces, count):
@@ -1493,7 +1607,6 @@
     total_parts = sections * count_dp
     pieces = features // 128
     spacing = pipe_spacing(pieces, count_z)
-    slots = 6 * spacing
     half_rows = 256
     plan = tuple((axis, shard.shape[axis]) for shard, axis in gathers)
     shapes = [
@@ -1516,7 +1629,8 @@
         ((cells, features), F32),
         ((count_z, 24, 2 * half_rows), F32),
     ] + [(shape, BF16) for shape in shapes]
-    buffer = pltpu.VMEM((slots, half_rows, 128), BF16)
+    rooms = 2 * spacing
+    buffer = pltpu.VMEM((rooms, half_rows, 128), BF16)
     copies = 11 * len(gathers) + count_z - 1
     halves = pltpu.VMEM((2, half_rows, features), F32)
     results = pl.pallas_call(
@@ -1528,7 +1642,7 @@
         + [pltpu.VMEM(shape, BF16) for shape in shapes[:-1]]
         + [pltpu.VMEM(shard.shape, BF16) for shard, _ in gathers]
         + [buffer] * 4
-        + [pltpu.SemaphoreType.DMA((slots,))] * 4
+        + [pltpu.SemaphoreType.DMA((rooms,))] * 4
         + [
             pltpu.SemaphoreType.DMA((copies,)),
             pltpu.SemaphoreType.DMA((copies,)),
@@ -1540,6 +1654,254 @@
         name="middle",
     )(attended, start, gain, bias, out_w, noise, centers, spreads, *[shard for shard, _ in gathers])
     return results[:12], results[12:]
+
+
+def back_kernel(
+    spacing, latent_total, ramp_step, counts, grad_rebuilt, decoder_pre, latent, spread_latent, respons, alive, centers,
+    spreads, upper, normed, scale, gain, genes_w, dec_w, latent_w, down_w, up_w, grad_genes,
+    pre_out, stats_out, weighted_out, hidden_out, upper_out, middle_out, low_out, sums_out,
+    genes_sum, genes_other, part, total, hidden_rows, counts_all, kl_scale, genes_in, dec_in, latent_in, down_in,
+    up_in, mine, theirs, from_x, from_y, inbound, *refs
+):
+    line, (sent, got, local_sem) = refs[:8], refs[8:]
+    section, z, dp = (lax.axis_index(name) for name in ("section", "mp", "dp"))
+    count_z, count_dp = lax.axis_size("mp"), lax.axis_size("dp")
+    row, col = dp // 2, dp % 2
+    peer_x, peer_y = row * 2 + (1 - col), (1 - row) * 2 + col
+    peers = (peer_x, peer_y, (1 - row) * 2 + (1 - col))
+    partner, to_x, to_y = {"section": 1 - section}, {"dp": peer_x}, {"dp": peer_y}
+    cells = upper.shape[0]
+    half_rows = part.shape[1]
+    comp_count = centers.shape[0]
+
+    barrier = pltpu.get_barrier_semaphore()
+    for device in (partner, to_x, to_y):
+        pl.semaphore_signal(barrier, inc=1, device_id=device)
+    for exists, neighbour in ((z > 0, z - 1), (z < count_z - 1, z + 1)):
+
+        @pl.when(exists)
+        def _(neighbour=neighbour):
+            pl.semaphore_signal(barrier, inc=1, device_id={"mp": neighbour})
+
+    at_end = (z == 0) | (z == count_z - 1)
+
+    @pl.when(at_end)
+    def _():
+        pl.semaphore_wait(barrier, 4)
+
+    @pl.when(jnp.logical_not(at_end))
+    def _():
+        pl.semaphore_wait(barrier, 5)
+
+    used = [0, 0]
+
+    def remote(src, dst, device):
+        index = used[0]
+        used[0] += 1
+        return pltpu.make_async_remote_copy(
+            src_ref=src, dst_ref=dst, send_sem=sent.at[index], recv_sem=got.at[index], device_id=device
+        )
+
+    def within(src, dst):
+        index = used[1]
+        used[1] += 1
+        return pltpu.make_async_copy(src, dst, local_sem.at[index])
+
+    count_rows = counts.shape[0]
+    around = (section, dp, peers, partner, to_x, to_y)
+    counting = spread(remote, counts, counts_all, 0, count_rows, *around)
+    count_steps = spread_steps(counting)
+    size = from_x.shape[0]
+    swap = remote(part_of(grad_genes, 0, 1 - section, size * count_dp), genes_other, partner)
+    indices = (peers[2], peer_x, peer_y, dp)
+    load_mine = [
+        within(block_of(grad_genes, 0, section * count_dp + index, size), mine.at[index])
+        for index in range(count_dp)
+    ]
+    load_theirs = [
+        within(block_of(genes_other, 0, index, size), theirs.at[index]) for index in range(count_dp)
+    ]
+    first, second, pass_on, conclude_genes = trade(
+        remote, mine, indices, from_x, from_y, inbound, to_x, to_y
+    )
+    load_genes = within(genes_w, genes_in)
+    fetches = [
+        within(src, dst)
+        for src, dst in ((dec_w, dec_in), (latent_w, latent_in), (down_w, down_in), (up_w, up_in))
+    ]
+
+    load_genes.start()
+    counts_all[pl.ds(pl.multiple_of((section * count_dp + dp) * count_rows, 8), count_rows), :] = (
+        counts[...]
+    )
+
+    def begin():
+        count_steps[0]()
+        swap.start()
+        for copy in fetches + load_mine:
+            copy.start()
+        load_genes.wait()
+
+    def count_cells():
+        for name in ("own", "relay_x", "relay_y", "relay_upper", "relay_lower"):
+            counting[name].wait_recv()
+        for copy in fetches:
+            copy.wait()
+        sums = sum(
+            counts_all[index * count_rows : index * count_rows + 8, :]
+            for index in range(counts_all.shape[0] // count_rows)
+        )
+        mean_kl = sums[0:1, :] / (latent_total * sums[1:2, :])
+        excess = mean_kl - FREE_BITS
+        small = jnp.exp(-jnp.abs(excess))
+        above = 1.0 + small
+        log_above = jnp.where(above == 1.0, small, jnp.log(above) * (small / (above - 1.0)))
+        softplus = jnp.maximum(excess, 0.0) + log_above
+        sigmoid = jnp.where(excess >= 0.0, 1.0, small) / above
+        kl_scale[0:1, :] = ramp_step[0:1, :] * softplus * sigmoid
+
+    def open_theirs():
+        swap.wait_recv()
+        for copy in load_theirs:
+            copy.start()
+
+    def trade_begins():
+        for copy in load_mine + load_theirs:
+            copy.wait()
+        mine[...] = (mine[...].astype(F32) + theirs[...].astype(F32)).astype(BF16)
+        for copy in first + second:
+            copy.start()
+
+    def rows_of(half):
+        return pl.ds(pl.multiple_of(half * (cells - half_rows), 16), half_rows)
+
+    def genes_product(half):
+        part[half] = mat_nt(grad_rebuilt[rows_of(half), :], genes_in[...])
+
+    def latents_back(half):
+        rows = rows_of(half)
+        pre = (total[half] * gelu_slope(decoder_pre[rows, :])).astype(BF16)
+        pre_out[rows, :] = pre
+        weight = kl_scale[0:1, 0:1] * alive[rows, :]
+        weighted = respons[rows, :] * weight
+        weighted_out[rows, :] = weighted
+        own_latent = latent[rows, :]
+        grad_latent = mat_nt(pre, dec_in[...])
+        for index in range(comp_count):
+            pulled = (own_latent - centers[index : index + 1, :]) * jnp.exp(
+                -spreads[index : index + 1, :]
+            )
+            grad_latent = grad_latent + weighted[:, index : index + 1] * pulled
+        grad_logs = grad_latent * (0.5 * spread_latent[rows, :]) - 0.5 * weight
+        stats = jnp.concatenate([grad_latent.astype(BF16), grad_logs.astype(BF16)], axis=1)
+        stats_out[rows, :] = stats
+        part[half] = mat_nt(stats, latent_in[...])
+
+    def feed_back(half):
+        rows = rows_of(half)
+        hidden = total[half].astype(BF16)
+        hidden_rows[half] = hidden
+        hidden_out[rows, :] = hidden
+        grad_upper = (mat_nt(hidden, down_in[...]) * gelu_slope(upper[rows, :])).astype(BF16)
+        upper_out[rows, :] = grad_upper
+        part[half] = mat_nt(grad_upper, up_in[...])
+
+    def conclude(half):
+        rows = rows_of(half)
+        grad_norm, own_normed = total[half], normed[rows, :]
+        grad_middle = hidden_rows[half].astype(F32) + norm_back(
+            grad_norm, own_normed, scale[rows, :], gain[...]
+        )
+        middle_out[rows, :] = grad_middle
+        low_out[rows, :] = grad_middle.astype(BF16)
+        return grad_norm * own_normed, grad_norm
+
+    def conclude_first(half):
+        scaled, plain = conclude(half)
+        sums_out[0:1, :] = jnp.sum(scaled, axis=0, keepdims=True)
+        sums_out[1:2, :] = jnp.sum(plain, axis=0, keepdims=True)
+
+    def produce(moment):
+        item = lax.div(moment, spacing)
+        half, stage = lax.rem(item, 2), lax.div(item, 2)
+        begins = lax.rem(moment, spacing) == 0
+        for number, work in enumerate((genes_product, latents_back, feed_back, conclude_first)):
+            pl.when(begins & (stage == number))(functools.partial(work, half))
+
+    hooks = [
+        (0, begin),
+        (4, count_steps[1]),
+        (6, count_steps[2]),
+        (8, count_steps[3]),
+        (10, open_theirs),
+        (13, trade_begins),
+        (2 * spacing, count_cells),
+        (2 * spacing + 6, pass_on),
+    ]
+    line_pipe(produce, hooks, 6, spacing, part, total, *line)
+    scaled, plain = conclude(1)
+    repeated = 2 * half_rows - cells
+    sums_out[0:1, :] += jnp.sum(scaled[repeated:, :], axis=0, keepdims=True)
+    sums_out[1:2, :] += jnp.sum(plain[repeated:, :], axis=0, keepdims=True)
+    genes_sum[...] = conclude_genes()
+    for copy in counting.values():
+        copy.wait_send()
+    swap.wait_send()
+
+
+def back(number, latent_total, ramp, counts, grad_rebuilt, decoder_pre, latent, spread_latent, respons, alive, centers,
+         spreads, upper, normed, scale, gain, genes_w, dec_w, latent_w, down_w, up_w, grad_genes):
+    sections, count_dp, count_z = (lax.axis_size(name) for name in ("section", "dp", "mp"))
+    cells, features = decoder_pre.shape
+    units, latents = upper.shape[1], latent.shape[1]
+    spacing = pipe_spacing(features // 128, count_z)
+    rooms, half_rows = 2 * spacing, 256
+    vmem, anywhere = pl.BlockSpec(memory_space=pltpu.VMEM), pl.BlockSpec(memory_space=pl.ANY)
+    piece = (grad_genes.shape[0] // (sections * count_dp), grad_genes.shape[1])
+    roles, one = pltpu.VMEM((count_dp,) + piece, BF16), pltpu.VMEM(piece, BF16)
+    buffer = pltpu.VMEM((rooms, half_rows, 128), BF16)
+    halves = pltpu.VMEM((2, half_rows, features), F32)
+    outputs = [
+        ((cells, features), BF16),
+        ((cells, 2 * latents), BF16),
+        (respons.shape, F32),
+        ((cells, features), BF16),
+        ((cells, units), BF16),
+        ((cells, features), F32),
+        ((cells, features), BF16),
+        ((8, features), F32),
+        (piece, F32),
+        ((piece[0] * count_dp, piece[1]), BF16),
+    ]
+    copies = 11 + 1 + 6
+    results = pl.pallas_call(
+        functools.partial(back_kernel, spacing, float(latent_total)),
+        out_shape=[jax.ShapeDtypeStruct(*item) for item in outputs],
+        in_specs=[vmem] * 14 + [anywhere] * 6,
+        out_specs=[vmem] * 9 + [anywhere],
+        scratch_shapes=[
+            halves,
+            halves,
+            pltpu.VMEM((2, half_rows, features), BF16),
+            pltpu.VMEM((sections * count_dp * counts.shape[0], 128), F32),
+            pltpu.VMEM((8, 128), F32),
+        ]
+        + [pltpu.VMEM(array.shape, BF16) for array in (genes_w, dec_w, latent_w, down_w, up_w)]
+        + [roles, roles, one, one, one]
+        + [buffer] * 4
+        + [pltpu.SemaphoreType.DMA((rooms,))] * 4
+        + [
+            pltpu.SemaphoreType.DMA((copies,)),
+            pltpu.SemaphoreType.DMA((copies,)),
+            pltpu.SemaphoreType.DMA((2 * count_dp + 5,)),
+        ],
+        compiler_params=pltpu.CompilerParams(
+            collective_id=number, has_side_effects=True, vmem_limit_bytes=62 * 2**20
+        ),
+        name="back",
+    )(ramp, counts, grad_rebuilt, decoder_pre, latent, spread_latent, respons, alive, centers, spreads, upper,
+      normed, scale, gain, genes_w, dec_w, latent_w, down_w, up_w, grad_genes)
+    return results[:9]
 
 
 def meet(tiled, number, reduce=None, gathers=(), swaps=(), exchanges=(), shares=(), pairs=()):
@@ -1617,12 +1979,10 @@
     def own(array, axis=0):
         return lax.dynamic_slice_in_dim(array, micro * cells, cells, axis)
 
-    genes_in = own(expression)
     alive = own(live_mask)
     alive_float = alive.astype(F32)
     noise = own(latent_noise)
     slide = slide_ids(lax.dynamic_index_in_dim(lengths, micro, 0, False), cells)
-    allowed = allowed_pairs(slide, alive)
 
     norm_block = jnp.pad(jnp.stack([ln1_gain, ln1_bias, ln2_gain, ln2_bias]), ((0, 12), (0, 0)))
     comp_block = jnp.pad(
@@ -1649,11 +2009,9 @@
     comps = small_all[:, 16:, :comp_width].transpose(1, 0, 2).reshape(2 * comp_count, -1)
     centers, spreads = comps[:comp_count], comps[comp_count:]
 
-    normed_one, scale_one = normalize(start)
-    first_low = (normed_one * gain_one + bias_one).astype(BF16)
-    projected = mat_nn(first_low, qkv).astype(BF16)
-    queries, keys, values = jnp.split(projected, 3, axis=1)
-    attended, log_totals = attend(queries, keys, values, allowed)
+    normed_one, scale_one, first_low, projected, attended, log_totals = attend(
+        start, gain_one, bias_one, qkv, slide, alive
+    )
     latent_shard = jnp.concatenate([w_mean, w_logvar], axis=1)
     precision = jnp.exp(-spreads)
     if tiled:
@@ -1712,30 +2070,86 @@
     log_prior = largest[0] + jnp.log(jnp.sum(jnp.exp(logits - largest), axis=0))
     respons = jnp.exp(logits - log_prior[None, :])
     divergence = jnp.sum((log_post - log_prior) * alive_float)
-    decoder_act = lax.optimization_barrier(gelu(decoder_pre).astype(BF16))
-    residual = (mat_nn(decoder_act, genes_w) - genes_in.astype(F32)) * alive_float[:, None]
-    grad_rebuilt = residual.astype(BF16)
-
-    grad_genes = mat_tn(decoder_act, grad_rebuilt).astype(BF16)
+    grad_rebuilt, grad_genes = decode(micro, decoder_pre, genes_w, expression, alive_float)
+
     counts = jnp.concatenate(
         [jnp.full((1, 128), divergence), jnp.full((31, 128), jnp.sum(alive_float))], axis=0
     )
-    (grad_act,), (count_parts,), (genes_other,), _, _, _ = meeting(
-        5, (grad_rebuilt, genes_w, True, False), gathers=((counts, 0),), swaps=((grad_genes, 0),)
-    )
-    count_parts = jnp.sum(count_parts.reshape(shards, 32, 128)[:, :, 0], axis=0)
-    mean_kl = count_parts[0] / (LATENT * count_parts[1])
     ramp_weight = jnp.minimum(1.0, (ramp_step[0] + 1).astype(F32) / RAMP)
-    kl_scale = (
-        ramp_weight * jax.nn.softplus(mean_kl - FREE_BITS) * jax.nn.sigmoid(mean_kl - FREE_BITS)
-    )
-    grad_pre = (grad_act * gelu_slope(decoder_pre)).astype(BF16)
-    grad_dec = mat_tn(latent_low, grad_pre).astype(BF16)
-    cell_weight = kl_scale * alive_float
     offsets = latent[None] - centers[:, None, :]
     pulled = offsets * precision[:, None, :]
-    weighted = (respons * cell_weight[None, :])[:, :, None]
-    grad_latent = mat_nt(grad_pre, dec_w) + jnp.sum(weighted * pulled, axis=0)
+    if tiled:
+        (grad_pre, grad_stats, weighted, grad_hidden, grad_upper, grad_middle, middle_low, norm_sums,
+         genes_parts) = back(
+            2,
+            LATENT,
+            jnp.full((8, 128), ramp_weight),
+            counts,
+            grad_rebuilt,
+            decoder_pre,
+            latent,
+            spread_latent,
+            jnp.pad(respons.T, ((0, 0), (0, 128 - comp_count))),
+            alive_float[:, None],
+            centers,
+            spreads,
+            upper,
+            normed_two,
+            scale_two,
+            gain_two,
+            genes_w,
+            dec_w,
+            latent_w,
+            down_w,
+            up_w,
+            grad_genes,
+        )
+        weighted = weighted[:, :comp_count].T[:, :, None]
+        grad_dec = mat_tn(latent_low, grad_pre).astype(BF16)
+        grad_latent_w = mat_tn(hidden, grad_stats).astype(BF16)
+        grad_down = mat_tn(activated, grad_hidden).astype(BF16)
+        grad_up = mat_tn(second_low, grad_upper).astype(BF16)
+    else:
+        (grad_act,), (count_parts,), (genes_other,), _, _, _ = meeting(
+            5, (grad_rebuilt, genes_w, True, False), gathers=((counts, 0),), swaps=((grad_genes, 0),)
+        )
+        count_parts = jnp.sum(count_parts.reshape(shards, 32, 128)[:, :, 0], axis=0)
+        mean_kl = count_parts[0] / (LATENT * count_parts[1])
+        kl_scale = (
+            ramp_weight * jax.nn.softplus(mean_kl - FREE_BITS) * jax.nn.sigmoid(mean_kl - FREE_BITS)
+        )
+        grad_pre = (grad_act * gelu_slope(decoder_pre)).astype(BF16)
+        grad_dec = mat_tn(latent_low, grad_pre).astype(BF16)
+        cell_weight = kl_scale * alive_float
+        weighted = (respons * cell_weight[None, :])[:, :, None]
+        grad_latent = mat_nt(grad_pre, dec_w) + jnp.sum(weighted * pulled, axis=0)
+        grad_means = grad_latent.astype(BF16)
+        grad_logs = (grad_latent * (0.5 * spread_latent) - 0.5 * cell_weight[:, None]).astype(BF16)
+        grad_stats = jnp.concatenate([grad_means, grad_logs], axis=1)
+        grad_latent_w = mat_tn(hidden, grad_stats).astype(BF16)
+        (summed,), _, (latent_other, dec_other), (genes_parts,), _, _ = meeting(
+            6,
+            (grad_stats, latent_w, True, False),
+            swaps=((grad_latent_w, 0), (grad_dec, 1)),
+            exchanges=((grad_genes, genes_other, 0),),
+        )
+        grad_hidden = summed.astype(BF16)
+
+        grad_down = mat_tn(activated, grad_hidden).astype(BF16)
+        grad_upper = (mat_nt(grad_hidden, down_w) * gelu_slope(upper)).astype(BF16)
+        grad_up = mat_tn(second_low, grad_upper).astype(BF16)
+        (grad_norm_two,), _, (down_other, up_other), _, _, _ = (
+            meeting(
+                7,
+                (grad_upper, up_w, True, False),
+                swaps=((grad_down, 1), (grad_up, 0)),
+            )
+        )
+        grad_middle = grad_hidden.astype(F32) + norm_back(
+            grad_norm_two, normed_two, scale_two, gain_two
+        )
+        middle_low = grad_middle.astype(BF16)
+        norm_sums = [jnp.sum(grad_norm_two * normed_two, axis=0), jnp.sum(grad_norm_two, axis=0)]
     grad_comps = jnp.concatenate(
         [
             -jnp.sum(weighted * pulled, axis=1),
@@ -1743,44 +2157,33 @@
         ],
         axis=0,
     )
-    grad_means = grad_latent.astype(BF16)
-    grad_logs = (grad_latent * (0.5 * spread_latent) - 0.5 * cell_weight[:, None]).astype(BF16)
-    grad_stats = jnp.concatenate([grad_means, grad_logs], axis=1)
-    grad_latent_w = mat_tn(hidden, grad_stats).astype(BF16)
-    (summed,), _, (latent_other, dec_other), (genes_parts,), _, _ = meeting(
-        6,
-        (grad_stats, latent_w, True, False),
-        swaps=((grad_latent_w, 0), (grad_dec, 1)),
-        exchanges=((grad_genes, genes_other, 0),),
-    )
-    grad_hidden = summed.astype(BF16)
-
-    grad_down = mat_tn(activated, grad_hidden).astype(BF16)
-    grad_upper = (mat_nt(grad_hidden, down_w) * gelu_slope(upper)).astype(BF16)
-    grad_up = mat_tn(second_low, grad_upper).astype(BF16)
-    (grad_norm_two,), _, (down_other, up_other), (latent_parts, dec_parts), _, _ = (
-        meeting(
-            7,
-            (grad_upper, up_w, True, False),
-            swaps=((grad_down, 1), (grad_up, 0)),
-            exchanges=(
-                (grad_latent_w, latent_other, 0),
-                (grad_dec, dec_other, 1),
-            ),
-        )
-    )
-    grad_middle = grad_hidden.astype(F32) + norm_back(
-        grad_norm_two, normed_two, scale_two, gain_two
-    )
-    middle_low = grad_middle.astype(BF16)
     grad_out = mat_tn(attended, middle_low).astype(BF16)
-    grad_qkv_act = attend_back(middle_low, out_w, projected, log_totals, slide, alive)
+    if tiled:
+        grad_qkv_act, (down_other, up_other, latent_other, dec_other) = attend_back(
+            3,
+            middle_low,
+            out_w,
+            projected,
+            log_totals,
+            slide,
+            alive,
+            ((grad_down, 1), (grad_up, 0), (grad_latent_w, 0), (grad_dec, 1)),
+        )
+    else:
+        grad_qkv_act, _ = attend_back(
+            11, middle_low, out_w, projected, log_totals, slide, alive, ()
+        )
     grad_qkv = mat_tn(first_low, grad_qkv_act).astype(BF16)
-    (grad_norm_one,), _, (qkv_other, out_other), (down_parts, up_parts), _, _ = meeting(
+    (grad_norm_one,), _, (qkv_other, out_other), (down_parts, up_parts, latent_parts, dec_parts), _, _ = meeting(
         8,
         (grad_qkv_act, qkv, True, False),
         swaps=((grad_qkv, 0), (grad_out, 1)),
-        exchanges=((grad_down, down_other, 1), (grad_up, up_other, 0)),
+        exchanges=(
+            (grad_down, down_other, 1),
+            (grad_up, up_other, 0),
+            (grad_latent_w, latent_other, 0),
+            (grad_dec, dec_other, 1),
+        ),
     )
     grad_start = grad_middle + norm_back(grad_norm_one, normed_one, scale_one, gain_one)
     start_low = grad_start.astype(BF16)
@@ -1789,8 +2192,8 @@
         [
             jnp.sum(grad_norm_one * normed_one, axis=0),
             jnp.sum(grad_norm_one, axis=0),
-            jnp.sum(grad_norm_two * normed_two, axis=0),
-            jnp.sum(grad_norm_two, axis=0),
+            norm_sums[0],
+            norm_sums[1],
         ]
     )
     norm_grads = norm_grads.reshape(4, shards, width).transpose(1, 0, 2)

time: 470 us -> 439 us (0.934)
  matrix products: 31.4 us -> 10 us
  other arithmetic: 27.4 us -> 13.2 us
  Pallas kernels: 369 us -> 376 us
    pallas_call x1 -> x4, Pallas kernels: 4.71 us -> 121 us  [the longest x1 97 us: back(): pl.pallas_call(functools.partial(back_kernel, spacing, float(latent_total...]
    pallas_call x4 -> x1, Pallas kernels: 146 us -> 37.3 us  [comm(): pl.pallas_call(functools.partial(comm_kernel, plan), out_shape=outputs, i...]
    dot_general x6 -> x0, matrix products: 15.5 us -> none  [the longest x2 8.73 us: mat_nn(): return jnp.dot(left, right, preferred_element_type=F32)]
    convert_element_type x3 -> x0, other arithmetic: 6.95 us -> none  [the longest x1 4.13 us: local(): middle_low = grad_middle.astype(BF16)]
    dot_general x7 -> x6, matrix products: 15.8 us -> 10 us  [mat_tn(): lax.dot_general(left, right, (((0,), (0,)), ((), ())), preferred_element_...]
    reduce_sum x5 -> x0, other arithmetic: 5.21 us -> none  [the longest x1 3.65 us: local(): jnp.sum(grad_norm_two * normed_two, axis=0)]
    unnamed x158 -> x104, local copies, waits for them, and re-layouts: 21 us -> 17.1 us
where the time goes in v4:
time: 439 us; the launch traced here: 433 us
  Pallas kernels  376 us (86%)
  local copies, waits for them, and re-layouts  31.4 us (7%)
  other arithmetic  13.2 us (3%)
  matrix products  10 us (2%)
    pallas_call x1, Pallas kernels, middle(): pl.pallas_call(functools.partial(middle_kernel, plan, spacing), out_shape...  104 us
    pallas_call x1, Pallas kernels, back(): pl.pallas_call(functools.partial(back_kernel, spacing, float(latent_total...  97 us
    pallas_call x1, Pallas kernels, head(): pl.pallas_call(functools.partial(head_kernel, plan), out_shape=[jax.Shape...  59 us
    pallas_call x1, Pallas kernels, tail(): pl.pallas_call(tail_kernel, out_shape=[jax.ShapeDtypeStruct((genes, width...  48.5 us
    pallas_call x1, Pallas kernels, comm(): pl.pallas_call(functools.partial(comm_kernel, plan), out_shape=outputs, i...  37.3 us
    unnamed x104, local copies, waits for them, and re-layouts  17.1 us
    pallas_call x1, Pallas kernels, decode(): pl.pallas_call(decode_kernel, grid_spec=pltpu.PrefetchScalarGridSpec(num_...  13.5 us
    dot_general x6, matrix products, mat_tn(): lax.dot_general(left, right, (((0,), (0,)), ((), ())), preferred_element_...  10 us

profile of v4, /device:TPU:0, one launch (start us, length us, event | category | flops | bytes accessed | tf_op | source)
XLA Modules:
  0.0 432.8 jit_solution(5312983831027731894)
XLA Ops:
  1.5 0.7 fusion.17
  2.2 0.2 reduce-window.4
  2.5 0.6 broadcast_in_dim.12.ramp_step
  3.1 0.8 constant_dynamic-slice_fusion.2
  3.9 0.7 fusion.16
  4.6 0.8 fusion.18
  5.3 0.7 fusion.8
  6.1 1.4 pad_maximum_fusion.1.refs_2_
  7.5 0.9 pad_maximum_fusion.refs_5_
  8.4 0.1 copy.104
  8.5 0.9 copy.97.alive
  9.4 0.7 constant_dynamic-slice_fusion.noise
  10.3 0.1 copy.91.slide_keys
  10.5 1.6 copy.94.refs_4_
  12.1 59.0 %head.1 = (f32[496,1024]{1,0:T(8,128)S(1)}, bf16[3376,1024]{1,0:T(8,128)(2,1)}, bf16[384,128]{1,0:T(8,128)(2,1)S(1)}, bf16[1024,768]{1,0:T(8,128)(2,1)S(1)}, bf16[256,1024]{1,0:T(8,128)(2,1)S(1)}) custom-call(f32[496,2]{1,0:T(8,128)S(1)} %bitcast.67, f32[1,256]{1,0:T(1,128)S(1)} %multiply_exponential_fusion.refs_1_, bf16[992,3376]{1,0:T(8,128)(2,1)} %expression.1, ...), custom_call_target="tpu_custom_call" | custom-call | tf_op jit(solution)/shard_map/head/pallas_call | solution.py:998
  71.1 1.3 copy-done.4
  72.4 0.8 copy-done.13
  73.2 0.7 slice_bitcast_fusion.7
  74.1 0.7 slice.96.centers
  74.8 5.3 %attend.1 = (f32[496,1024]{1,0:T(8,128)}, f32[496,1]{1,0:T(8,128)S(1)}, bf16[496,1024]{1,0:T(8,128)(2,1)S(1)}, bf16[496,768]{1,0:T(8,128)(2,1)S(1)}, bf16[496,256]{1,0:T(8,128)(2,1)S(1)}, /*index=5*/f32[4,496]{1,0:T(4,128)S(1)}) custom-call(f32[496,1024]{1,0:T(8,128)} %copy-done.4, f32[1,1024]{1,0:T(1,128)S(1)} %bitcast.74, f32[1,1024]{1,0:T(1,128)S(1)} %bitcast.73, ...), custom_call_target="tpu_custom_call" | custom-call | tf_op jit(solution)/shard_map/attend/pallas_call | solution.py:115
  80.2 0.7 copy-done.15
  80.9 0.9 copy-done.19
  81.7 0.6 copy-done.25
  82.3 1.0 copy-done.27
  83.3 0.1 reduce
  83.4 104.0 %middle.1 = (f32[496,1024]{1,0:T(8,128)}, f32[496,1]{1,0:T(8,128)}, bf16[496,1024]{1,0:T(8,128)(2,1)}, f32[496,1024]{1,0:T(8,128)}, bf16[496,1024]{1,0:T(8,128)(...) custom-call(bf16[496,256]{1,0:T(8,128)(2,1)} %copy-done.15, ...), custom_call_target="tpu_custom_call" | custom-call | tf_op jit(solution)/shard_map/middle/pallas_call | solution.py:1636
  187.5 1.1 reduce_sum.100
  188.8 0.1 add_reduce_fusion
  188.9 0.2 exponential_reduce_fusion
  189.2 0.6 convert_reduce_fusion
  189.9 0.7 pad.23.respons
  190.7 1.3 concatenate.33
  192.0 0.7 concatenate.34.counts
  192.6 13.5 %decode.1 = (bf16[496,3376]{1,0:T(8,128)(2,1)S(1)}, bf16[1024,3376]{1,0:T(8,128)(2,1)}) custom-call(s32[1]{0:T(128)} %bitcast.21.section, f32[496,1024]{1,0:T(8,128)S(1)} %copy-done.3, bf16[1024,3376]{1,0:T(8,128)(2,1)} %get-tuple-element.81.weights.genes_w, bf16[992,3376]{1,0:T(8,128)(2,1)} %expression.1, f32[496,1]{1,0:T(8,128)S(1)} %copy-done.8), custom_call_target="tpu_custom_call" | custom-call | tf_op jit(solution)/shard_map/decode/pallas_call | solution.py:147
  206.2 1.8 copy-done.2
  207.9 97.0 %back.1 = (bf16[496,1024]{1,0:T(8,128)(2,1)}, bf16[496,256]{1,0:T(8,128)(2,1)}, f32[496,128]{1,0:T(8,128)}, bf16[496,1024]{1,0:T(8,128)(2,1)}, bf16[496,1024]{1,...) custom-call(f32[8,128]{1,0:T(8,128)} %broadcast_in_dim.12.ramp_step,, ...), custom_call_target="tpu_custom_call" | custom-call | tf_op jit(solution)/shard_map/back/pallas_call | solution.py:1877
  305.0 1.9 convolution_convert_fusion.4.refs_2_.refs_6_
  306.9 0.9 slice_bitcast_fusion.1
  307.8 0.3 convolution_convert_fusion.5.refs_3_.refs_7_
  308.2 1.9 fusion.2
  310.4 0.5 convolution_convert_fusion.3.refs_3_.out
  310.9 0.7 copy-done.43
  311.5 0.3 copy-done.45
  311.9 2.6 convolution_convert_fusion.1.refs_0_.refs_4_
  314.5 2.6 convolution_convert_fusion.refs_1_.refs_5_
  317.2 5.2 %attend_back.1 = (bf16[496,768]{1,0:T(8,128)(2,1)S(1)}, bf16[1024,512]{1,0:T(8,128)(2,1)S(1)}, bf16[512,1024]{1,0:T(8,128)(2,1)}, bf16[512,256]{1,0:T(8,128)(2,1)S(1)}, bf16[128,512]{1,0:T(8,128)(2,1)S(1)}) custom-call(bf16[496,1024]{1,0:T(8,128)(2,1)S(1)} %copy-done.7, bf16[256,1024]{1,0:T(8,128)(2,1)S(1)} %copy-done.14, bf16[496,768]{1,0:T(8,128)(2,1)S(1)} %copy-done.20, ...), custom_call_target="tpu_custom_call" | custom-call | tf_op jit(solution)/shard_map/attend_back/pallas_call | solution.py:227
  322.4 2.2 convolution_convert_fusion.2.refs_2_.qkv
  324.6 37.3 %meet.1 = (f32[496,1024]{1,0:T(8,128)}, bf16[512,768]{1,0:T(8,128)(2,1)S(1)}, bf16[256,512]{1,0:T(8,128)(2,1)S(1)}, f32[1024,128]{1,0:T(8,128)S(1)}, f32[128,102...) custom-call(bf16[496,768]{1,0:T(8,128)(2,1)S(1)} %get-tuple-element.106.refs_0_, ...), custom_call_target="tpu_custom_call" | custom-call | flops 1000000 | bytes 90000000 | tf_op jit(solution)/shard_map/meet/pallas_call | solution.py:733
  361.9 2.6 multiply_reduce_fusion
  364.6 0.5 copy-done.31
  365.1 1.5 add_convert_fusion.start
  366.5 0.7 copy.102
  367.2 48.5 %tail.1 = (f32[3376,128]{1,0:T(8,128)}, f32[128,768]{1,0:T(8,128)}, f32[256,128]{1,0:T(8,128)}, f32[48,128]{1,0:T(8,128)}, bf16[496,3376]{1,0:T(8,128)(2,1)}, /*index=5*/bf16[496,3376]{1,0:T(8,128)(2,1)}) custom-call(bf16[496,1024]{1,0:T(8,128)(2,1)} %add_convert_fusion.start, bf16[992,3376]{1,0:T(8,128)(2,1)} %expression.1, ...), custom_call_target="tpu_custom_call" | custom-call | tf_op jit(solution)/shard_map/tail/pallas_call | solution.py:1248
  415.7 1.4 slice_bitcast_fusion.2
  417.1 1.3 fusion.22
  418.4 0.7 fusion.20
  419.1 1.8 fusion.19
  420.9 1.7 copy.103
  422.5 6.0 %assemble.1 = bf16[992,3376]{1,0:T(8,128)(2,1)} custom-call(bf16[496,3376]{1,0:T(8,128)(2,1)} %get-tuple-element.128.own, bf16[496,3376]{1,0:T(8,128)(2,1)} %get-tuple-element.129.other), custom_call_target="tpu_custom_call" | custom-call | tf_op jit(solution)/shard_map/assemble/pallas_call | solution.py:1282
  428.5 1.2 copy.120
  429.7 0.7 copy.121
  430.4 0.8 copy.122
  431.2 0.8 copy.123
  432.0 0.6 copy.124
  (111 shorter events, 1.3 us)
Async XLA Ops:
  0.7 8.7 %copy-start = (f32[992,128]{1,0:T(8,128)S(1)}, f32[992,128]{1,0:T(8,128)}, u32[]{:S(2)}) copy-start(f32[992,128]{1,0:T(8,128)} %param.28) | copy-start | bytes 1523716
  0.7 9.8 %copy-start.36 = (bf16[128,3376]{0,1:T(8,128)(2,1)S(1)}, bf16[128,3376]{0,1:T(8,128)(2,1)}, u32[]{:S(2)}) copy-start(bf16[128,3376]{0,1:T(8,128)(2,1)} %param.45) | copy-start | bytes 2592772
  0.7 11.4 %copy-start.22 = (bf16[256,128]{1,0:T(8,128)(2,1)S(1)}, bf16[256,128]{1,0:T(8,128)(2,1)}, u32[]{:S(2)}) copy-start(bf16[256,128]{1,0:T(8,128)(2,1)} %refs_6_.1) | copy-start | bytes 196612
  0.7 11.4 %copy-start.17 = (bf16[3376,128]{1,0:T(8,128)(2,1)S(1)}, bf16[3376,128]{1,0:T(8,128)(2,1)}, u32[]{:S(2)}) copy-start(bf16[3376,128]{1,0:T(8,128)(2,1)} %refs_3_.2) | copy-start | bytes 2592772
  2.5 72.3 %copy-start.23 = (s32[496]{0:T(512)}, s32[496]{0:T(512)S(1)}, u32[]{:S(2)}) copy-start(s32[496]{0:T(512)S(1)} %fusion.13) | copy-start | bytes 5956
  10.3 64.5 %copy-start.9 = (s32[496,1]{1,0:T(8,128)}, s32[496,1]{1,0:T(8,128)S(1)}, u32[]{:S(2)}) copy-start(s32[496,1]{1,0:T(8,128)S(1)} %copy.92.alive_keys) | copy-start | bytes 5956
  10.4 64.3 %copy-start.11 = (s32[496,1]{1,0:T(8,128)}, s32[496,1]{1,0:T(8,128)S(1)}, u32[]{:S(2)}) copy-start(s32[496,1]{1,0:T(8,128)S(1)} %copy.91.slide_keys) | copy-start | bytes 5956
  71.1 1.3 copy-start.4
  72.4 0.8 copy-start.13
  73.2 6.9 %copy-start.5 = (bf16[1024,768]{1,0:T(8,128)(2,1)}, bf16[1024,768]{1,0:T(8,128)(2,1)S(1)}, u32[]{:S(2)}) copy-start(bf16[1024,768]{1,0:T(8,128)(2,1)S(1)} %get-tuple-element.76.weights.refs_1_) | copy-start | bytes 4718596
  74.1 6.1 %copy-start.39 = (f32[16,128]{1,0:T(8,128)}, f32[16,128]{1,0:T(8,128)S(1)}, u32[]{:S(2)}) copy-start(f32[16,128]{1,0:T(8,128)S(1)} %slice.98.spreads) | copy-start | bytes 24580
  80.2 0.7 copy-start.15
  80.9 0.9 copy-start.19
  81.7 0.6 copy-start.25
  82.3 1.0 copy-start.27
  187.4 5.2 %copy-start.3 = (f32[496,1024]{1,0:T(8,128)S(1)}, f32[496,1024]{1,0:T(8,128)}, u32[]{:S(2)}) copy-start(f32[496,1024]{1,0:T(8,128)} %get-tuple-element.80.pre.decoder_pre) | copy-start | bytes 6094852
  187.4 5.2 %copy-start.8 = (f32[496,1]{1,0:T(8,128)S(1)}, f32[496,1]{1,0:T(8,128)}, u32[]{:S(2)}) copy-start(f32[496,1]{1,0:T(8,128)} %copy.97.alive) | copy-start | bytes 5956
  206.2 1.8 copy-start.2
  305.0 2.8 copy-start.35
  305.0 2.8 copy-start.41
  305.0 3.1 copy-start.37
  305.0 3.3 copy-start.34
  305.0 3.2 copy-start.38
  306.9 3.5 copy-start.7
  306.9 3.5 copy-start.16
  310.3 1.2 copy-start.43
  310.3 1.5 copy-start.45
  311.9 12.7 %copy-start.6 = (bf16[256,1024]{1,0:T(8,128)(2,1)}, bf16[256,1024]{1,0:T(8,128)(2,1)S(1)}, u32[]{:S(2)}) copy-start(bf16[256,1024]{1,0:T(8,128)(2,1)S(1)} %convolution_convert_fusion.3.refs_3_.out) | copy-start | bytes 1572868
  311.9 2.6 copy-start.42
  311.9 2.6 copy-start.44
  314.5 2.7 copy-start.10
  314.5 2.7 copy-start.12
  314.5 2.7 copy-start.14
  314.5 2.7 copy-start.20
  314.5 2.7 copy-start.24
  314.5 2.7 copy-start.26
  317.2 5.2 %copy-start.28 = (bf16[496,1024]{1,0:T(8,128)(2,1)S(1)}, bf16[496,1024]{1,0:T(8,128)(2,1)}, u32[]{:S(2)}) copy-start(bf16[496,1024]{1,0:T(8,128)(2,1)} %copy-done.27) | copy-start | bytes 3047428
  324.6 37.3 %copy-start.29 = (f32[496,1024]{1,0:T(8,128)S(1)}, f32[496,1024]{1,0:T(8,128)}, u32[]{:S(2)}) copy-start(f32[496,1024]{1,0:T(8,128)} %get-tuple-element.113) | copy-start | bytes 6094852
  361.9 2.6 copy-start.18
  361.9 2.6 copy-start.21
  361.9 2.7 copy-start.30
  361.9 3.1 copy-start.31
  367.2 53.6 %copy-start.32 = (f32[128,3376]{1,0:T(8,128)S(1)}, f32[128,3376]{1,0:T(8,128)}, u32[]{:S(2)}) copy-start(f32[128,3376]{1,0:T(8,128)} %get-tuple-element.218) | copy-start | bytes 5185540
  422.5 6.0 %copy-start.33 = (f32[3376,128]{1,0:T(8,128)S(1)}, f32[3376,128]{1,0:T(8,128)}, u32[]{:S(2)}) copy-start(f32[3376,128]{1,0:T(8,128)} %get-tuple-element.269) | copy-start | bytes 5185540
  428.5 1.2 copy-start.40
  428.5 4.1 copy-start.1

commit v5 on v4

--- a/solution.py
+++ b/solution.py
@@ -18,6 +18,10 @@
 WINDOW = 3
 BLOCK_STEP = 4
 TILE = 256
+PARTS = 4
+PART_ROWS = 128
+PIECE_COLUMNS = 256
+TILES_FROM = 15
 LINK_BYTES_PER_US = 92000.0
 MOMENT_US = 1.3
 SPREAD = 1
@@ -81,7 +85,15 @@
     return jnp.sum((index[:, None] >= bounds[None, :]).astype(jnp.int32), axis=1)
 
 
-def attend_kernel(start, gain, bias, weights, slide_keys, slide_queries, alive_keys, *outs):
+def allowed_pairs(info):
+    columns = info[...].T
+    cells = columns.shape[0]
+    shape = (cells, cells)
+    own_key = lax.broadcasted_iota(jnp.int32, shape, 0) == lax.broadcasted_iota(jnp.int32, shape, 1)
+    return (columns[:, 0:1] == info[0:1, :]) & ((columns[:, 1:2] == 1.0) | own_key)
+
+
+def attend_kernel(start, gain, bias, weights, info, *outs):
     normed_out, scale_out, low_out, projected_out, attended_out, totals_out = outs
     cells, width = attended_out.shape
     factor = HEAD ** (-0.5)
@@ -92,9 +104,7 @@
     low_out[...] = low
     projected = mat_nn(low, weights[...]).astype(BF16)
     projected_out[...] = projected
-    shape = (cells, cells)
-    own_key = lax.broadcasted_iota(jnp.int32, shape, 0) == lax.broadcasted_iota(jnp.int32, shape, 1)
-    allowed = (slide_keys[...] == slide_queries[...]) & ((alive_keys[...] == 1) | own_key)
+    allowed = allowed_pairs(info)
     for head_index in range(width // HEAD):
         first = head_index * HEAD
         q = projected[:, first : first + HEAD]
@@ -109,7 +119,7 @@
         totals_out[head_index : head_index + 1, :] = largest + jnp.log(sums)
 
 
-def attend(start, gain, bias, weights, slide, alive):
+def attend(start, gain, bias, weights, info):
     cells, features = start.shape
     width = weights.shape[1] // 3
     return pl.pallas_call(
@@ -124,7 +134,7 @@
         ],
         compiler_params=pltpu.CompilerParams(vmem_limit_bytes=48 * 2**20),
         name="attend",
-    )(start, gain, bias, weights, slide[:, None], slide[None, :], alive[:, None])
+    )(start, gain, bias, weights, info)
 
 
 def decode_kernel(section, pre, weights, cells, alive, residual, grad, act, act_turned):
@@ -170,7 +180,7 @@
     )(micro.astype(jnp.int32).reshape(1), pre, weights, expression, alive[:, None])
 
 
-def attend_back_kernel(plan, middle, out_w, projected, log_totals, slide_keys, slide_queries, alive_keys, *refs):
+def attend_back_kernel(plan, middle, out_w, projected, log_totals, info, *refs):
     swapped, out, received = refs[: len(plan)], refs[len(plan)], refs[len(plan) + 1 : 2 * len(plan) + 1]
     sent, got = refs[2 * len(plan) + 1 :]
     section = lax.axis_index("section")
@@ -192,9 +202,7 @@
         copy.start()
     cells, width = out.shape[0], out.shape[1] // 3
     factor = HEAD ** (-0.5)
-    shape = (cells, cells)
-    own_key = lax.broadcasted_iota(jnp.int32, shape, 0) == lax.broadcasted_iota(jnp.int32, shape, 1)
-    allowed = (slide_keys[...] == slide_queries[...]) & ((alive_keys[...] == 1) | own_key)
+    allowed = allowed_pairs(info)
     grad_out = mat_nt(middle[...], out_w[...]).astype(BF16)
     for head in range(width // HEAD):
         first = head * HEAD
@@ -216,7 +224,7 @@
         copy.wait()
 
 
-def attend_back(number, middle, out_w, projected, log_totals, slide, alive, swaps):
+def attend_back(number, middle, out_w, projected, log_totals, info, swaps):
     plan = tuple((axis, array.shape[axis] // 2) for array, axis in swaps)
     halves = [
         array.shape[:axis] + (array.shape[axis] // 2,) + array.shape[axis + 1 :]
@@ -228,7 +236,7 @@
         functools.partial(attend_back_kernel, plan),
         out_shape=[jax.ShapeDtypeStruct(projected.shape, BF16)]
         + [jax.ShapeDtypeStruct(half, BF16) for half in halves],
-        in_specs=[vmem] * 7 + [anywhere] * count,
+        in_specs=[vmem] * 5 + [anywhere] * count,
         out_specs=[vmem] + [anywhere] * count,
         scratch_shapes=[pltpu.SemaphoreType.DMA((max(count, 1),))] * 2,
         compiler_params=pltpu.CompilerParams(
@@ -240,9 +248,7 @@
         out_w,
         projected,
         log_totals,
-        slide[:, None],
-        slide[None, :],
-        alive[:, None],
+        info,
         *[array for array, _ in swaps],
     )
     return results[0], results[1:]
@@ -1275,7 +1281,7 @@
             pltpu.SemaphoreType.DMA((22,)),
         ],
         compiler_params=pltpu.CompilerParams(
-            collective_id=number, has_side_effects=True, vmem_limit_bytes=56 * 2**20
+            collective_id=number, has_side_effects=True, vmem_limit_bytes=62 * 2**20
         ),
         name="tail",
     )(start, expression, embed, grad_rebuilt, qkv, out, small, qkv_other, out_other)
@@ -1286,7 +1292,7 @@
         out_specs=anywhere,
         scratch_shapes=[pltpu.VMEM((2, rows, genes), BF16)]
         + [pltpu.SemaphoreType.DMA((2 * (-(-rows // 128)),))] * 2,
-        compiler_params=pltpu.CompilerParams(vmem_limit_bytes=56 * 2**20),
+        compiler_params=pltpu.CompilerParams(vmem_limit_bytes=62 * 2**20),
         name="assemble",
     )(results[4], results[5])
     return list(results[:4]) + [whole]
@@ -1294,12 +1300,13 @@
 
 def line_pipe(produce, hooks, items, spacing, part, total, from_left, from_right, to_right, to_left, got_left, got_right, sent_right, sent_left):
     me, count = lax.axis_index("mp"), lax.axis_size("mp")
-    pieces = part.shape[2] // 128
+    columns = from_left.shape[2]
+    pieces = part.shape[2] // columns
     has_right, has_left = me < count - 1, me > 0
 
     def place(slot):
-        column = lax.rem(slot, spacing) * 128
-        return (lax.rem(lax.div(slot, spacing), 2), slice(None), pl.ds(pl.multiple_of(column, 128), 128))
+        first = pl.multiple_of(lax.rem(slot, spacing) * columns, columns)
+        return (lax.rem(lax.div(slot, spacing), PARTS), slice(None), pl.ds(first, columns))
 
     rooms = from_left.shape[0]
 
@@ -1385,7 +1392,7 @@
 
         return carry
 
-    lax.fori_loop(0, (items + 1) * spacing, step, 0)
+    lax.fori_loop(0, (items + PARTS - 1) * spacing, step, 0)
 
     def finish(slot, carry):
         @pl.when(used(slot) & has_right)
@@ -1402,11 +1409,17 @@
 
 
 def pipe_spacing(pieces, count):
-    return max(pieces + 1, (pieces - 1 + HOP_LAG * (count - 1)) // 2 + 1)
+    return max(pieces, (pieces - 1 + HOP_LAG * (count - 1)) // PARTS + 1)
+
+
+def part_rows(part, cells):
+    last = lax.div(part, PARTS - 1) * (PARTS * PART_ROWS - cells)
+    return pl.ds(pl.multiple_of(part * PART_ROWS - last, 16), PART_ROWS)
 
 
 def middle_kernel(
-    plan, spacing, attended, start, gain, bias, out_w, noise, centers, spreads, *refs
+    plan, spacing, start, gain_one, bias_one, qkv_w, info, gain, bias, out_w, noise,
+    centers, spreads, *refs
 ):
     refs = list(refs)
 
@@ -1420,6 +1433,8 @@
     (normed_out, scale_out, second_out, upper_out, active_out, hidden_out, log_vars_out,
      latent_out, spread_out, latent_low_out, decoder_out, density_all) = take(12)
     gathered = take(count)
+    attend_outs = take(6)
+    attended = attend_outs[4]
     part, total, kept_rows, density = take(4)
     up_in, down_in, latent_in, dec_in = take(4)
     held = take(count)
@@ -1490,17 +1505,19 @@
         for copy in keeps:
             copy.start()
 
-    near, far = list(range(count - 1)), [count - 1]
-
-    def fetch():
-        for item in near:
-            for name in ("own", "relay_x", "relay_y", "relay_upper", "relay_lower"):
-                spreads_of[item][name].wait_recv()
-            keeps[item].wait()
-        for copy in fetches:
-            copy.start()
-        for copy in fetches:
-            copy.wait()
+    near, mid, far = [0, 1], [2, 3], [4]
+
+    def fetch(items):
+        def run():
+            for item in items:
+                for name in ("own", "relay_x", "relay_y", "relay_upper", "relay_lower"):
+                    spreads_of[item][name].wait_recv()
+                keeps[item].wait()
+                fetches[item].start()
+            for item in items:
+                fetches[item].wait()
+
+        return run
 
     def share():
         for copy in density_sends + [density_keep]:
@@ -1508,9 +1525,11 @@
 
     for load in loads:
         load.start()
+    run_steps(near, 0)()
+    attend_kernel(start, gain_one, bias_one, qkv_w, info, *attend_outs)
 
     def rows_of(half):
-        return pl.ds(pl.multiple_of(half * (cells - half_rows), 16), half_rows)
+        return part_rows(half, cells)
 
     def out_product(half):
         part[half] = mat_nn(attended[rows_of(half), :], out_w[...])
@@ -1568,26 +1587,29 @@
 
     def produce(moment):
         item = lax.div(moment, spacing)
-        half, stage = lax.rem(item, 2), lax.div(item, 2)
+        half, stage = lax.rem(item, PARTS), lax.div(item, PARTS)
         begins = lax.rem(moment, spacing) == 0
         for number, work in enumerate((out_product, feed_forward, latents_of, conclude)):
             pl.when(begins & (stage == number))(functools.partial(work, half))
 
     hooks = [
-        (0, run_steps(near, 0)),
         (1, keep),
-        (7, run_steps(near, 1)),
-        (13, run_steps(near, 2)),
-        (16, run_steps(near, 3)),
-        (2 * spacing, fetch),
-        (2 * spacing + 1, run_steps(far, 0)),
-        (2 * spacing + 10, run_steps(far, 1)),
-        (2 * spacing + 18, run_steps(far, 2)),
-        (2 * spacing + 26, run_steps(far, 3)),
-        (5 * spacing + 1, share),
+        (3, run_steps(near, 1)),
+        (7, run_steps(near, 2)),
+        (11, run_steps(near, 3)),
+        (12, run_steps(mid + far, 0)),
+        (PARTS * spacing, fetch(near)),
+        (PARTS * spacing + 3, run_steps(mid, 1)),
+        (PARTS * spacing + 5, run_steps(mid, 2)),
+        (PARTS * spacing + 7, run_steps(mid, 3)),
+        (PARTS * spacing + 10, run_steps(far, 1)),
+        (2 * PARTS * spacing - 1, fetch(mid)),
+        (2 * PARTS * spacing + 2, run_steps(far, 2)),
+        (2 * PARTS * spacing + 10, run_steps(far, 3)),
+        (3 * PARTS * spacing - spacing + 1, share),
     ]
-    line_pipe(produce, hooks, 6, spacing, part, total, *line)
-    conclude(1)
+    line_pipe(produce, hooks, 3 * PARTS, spacing, part, total, *line)
+    conclude(PARTS - 1)
     for item in far:
         for name in ("own", "relay_x", "relay_y", "relay_upper", "relay_lower"):
             spreads_of[item][name].wait_recv()
@@ -1600,14 +1622,12 @@
     density_keep.wait()
 
 
-def middle(number, attended, start, gain, bias, out_w, noise, centers, spreads, gathers):
+def middle(number, start, norm_one, qkv_w, info, gain, bias, out_w, noise, centers, spreads, gathers):
     sections, count_dp, count_z = (lax.axis_size(name) for name in ("section", "dp", "mp"))
     cells, features = start.shape
     latents = noise.shape[1]
     total_parts = sections * count_dp
-    pieces = features // 128
-    spacing = pipe_spacing(pieces, count_z)
-    half_rows = 256
+    spacing = pipe_spacing(features // PIECE_COLUMNS, count_z)
     plan = tuple((axis, shard.shape[axis]) for shard, axis in gathers)
     shapes = [
         shard.shape[:axis] + (shard.shape[axis] * total_parts,) + shard.shape[axis + 1 :]
@@ -1627,18 +1647,27 @@
         ((cells, latents), F32),
         ((cells, latents), BF16),
         ((cells, features), F32),
-        ((count_z, 24, 2 * half_rows), F32),
+        ((count_z, 24, PARTS * PART_ROWS), F32),
     ] + [(shape, BF16) for shape in shapes]
-    rooms = 2 * spacing
-    buffer = pltpu.VMEM((rooms, half_rows, 128), BF16)
+    width = qkv_w.shape[1] // 3
+    outputs += [
+        ((cells, features), F32),
+        ((cells, 1), F32),
+        ((cells, features), BF16),
+        ((cells, 3 * width), BF16),
+        ((cells, width), BF16),
+        ((width // HEAD, cells), F32),
+    ]
+    rooms = PARTS * spacing
+    buffer = pltpu.VMEM((rooms, PART_ROWS, PIECE_COLUMNS), BF16)
     copies = 11 * len(gathers) + count_z - 1
-    halves = pltpu.VMEM((2, half_rows, features), F32)
+    halves = pltpu.VMEM((PARTS, PART_ROWS, features), F32)
     results = pl.pallas_call(
         functools.partial(middle_kernel, plan, spacing),
         out_shape=[jax.ShapeDtypeStruct(*item) for item in outputs],
-        in_specs=[vmem] * 8 + [anywhere] * len(gathers),
-        out_specs=[vmem] * 11 + [anywhere] * (1 + len(gathers)),
-        scratch_shapes=[halves, halves, halves, pltpu.VMEM((24, 2 * half_rows), F32)]
+        in_specs=[vmem] * 11 + [anywhere] * len(gathers),
+        out_specs=[vmem] * 11 + [anywhere] * (1 + len(gathers)) + [vmem] * 6,
+        scratch_shapes=[halves, halves, halves, pltpu.VMEM((24, PARTS * PART_ROWS), F32)]
         + [pltpu.VMEM(shape, BF16) for shape in shapes[:-1]]
         + [pltpu.VMEM(shard.shape, BF16) for shard, _ in gathers]
         + [buffer] * 4
@@ -1649,19 +1678,22 @@
             pltpu.SemaphoreType.DMA((3 * len(gathers),)),
         ],
         compiler_params=pltpu.CompilerParams(
-            collective_id=number, has_side_effects=True, vmem_limit_bytes=60 * 2**20
+            collective_id=number, has_side_effects=True, vmem_limit_bytes=62 * 2**20
         ),
         name="middle",
-    )(attended, start, gain, bias, out_w, noise, centers, spreads, *[shard for shard, _ in gathers])
-    return results[:12], results[12:]
+    )(
+        start, *norm_one, qkv_w, info, gain, bias, out_w, noise, centers,
+        spreads, *[shard for shard, _ in gathers],
+    )
+    return results[:12], results[12:-6], results[-6:]
 
 
 def back_kernel(
-    spacing, latent_total, ramp_step, counts, grad_rebuilt, decoder_pre, latent, spread_latent, respons, alive, centers,
-    spreads, upper, normed, scale, gain, genes_w, dec_w, latent_w, down_w, up_w, grad_genes,
-    pre_out, stats_out, weighted_out, hidden_out, upper_out, middle_out, low_out, sums_out,
-    genes_sum, genes_other, part, total, hidden_rows, counts_all, kl_scale, genes_in, dec_in, latent_in, down_in,
-    up_in, mine, theirs, from_x, from_y, inbound, *refs
+    spacing, latent_total, ramp_step, density_parts, info, latent, spread_latent, centers,
+    spreads, upper, scale, gain, decoder_pre, normed, genes_w, dec_w, latent_w, down_w, up_w, expression,
+    pre_out, stats_out, comps_out, hidden_out, upper_out, middle_out, low_out, sums_out,
+    genes_sum, rebuilt_out, part, total, wide, counts, respons, info_columns, counts_all, kl_scale, genes_in, dec_in, latent_in, down_in,
+    up_in, cells_in, residual, act_turned, grad, cells_sem, free, *refs
 ):
     line, (sent, got, local_sem) = refs[:8], refs[8:]
     section, z, dp = (lax.axis_index(name) for name in ("section", "mp", "dp"))
@@ -1711,36 +1743,69 @@
     around = (section, dp, peers, partner, to_x, to_y)
     counting = spread(remote, counts, counts_all, 0, count_rows, *around)
     count_steps = spread_steps(counting)
-    size = from_x.shape[0]
-    swap = remote(part_of(grad_genes, 0, 1 - section, size * count_dp), genes_other, partner)
-    indices = (peers[2], peer_x, peer_y, dp)
-    load_mine = [
-        within(block_of(grad_genes, 0, section * count_dp + index, size), mine.at[index])
-        for index in range(count_dp)
+    size = genes_sum.shape[0]
+    act = pre_out
+    theirs = genes_in.at[pl.ds(0, count_dp)]
+    from_x, from_y, inbound = (genes_in.at[count_dp + room] for room in range(3))
+    swap = remote(grad.at[pl.ds((1 - section) * count_dp, count_dp)], theirs, partner)
+    indices = tuple(section * count_dp + index for index in (peers[2], peer_x, peer_y, dp))
+    first, second, pass_on, conclude_genes = trade(
+        remote, grad, indices, from_x, from_y, inbound, to_x, to_y
+    )
+    load_genes = [
+        within(genes_w.at[pl.ds(index * size, size), :], genes_in.at[index])
+        for index in range(genes_in.shape[0])
     ]
-    load_theirs = [
-        within(block_of(genes_other, 0, index, size), theirs.at[index]) for index in range(count_dp)
-    ]
-    first, second, pass_on, conclude_genes = trade(
-        remote, mine, indices, from_x, from_y, inbound, to_x, to_y
-    )
-    load_genes = within(genes_w, genes_in)
+    keep_residual = within(residual, rebuilt_out)
+    load_pre, load_normed = within(decoder_pre, wide), within(normed, wide)
+
+    def load_cells(part_index, room):
+        rows = part_rows(part_index, cells)
+        first_row = pl.multiple_of(section * cells + rows.start, 16)
+        return pltpu.make_async_copy(
+            expression.at[pl.ds(first_row, PART_ROWS), :], cells_in.at[room], cells_sem.at[room]
+        )
     fetches = [
         within(src, dst)
         for src, dst in ((dec_w, dec_in), (latent_w, latent_in), (down_w, down_in), (up_w, up_in))
     ]
 
-    load_genes.start()
-    counts_all[pl.ds(pl.multiple_of((section * count_dp + dp) * count_rows, 8), count_rows), :] = (
-        counts[...]
-    )
+    load_pre.start()
+    for copy in load_genes:
+        copy.start()
+    for room in range(2):
+        load_cells(room, room).start()
+    sums_out[...] = jnp.zeros_like(sums_out)
+    comps_out[...] = jnp.zeros_like(comps_out)
+    def mixture():
+        density = sum(density_parts[index] for index in range(count_z))
+        logits = density[:comp_count, :] - math.log(comp_count)
+        largest = jnp.max(logits, axis=0, keepdims=True)
+        log_prior = largest + jnp.log(jnp.sum(jnp.exp(logits - largest), axis=0, keepdims=True))
+        respons[...] = jnp.exp(logits - log_prior).T
+        info_columns[...] = info[...].T
+        kept = info[1:2, :]
+        early = (PARTS - 1) * PART_ROWS
+        by_part = jnp.concatenate([kept[:, :early], kept[:, cells - PART_ROWS :]], axis=1)
+        lane = lax.broadcasted_iota(jnp.int32, by_part.shape, 1)
+        repeated = (lane >= early) & (lane < PARTS * PART_ROWS - (cells - early))
+        by_part = jnp.where(repeated, 0.0, by_part)
+        difference = density[comp_count : comp_count + 1, :] - log_prior
+        divergence = jnp.sum(difference * by_part, axis=1, keepdims=True)
+        live = jnp.sum(kept, axis=1, keepdims=True)
+        line_of = lax.broadcasted_iota(jnp.int32, counts.shape, 0)
+        counts[...] = jnp.where(line_of == 0, divergence, live)
+        mine = pl.ds(pl.multiple_of((section * count_dp + dp) * count_rows, 8), count_rows)
+        counts_all[mine, :] = counts[...]
 
     def begin():
+        mixture()
         count_steps[0]()
-        swap.start()
-        for copy in fetches + load_mine:
+        for copy in fetches:
             copy.start()
-        load_genes.wait()
+        load_pre.wait()
+        for copy in load_genes:
+            copy.wait()
 
     def count_cells():
         for name in ("own", "relay_x", "relay_y", "relay_upper", "relay_lower"):
@@ -1760,38 +1825,71 @@
         sigmoid = jnp.where(excess >= 0.0, 1.0, small) / above
         kl_scale[0:1, :] = ramp_step[0:1, :] * softplus * sigmoid
 
-    def open_theirs():
+    def residual_done():
+        for device in (partner, to_x, to_y):
+            pl.semaphore_signal(free, inc=1, device_id=device)
+        keep_residual.start()
+        act_turned[...] = act[...].T
+
+    genes = residual.shape[1]
+    whole = genes // TILE
+
+    def grad_tile(span, width):
+        tile = mat_nn(act_turned[...], residual[:, span])
+        grad[:, :, span] = tile.reshape(grad.shape[0], size, width).astype(BF16)
+
+    def swap_halves():
+        if genes % TILE:
+            grad_tile(pl.ds(whole * TILE, genes % TILE), genes % TILE)
+        pl.semaphore_wait(free, 3)
+        swap.start()
+
+    def trade_begins():
         swap.wait_recv()
-        for copy in load_theirs:
-            copy.start()
-
-    def trade_begins():
-        for copy in load_mine + load_theirs:
-            copy.wait()
-        mine[...] = (mine[...].astype(F32) + theirs[...].astype(F32)).astype(BF16)
+        mine = pl.ds(section * count_dp, count_dp)
+        grad[mine] = (grad[mine].astype(F32) + genes_in[0:count_dp].astype(F32)).astype(BF16)
         for copy in first + second:
             copy.start()
 
     def rows_of(half):
-        return pl.ds(pl.multiple_of(half * (cells - half_rows), 16), half_rows)
+        return part_rows(half, cells)
 
     def genes_product(half):
-        part[half] = mat_nt(grad_rebuilt[rows_of(half), :], genes_in[...])
+        rows, room = rows_of(half), lax.rem(half, 2)
+        weights = genes_in[...].reshape(genes_in.shape[0] * size, genes)
+        own_act = gelu(wide[rows, :]).astype(BF16)
+        act[rows, :] = own_act
+        load_cells(half, room).wait()
+        rebuilt = mat_nn(own_act, weights)
+        difference = ((rebuilt - cells_in[room].astype(F32)) * info_columns[rows, 1:2]).astype(BF16)
+        residual[rows, :] = difference
+        part[half] = mat_nt(difference, weights)
+
+        @pl.when(half + 2 < PARTS)
+        def _():
+            load_cells(half + 2, room).start()
 
     def latents_back(half):
         rows = rows_of(half)
-        pre = (total[half] * gelu_slope(decoder_pre[rows, :])).astype(BF16)
+        pre = (total[half] * gelu_slope(wide[rows, :])).astype(BF16)
         pre_out[rows, :] = pre
-        weight = kl_scale[0:1, 0:1] * alive[rows, :]
-        weighted = respons[rows, :] * weight
-        weighted_out[rows, :] = weighted
+        weight = kl_scale[0:1, 0:1] * info_columns[rows, 1:2]
+        by_part = pl.ds(pl.multiple_of(half * PART_ROWS, PART_ROWS), PART_ROWS)
+        weighted = respons[by_part, :] * weight
         own_latent = latent[rows, :]
         grad_latent = mat_nt(pre, dec_in[...])
+        line_of = lax.broadcasted_iota(jnp.int32, weighted.shape, 0)
+        repeated = jnp.where(half < PARTS - 1, 0, PARTS * PART_ROWS - cells)
+        counted = jnp.where(line_of >= repeated, weighted, 0.0)
         for index in range(comp_count):
-            pulled = (own_latent - centers[index : index + 1, :]) * jnp.exp(
-                -spreads[index : index + 1, :]
+            offset = own_latent - centers[index : index + 1, :]
+            pulled = offset * jnp.exp(-spreads[index : index + 1, :])
+            grad_latent = grad_latent + weighted[:, index : index + 1] * pulled
+            share = counted[:, index : index + 1]
+            comps_out[index : index + 1, :] -= jnp.sum(share * pulled, axis=0, keepdims=True)
+            comps_out[comp_count + index : comp_count + index + 1, :] -= jnp.sum(
+                share * (0.5 * offset * pulled - 0.5), axis=0, keepdims=True
             )
-            grad_latent = grad_latent + weighted[:, index : index + 1] * pulled
         grad_logs = grad_latent * (0.5 * spread_latent[rows, :]) - 0.5 * weight
         stats = jnp.concatenate([grad_latent.astype(BF16), grad_logs.astype(BF16)], axis=1)
         stats_out[rows, :] = stats
@@ -1800,7 +1898,6 @@
     def feed_back(half):
         rows = rows_of(half)
         hidden = total[half].astype(BF16)
-        hidden_rows[half] = hidden
         hidden_out[rows, :] = hidden
         grad_upper = (mat_nt(hidden, down_in[...]) * gelu_slope(upper[rows, :])).astype(BF16)
         upper_out[rows, :] = grad_upper
@@ -1808,100 +1905,122 @@
 
     def conclude(half):
         rows = rows_of(half)
-        grad_norm, own_normed = total[half], normed[rows, :]
-        grad_middle = hidden_rows[half].astype(F32) + norm_back(
+        grad_norm, own_normed = total[half], wide[rows, :]
+        grad_middle = hidden_out[rows, :].astype(F32) + norm_back(
             grad_norm, own_normed, scale[rows, :], gain[...]
         )
         middle_out[rows, :] = grad_middle
         low_out[rows, :] = grad_middle.astype(BF16)
         return grad_norm * own_normed, grad_norm
 
-    def conclude_first(half):
+    def conclude_early(half):
         scaled, plain = conclude(half)
-        sums_out[0:1, :] = jnp.sum(scaled, axis=0, keepdims=True)
-        sums_out[1:2, :] = jnp.sum(plain, axis=0, keepdims=True)
+        sums_out[0:1, :] += jnp.sum(scaled, axis=0, keepdims=True)
+        sums_out[1:2, :] += jnp.sum(plain, axis=0, keepdims=True)
 
     def produce(moment):
         item = lax.div(moment, spacing)
-        half, stage = lax.rem(item, 2), lax.div(item, 2)
+        half, stage = lax.rem(item, PARTS), lax.div(item, PARTS)
         begins = lax.rem(moment, spacing) == 0
-        for number, work in enumerate((genes_product, latents_back, feed_back, conclude_first)):
+        for number, work in enumerate((genes_product, latents_back, feed_back, conclude_early)):
             pl.when(begins & (stage == number))(functools.partial(work, half))
+
+        tile = moment - TILES_FROM
+
+        @pl.when((tile >= 0) & (tile < whole))
+        def _():
+            grad_tile(pl.ds(pl.multiple_of(tile * TILE, TILE), TILE), TILE)
 
     hooks = [
         (0, begin),
         (4, count_steps[1]),
         (6, count_steps[2]),
         (8, count_steps[3]),
-        (10, open_theirs),
-        (13, trade_begins),
-        (2 * spacing, count_cells),
-        (2 * spacing + 6, pass_on),
+        (PARTS * spacing - 3, residual_done),
+        (PARTS * spacing, count_cells),
+        (TILES_FROM + whole, swap_halves),
+        (TILES_FROM + whole + 6, trade_begins),
+        (TILES_FROM + whole + 15, pass_on),
+        (2 * PARTS * spacing - 1, load_normed.start),
+        (3 * PARTS * spacing - 1, load_normed.wait),
     ]
-    line_pipe(produce, hooks, 6, spacing, part, total, *line)
-    scaled, plain = conclude(1)
-    repeated = 2 * half_rows - cells
+    line_pipe(produce, hooks, 3 * PARTS, spacing, part, total, *line)
+    scaled, plain = conclude(PARTS - 1)
+    repeated = PARTS * PART_ROWS - cells
     sums_out[0:1, :] += jnp.sum(scaled[repeated:, :], axis=0, keepdims=True)
     sums_out[1:2, :] += jnp.sum(plain[repeated:, :], axis=0, keepdims=True)
     genes_sum[...] = conclude_genes()
     for copy in counting.values():
         copy.wait_send()
     swap.wait_send()
-
-
-def back(number, latent_total, ramp, counts, grad_rebuilt, decoder_pre, latent, spread_latent, respons, alive, centers,
-         spreads, upper, normed, scale, gain, genes_w, dec_w, latent_w, down_w, up_w, grad_genes):
+    keep_residual.wait()
+
+
+def back(number, latent_total, ramp, density_parts, info, decoder_pre, latent, spread_latent, centers,
+         spreads, upper, normed, scale, gain, genes_w, dec_w, latent_w, down_w, up_w, expression):
     sections, count_dp, count_z = (lax.axis_size(name) for name in ("section", "dp", "mp"))
     cells, features = decoder_pre.shape
     units, latents = upper.shape[1], latent.shape[1]
-    spacing = pipe_spacing(features // 128, count_z)
-    rooms, half_rows = 2 * spacing, 256
+    comp_count, count_rows = centers.shape[0], 32
+    spacing = pipe_spacing(features // PIECE_COLUMNS, count_z)
+    rooms = PARTS * spacing
     vmem, anywhere = pl.BlockSpec(memory_space=pltpu.VMEM), pl.BlockSpec(memory_space=pl.ANY)
-    piece = (grad_genes.shape[0] // (sections * count_dp), grad_genes.shape[1])
-    roles, one = pltpu.VMEM((count_dp,) + piece, BF16), pltpu.VMEM(piece, BF16)
-    buffer = pltpu.VMEM((rooms, half_rows, 128), BF16)
-    halves = pltpu.VMEM((2, half_rows, features), F32)
+    piece = (genes_w.shape[0] // (sections * count_dp), genes_w.shape[1])
+    parts = pltpu.VMEM((sections * count_dp,) + piece, BF16)
+    buffer = pltpu.VMEM((rooms, PART_ROWS, PIECE_COLUMNS), BF16)
+    halves = pltpu.VMEM((PARTS, PART_ROWS, features), F32)
     outputs = [
         ((cells, features), BF16),
         ((cells, 2 * latents), BF16),
-        (respons.shape, F32),
+        ((2 * comp_count, latents), F32),
         ((cells, features), BF16),
         ((cells, units), BF16),
         ((cells, features), F32),
         ((cells, features), BF16),
         ((8, features), F32),
         (piece, F32),
-        ((piece[0] * count_dp, piece[1]), BF16),
+        ((cells, piece[1]), BF16),
     ]
     copies = 11 + 1 + 6
     results = pl.pallas_call(
         functools.partial(back_kernel, spacing, float(latent_total)),
         out_shape=[jax.ShapeDtypeStruct(*item) for item in outputs],
-        in_specs=[vmem] * 14 + [anywhere] * 6,
+        in_specs=[vmem] * 10 + [anywhere] * 8,
         out_specs=[vmem] * 9 + [anywhere],
         scratch_shapes=[
             halves,
             halves,
-            pltpu.VMEM((2, half_rows, features), BF16),
-            pltpu.VMEM((sections * count_dp * counts.shape[0], 128), F32),
+            pltpu.VMEM((cells, features), F32),
+            pltpu.VMEM((count_rows, 128), F32),
+            pltpu.VMEM((PARTS * PART_ROWS, comp_count), F32),
+            pltpu.VMEM((cells, info.shape[0]), F32),
+            pltpu.VMEM((sections * count_dp * count_rows, 128), F32),
             pltpu.VMEM((8, 128), F32),
         ]
-        + [pltpu.VMEM(array.shape, BF16) for array in (genes_w, dec_w, latent_w, down_w, up_w)]
-        + [roles, roles, one, one, one]
+        + [parts]
+        + [pltpu.VMEM(array.shape, BF16) for array in (dec_w, latent_w, down_w, up_w)]
+        + [
+            pltpu.VMEM((2, PART_ROWS, piece[1]), BF16),
+            pltpu.VMEM((cells, piece[1]), BF16),
+            pltpu.VMEM((features, cells), BF16),
+            parts,
+            pltpu.SemaphoreType.DMA((2,)),
+            pltpu.SemaphoreType.REGULAR,
+        ]
         + [buffer] * 4
         + [pltpu.SemaphoreType.DMA((rooms,))] * 4
         + [
             pltpu.SemaphoreType.DMA((copies,)),
             pltpu.SemaphoreType.DMA((copies,)),
-            pltpu.SemaphoreType.DMA((2 * count_dp + 5,)),
+            pltpu.SemaphoreType.DMA((sections * count_dp + 7,)),
         ],
         compiler_params=pltpu.CompilerParams(
             collective_id=number, has_side_effects=True, vmem_limit_bytes=62 * 2**20
         ),
         name="back",
-    )(ramp, counts, grad_rebuilt, decoder_pre, latent, spread_latent, respons, alive, centers, spreads, upper,
-      normed, scale, gain, genes_w, dec_w, latent_w, down_w, up_w, grad_genes)
-    return results[:9]
+    )(ramp, density_parts, info, latent, spread_latent, centers, spreads, upper, scale, gain, decoder_pre, normed,
+      genes_w, dec_w, latent_w, down_w, up_w, expression)
+    return results
 
 
 def meet(tiled, number, reduce=None, gathers=(), swaps=(), exchanges=(), shares=(), pairs=()):
@@ -1983,6 +2102,7 @@
     alive_float = alive.astype(F32)
     noise = own(latent_noise)
     slide = slide_ids(lax.dynamic_index_in_dim(lengths, micro, 0, False), cells)
+    info = jnp.pad(jnp.stack([slide.astype(F32), alive_float]), ((0, 6), (0, 0)))
 
     norm_block = jnp.pad(jnp.stack([ln1_gain, ln1_bias, ln2_gain, ln2_bias]), ((0, 12), (0, 0)))
     comp_block = jnp.pad(
@@ -2009,16 +2129,15 @@
     comps = small_all[:, 16:, :comp_width].transpose(1, 0, 2).reshape(2 * comp_count, -1)
     centers, spreads = comps[:comp_count], comps[comp_count:]
 
-    normed_one, scale_one, first_low, projected, attended, log_totals = attend(
-        start, gain_one, bias_one, qkv, slide, alive
-    )
     latent_shard = jnp.concatenate([w_mean, w_logvar], axis=1)
     precision = jnp.exp(-spreads)
     if tiled:
-        states, (up_w, down_w, latent_w, dec_w, genes_w) = middle(
+        states, (up_w, down_w, latent_w, dec_w, genes_w), attention = middle(
             1,
-            attended,
             start,
+            (gain_one, bias_one),
+            qkv,
+            info,
             gain_two,
             bias_two,
             out_w,
@@ -2029,10 +2148,11 @@
         )
         (normed_two, scale_two, second_low, upper, activated, hidden, log_vars, latent, spread_latent,
          latent_low, decoder_pre, density_parts) = states
-        density = jnp.sum(density_parts, axis=0)
-        rows = density.shape[1] // 2
-        densities = jnp.concatenate([density[:, :rows], density[:, 3 * rows - cells :]], axis=1)
+        normed_one, scale_one, first_low, projected, attended, log_totals = attention
     else:
+        normed_one, scale_one, first_low, projected, attended, log_totals = attend(
+            start, gain_one, bias_one, qkv, info
+        )
         (summed,), (up_w, down_w, latent_w, dec_w), _, _, _, _ = meeting(
             2, (attended, out_w, False, False), gathers=((w_up, 0), (w_down, 1), (latent_shard, 0), (w_dec, 1))
         )
@@ -2064,33 +2184,28 @@
             4, (latent_low, dec_w, False, False), shares=(density_part,)
         )
         densities = jnp.sum(density_parts, axis=0)[:, :cells]
-    logits = densities[:comp_count] - math.log(comp_count)
-    log_post = densities[comp_count]
-    largest = jnp.max(logits, axis=0, keepdims=True)
-    log_prior = largest[0] + jnp.log(jnp.sum(jnp.exp(logits - largest), axis=0))
-    respons = jnp.exp(logits - log_prior[None, :])
-    divergence = jnp.sum((log_post - log_prior) * alive_float)
-    grad_rebuilt, grad_genes = decode(micro, decoder_pre, genes_w, expression, alive_float)
-
-    counts = jnp.concatenate(
-        [jnp.full((1, 128), divergence), jnp.full((31, 128), jnp.sum(alive_float))], axis=0
-    )
+        logits = densities[:comp_count] - math.log(comp_count)
+        log_post = densities[comp_count]
+        largest = jnp.max(logits, axis=0, keepdims=True)
+        log_prior = largest[0] + jnp.log(jnp.sum(jnp.exp(logits - largest), axis=0))
+        respons = jnp.exp(logits - log_prior[None, :])
+        divergence = jnp.sum((log_post - log_prior) * alive_float)
+        counts = jnp.concatenate(
+            [jnp.full((1, 128), divergence), jnp.full((31, 128), jnp.sum(alive_float))], axis=0
+        )
+
     ramp_weight = jnp.minimum(1.0, (ramp_step[0] + 1).astype(F32) / RAMP)
-    offsets = latent[None] - centers[:, None, :]
-    pulled = offsets * precision[:, None, :]
     if tiled:
-        (grad_pre, grad_stats, weighted, grad_hidden, grad_upper, grad_middle, middle_low, norm_sums,
-         genes_parts) = back(
+        (grad_pre, grad_stats, grad_comps, grad_hidden, grad_upper, grad_middle, middle_low, norm_sums,
+         genes_parts, grad_rebuilt) = back(
             2,
             LATENT,
             jnp.full((8, 128), ramp_weight),
-            counts,
-            grad_rebuilt,
+            density_parts,
+            info,
             decoder_pre,
             latent,
             spread_latent,
-            jnp.pad(respons.T, ((0, 0), (0, 128 - comp_count))),
-            alive_float[:, None],
             centers,
             spreads,
             upper,
@@ -2102,14 +2217,14 @@
             latent_w,
             down_w,
             up_w,
-            grad_genes,
-        )
-        weighted = weighted[:, :comp_count].T[:, :, None]
+            expression,
+        )
         grad_dec = mat_tn(latent_low, grad_pre).astype(BF16)
         grad_latent_w = mat_tn(hidden, grad_stats).astype(BF16)
         grad_down = mat_tn(activated, grad_hidden).astype(BF16)
         grad_up = mat_tn(second_low, grad_upper).astype(BF16)
     else:
+        grad_rebuilt, grad_genes = decode(micro, decoder_pre, genes_w, expression, alive_float)
         (grad_act,), (count_parts,), (genes_other,), _, _, _ = meeting(
             5, (grad_rebuilt, genes_w, True, False), gathers=((counts, 0),), swaps=((grad_genes, 0),)
         )
@@ -2150,13 +2265,13 @@
         )
         middle_low = grad_middle.astype(BF16)
         norm_sums = [jnp.sum(grad_norm_two * normed_two, axis=0), jnp.sum(grad_norm_two, axis=0)]
-    grad_comps = jnp.concatenate(
-        [
-            -jnp.sum(weighted * pulled, axis=1),
-            -jnp.sum(weighted * (0.5 * offsets * pulled - 0.5), axis=1),
-        ],
-        axis=0,
-    )
+        grad_comps = jnp.concatenate(
+            [
+                -jnp.sum(weighted * pulled, axis=1),
+                -jnp.sum(weighted * (0.5 * offsets * pulled - 0.5), axis=1),
+            ],
+            axis=0,
+        )
     grad_out = mat_tn(attended, middle_low).astype(BF16)
     if tiled:
         grad_qkv_act, (down_other, up_other, latent_other, dec_other) = attend_back(
@@ -2165,13 +2280,12 @@
             out_w,
             projected,
             log_totals,
-            slide,
-            alive,
+            info,
             ((grad_down, 1), (grad_up, 0), (grad_latent_w, 0), (grad_dec, 1)),
         )
     else:
         grad_qkv_act, _ = attend_back(
-            11, middle_low, out_w, projected, log_totals, slide, alive, ()
+            11, middle_low, out_w, projected, log_totals, info, ()
         )
     grad_qkv = mat_tn(first_low, grad_qkv_act).astype(BF16)
     (grad_norm_one,), _, (qkv_other, out_other), (down_parts, up_parts, latent_parts, dec_parts), _, _ = meeting(

time: 439 us -> 415 us (0.945)
  Pallas kernels: 376 us -> 362 us
  local copies, waits for them, and re-layouts: 31.4 us -> 25.6 us
    pallas_call x2 -> x0, Pallas kernels: 18.9 us -> none  [the longest x1 13.5 us: decode(): pl.pallas_call(decode_kernel, grid_spec=pltpu.PrefetchScalarGridSpec(num_...]
    unnamed x104 -> x78, local copies, waits for them, and re-layouts: 17.1 us -> 15.6 us
where the time goes in v5:
time: 415 us; the launch traced here: 410 us
  Pallas kernels  362 us (87%)
  local copies, waits for them, and re-layouts  25.6 us (6%)
  other arithmetic  10.5 us (3%)
  matrix products  10.1 us (2%)
    pallas_call x1, Pallas kernels, middle(): pl.pallas_call(functools.partial(middle_kernel, plan, spacing), out_shape...  105 us
    pallas_call x1, Pallas kernels, back(): pl.pallas_call(functools.partial(back_kernel, spacing, float(latent_total...  101 us
    pallas_call x1, Pallas kernels, head(): pl.pallas_call(functools.partial(head_kernel, plan), out_shape=[jax.Shape...  59 us
    pallas_call x1, Pallas kernels, tail(): pl.pallas_call(tail_kernel, out_shape=[jax.ShapeDtypeStruct((genes, width...  48.1 us
    pallas_call x1, Pallas kernels, comm(): pl.pallas_call(functools.partial(comm_kernel, plan), out_shape=outputs, i...  37.6 us
    unnamed x78, local copies, waits for them, and re-layouts  15.6 us
    dot_general x6, matrix products, mat_tn(): lax.dot_general(left, right, (((0,), (0,)), ((), ())), preferred_element_...  10.1 us

profile of v5, /device:TPU:0, one launch (start us, length us, event | category | flops | bytes accessed | tf_op | source)
XLA Modules:
  0.0 409.9 jit_solution(2539119265555306709)
XLA Ops:
  0.7 0.0 copy-start
  0.7 0.0 copy-start.21
  0.7 0.0 copy-start.15
  0.7 0.0 copy-start.8
  1.5 0.7 fusion.11
  2.2 0.2 reduce-window.4
  2.4 0.1 fusion.7
  2.5 0.8 dynamic-slice_convert_fusion
  3.3 0.6 broadcast_in_dim.2.ramp_step
  3.9 0.8 constant_dynamic-slice_fusion.2
  4.6 0.7 fusion.10
  5.3 0.7 fusion.2
  6.1 0.6 select_maximum_fusion.1.info
  6.7 1.4 pad_maximum_fusion.1.refs_2_
  8.1 0.9 pad_maximum_fusion.refs_5_
  9.0 0.1 copy.82
  9.2 0.7 constant_dynamic-slice_fusion.noise
  9.9 1.6 copy.77.refs_4_
  11.5 59.0 %head.1 = (f32[496,1024]{1,0:T(8,128)S(1)}, bf16[3376,1024]{1,0:T(8,128)(2,1)}, bf16[384,128]{1,0:T(8,128)(2,1)S(1)}, bf16[1024,768]{1,0:T(8,128)(2,1)S(1)}, bf16[256,1024]{1,0:T(8,128)(2,1)S(1)}) custom-call(f32[496,2]{1,0:T(8,128)S(1)} %bitcast.59, f32[1,256]{1,0:T(1,128)S(1)} %multiply_exponential_fusion.refs_1_, bf16[992,3376]{1,0:T(8,128)(2,1)} %expression.3, ...), custom_call_target="tpu_custom_call" | custom-call | tf_op jit(solution)/shard_map/head/pallas_call | solution.py:1004
  70.5 0.0 copy-start.2
  70.5 1.1 copy-done.2
  71.7 0.8 copy-done.5
  72.4 1.3 copy-done.7
  73.8 0.6 slice_bitcast_fusion.6
  74.4 0.1 copy.91
  74.5 0.7 slice.83.spreads
  75.2 0.7 slice.81.centers
  75.8 104.7 %middle.1 = (f32[496,1024]{1,0:T(8,128)}, f32[496,1]{1,0:T(8,128)}, bf16[496,1024]{1,0:T(8,128)(2,1)}, f32[496,1024]{1,0:T(8,128)}, bf16[496,1024]{1,0:T(8,128)(...) custom-call(f32[496,1024]{1,0:T(8,128)} %copy-done.7, ...), custom_call_target="tpu_custom_call" | custom-call | tf_op jit(solution)/shard_map/middle/pallas_call | solution.py:1665
  180.6 101.2 %back.1 = (bf16[496,1024]{1,0:T(8,128)(2,1)}, bf16[496,256]{1,0:T(8,128)(2,1)}, f32[32,128]{1,0:T(8,128)}, bf16[496,1024]{1,0:T(8,128)(2,1)}, bf16[496,1024]{1,0...) custom-call(f32[8,128]{1,0:T(8,128)} %broadcast_in_dim.2.ramp_step, ...), custom_call_target="tpu_custom_call" | custom-call | tf_op jit(solution)/shard_map/back/pallas_call | solution.py:1985
  281.8 1.9 convolution_convert_fusion.4.refs_2_.refs_6_
  283.7 0.1 reduce
  283.9 0.8 slice_bitcast_fusion
  284.7 0.1 copy.78
  284.7 0.1 copy.86
  284.9 0.3 convolution_convert_fusion.5.refs_3_.refs_7_
  285.2 0.5 convolution_convert_fusion.3.refs_3_.out
  285.7 0.4 copy-done.29
  286.1 0.3 copy-done.31
  286.4 2.6 convolution_convert_fusion.1.refs_0_.refs_4_
  289.0 0.0 copy-start.14
  289.0 2.6 convolution_convert_fusion.refs_1_.refs_5_
  291.7 5.2 %attend_back.1 = (bf16[496,768]{1,0:T(8,128)(2,1)S(1)}, bf16[1024,512]{1,0:T(8,128)(2,1)S(1)}, bf16[512,1024]{1,0:T(8,128)(2,1)}, bf16[512,256]{1,0:T(8,128)(2,1)S(1)}, bf16[128,512]{1,0:T(8,128)(2,1)S(1)}) custom-call(bf16[496,1024]{1,0:T(8,128)(2,1)S(1)} %copy-done.4, bf16[256,1024]{1,0:T(8,128)(2,1)S(1)} %copy-done.6, bf16[496,768]{1,0:T(8,128)(2,1)S(1)} %copy-done.10, ...), custom_call_target="tpu_custom_call" | custom-call | tf_op jit(solution)/shard_map/attend_back/pallas_call | solution.py:235
  296.9 2.2 convolution_convert_fusion.2.refs_2_.qkv
  299.1 37.6 %meet.1 = (f32[496,1024]{1,0:T(8,128)}, bf16[512,768]{1,0:T(8,128)(2,1)S(1)}, bf16[256,512]{1,0:T(8,128)(2,1)S(1)}, f32[1024,128]{1,0:T(8,128)S(1)}, f32[128,102...) custom-call(bf16[496,768]{1,0:T(8,128)(2,1)S(1)} %get-tuple-element.102.refs_0_, ...), custom_call_target="tpu_custom_call" | custom-call | flops 1000000 | bytes 90000000 | tf_op jit(solution)/shard_map/meet/pallas_call | solution.py:739
  336.7 0.0 copy-start.9
  336.7 0.0 copy-start.11
  336.8 2.8 multiply_reduce_fusion
  339.6 0.5 copy-done.19
  340.1 1.5 add_convert_fusion.start
  341.6 0.7 select_maximum_fusion
  342.3 48.1 %tail.1 = (f32[3376,128]{1,0:T(8,128)}, f32[128,768]{1,0:T(8,128)}, f32[256,128]{1,0:T(8,128)}, f32[48,128]{1,0:T(8,128)}, bf16[496,3376]{1,0:T(8,128)(2,1)}, /*index=5*/bf16[496,3376]{1,0:T(8,128)(2,1)}) custom-call(bf16[496,1024]{1,0:T(8,128)(2,1)} %add_convert_fusion.start, bf16[992,3376]{1,0:T(8,128)(2,1)} %expression.3, ...), custom_call_target="tpu_custom_call" | custom-call | tf_op jit(solution)/shard_map/tail/pallas_call | solution.py:1254
  390.3 1.4 slice_bitcast_fusion.1
  391.7 1.3 fusion.15
  393.0 0.7 fusion.13
  393.7 1.8 fusion.12
  395.5 2.7 copy.81
  398.1 5.8 %assemble.1 = bf16[992,3376]{1,0:T(8,128)(2,1)} custom-call(bf16[496,3376]{1,0:T(8,128)(2,1)} %get-tuple-element.126.own, bf16[496,3376]{1,0:T(8,128)(2,1)} %get-tuple-element.127.other), custom_call_target="tpu_custom_call" | custom-call | tf_op jit(solution)/shard_map/assemble/pallas_call | solution.py:1288
  404.0 0.0 copy-start.12
  404.0 0.0 copy-start.1
  404.0 2.9 copy.100
  406.9 0.7 copy.101
  407.5 0.8 copy.102
  408.3 0.8 copy.103
  409.1 0.6 copy.104
  (60 shorter events, 0.2 us)
Async XLA Ops:
  0.7 8.5 %copy-start = (f32[992,128]{1,0:T(8,128)S(1)}, f32[992,128]{1,0:T(8,128)}, u32[]{:S(2)}) copy-start(f32[992,128]{1,0:T(8,128)} %param.28) | copy-start | bytes 1523716
  0.7 9.2 %copy-start.21 = (bf16[128,3376]{0,1:T(8,128)(2,1)S(1)}, bf16[128,3376]{0,1:T(8,128)(2,1)}, u32[]{:S(2)}) copy-start(bf16[128,3376]{0,1:T(8,128)(2,1)} %param.45) | copy-start | bytes 2592772
  0.7 10.8 %copy-start.15 = (bf16[256,128]{1,0:T(8,128)(2,1)S(1)}, bf16[256,128]{1,0:T(8,128)(2,1)}, u32[]{:S(2)}) copy-start(bf16[256,128]{1,0:T(8,128)(2,1)} %refs_6_.1) | copy-start | bytes 196612
  0.7 10.8 %copy-start.8 = (bf16[3376,128]{1,0:T(8,128)(2,1)S(1)}, bf16[3376,128]{1,0:T(8,128)(2,1)}, u32[]{:S(2)}) copy-start(bf16[3376,128]{1,0:T(8,128)(2,1)} %refs_3_.2) | copy-start | bytes 2592772
  70.5 1.1 copy-start.2
  71.7 0.8 copy-start.5
  72.4 1.3 copy-start.7
  281.8 2.0 copy-start.23
  281.8 2.9 copy-start.26
  281.8 3.1 copy-start.20
  281.8 3.1 copy-start.25
  281.8 3.4 copy-start.4
  281.8 3.4 copy-start.22
  284.9 1.2 copy-start.29
  284.9 1.5 copy-start.31
  286.4 12.7 %copy-start.3 = (bf16[256,1024]{1,0:T(8,128)(2,1)}, bf16[256,1024]{1,0:T(8,128)(2,1)S(1)}, u32[]{:S(2)}) copy-start(bf16[256,1024]{1,0:T(8,128)(2,1)S(1)} %convolution_convert_fusion.3.refs_3_.out) | copy-start | bytes 1572868
  286.4 2.6 copy-start.28
  286.4 2.6 copy-start.30
  289.0 2.7 copy-start.6
  289.0 2.7 copy-start.10
  289.0 2.7 copy-start.14
  289.0 2.6 copy-start.16
  291.7 5.2 %copy-start.27 = (bf16[496,1024]{1,0:T(8,128)(2,1)S(1)}, bf16[496,1024]{1,0:T(8,128)(2,1)}, u32[]{:S(2)}) copy-start(bf16[496,1024]{1,0:T(8,128)(2,1)} %get-tuple-element.103) | copy-start | bytes 3047428
  299.1 37.7 %copy-start.17 = (f32[496,1024]{1,0:T(8,128)S(1)}, f32[496,1024]{1,0:T(8,128)}, u32[]{:S(2)}) copy-start(f32[496,1024]{1,0:T(8,128)} %get-tuple-element.110) | copy-start | bytes 6094852
  336.7 2.8 copy-start.9
  336.7 2.8 copy-start.11
  336.8 2.8 copy-start.13
  336.8 2.9 copy-start.18
  336.8 3.3 copy-start.19
  404.0 2.9 copy-start.24
  404.0 3.5 copy-start.12
  404.0 5.8 %copy-start.1 = (f32[992,128]{1,0:T(8,128)S(1)}, f32[992,128]{1,0:T(8,128)}, u32[]{:S(2)}) copy-start(f32[992,128]{1,0:T(8,128)} %param.28) | copy-start | bytes 1523716
